TPU v7x, 128 devices: a whole 4x4x4 slice. The times are simulated.
128 devices in a mesh: dp: 16 (over z, x_lo, core), factor: 8 (over x_hi, y).
Axes of the slice: x: 4 (x_hi: 2, x_lo: 2; x = x_hi * 2 + x_lo), y: 4, z: 4, core: 2. Of those that a mesh axis runs over, the one named last changes fastest.
Arguments:
- activations: bfloat16 [8192, 3072], P('dp'), may hold values from -6 to 6
- cotangents: bfloat16 [8192, 12288], P('dp', 'factor'), may hold values from -6 to 6
- basis_in: bfloat16 [1536, 2, 1536], P('dp', None, 'factor'), may hold values from -0.15625 to 0.15625
- basis_out: bfloat16 [12288, 1536], P('factor'), may hold values from -0.15625 to 0.15625
- factor_in: float32 [1536, 2, 1536], P('dp', None, 'factor'), may hold values from -0.15625 to 0.15625
- factor_out: float32 [1536, 12288], P('dp', 'factor'), may hold values from -0.15625 to 0.15625
- scale_in: float32 [2, 1536], replicated, may hold values from 0.02 to 0.3
- scale_out: float32 [12288], P('factor'), may hold values from 0.02 to 0.3
- overflow: int32 [8192], P('dp'), may hold values from 0 to 1, as said below
Outputs:
- precond: bfloat16 [1536, 2, 12288], P('dp', None, 'factor')
- new_factor_in: float32 [1536, 2, 1536], P('dp', None, 'factor')
- new_factor_out: float32 [1536, 12288], P('dp', 'factor')
Inputs may be any that keep to these rules, and one draw needn't show every extreme that they name: `overflow`: rows of odd index are never marked; so at least half of the rows are healthy.
All inputs are finite; a program needn't handle non-finite values.
Results may differ from a plain program's by a relative error of at most 0.017.
Values may be sent and summed in bfloat16 or wider, within the bound.
No kernel may reach another device: no remote copies, remote signals or barrier semaphores. Data moves between devices by JAX's collectives and lax.ppermute only.
A program may use at most 128 MiB of HBM per device.

v0:
```python
import jax
import jax.numpy as jnp
from jax import lax
from jax.sharding import PartitionSpec as P

decay_rate = 0.9
damping = 0.001


def per_device(
    activations,
    cotangents,
    basis_in,
    basis_out,
    factor_in,
    factor_out,
    scale_in,
    scale_out,
    overflow,
):
    tok_rows = activations.shape[0]
    blocks = scale_in.shape[0]
    block_width = scale_in.shape[1]
    own_rows = factor_in.shape[0]
    local_columns = factor_in.shape[2]
    healthy = (overflow == 0)[:, None]
    input_masked_rows = jnp.where(healthy, activations, jnp.zeros_like(activations)).reshape(
        tok_rows, blocks, block_width
    )
    masked_out = jnp.where(healthy, cotangents, jnp.zeros_like(cotangents))
    local_count = jnp.sum(overflow.astype(jnp.float32))
    total_count = lax.psum(local_count, "dp")
    basis_rows = lax.all_gather(basis_in, "factor", axis=2, tiled=True)
    eigen_part = jnp.einsum(
        "tar,rak->tak",
        input_masked_rows,
        lax.all_gather(basis_in, "dp", axis=0, tiled=True),
        preferred_element_type=jnp.float32,
    ).astype(jnp.bfloat16)
    eigen_in = lax.all_gather(eigen_part, "factor", axis=2, tiled=True)
    output_eigenvalues = jnp.dot(masked_out, basis_out, preferred_element_type=jnp.float32).astype(
        jnp.bfloat16
    )
    in_squares = jnp.sum(jnp.square(eigen_in.astype(jnp.float32)), axis=0)
    out_squares = jnp.sum(jnp.square(output_eigenvalues.astype(jnp.float32)), axis=0)
    in_total, out_total = lax.psum((in_squares, out_squares), "dp")
    column_start = lax.axis_index("factor") * local_columns
    input_feature_columns = lax.dynamic_slice_in_dim(
        input_masked_rows, column_start, local_columns, 2
    )
    input_covariance = jnp.einsum(
        "eku,eks->uks", input_masked_rows, input_feature_columns, preferred_element_type=jnp.float32
    )
    cov_out = jnp.einsum("tr,tc->rc", masked_out, masked_out, preferred_element_type=jnp.float32)
    grad_rows = lax.psum_scatter(
        jnp.einsum(
            "tak,tg->kag", eigen_in, output_eigenvalues, preferred_element_type=jnp.float32
        ).astype(jnp.bfloat16),
        "dp",
        scatter_dimension=0,
        tiled=True,
    ).astype(jnp.float32)
    sum_in, sum_out = (
        lax.psum_scatter(
            input_covariance.astype(jnp.bfloat16), "dp", scatter_dimension=0, tiled=True
        ).astype(jnp.float32),
        lax.psum_scatter(
            cov_out.astype(jnp.bfloat16), "dp", scatter_dimension=0, tiled=True
        ).astype(jnp.float32),
    )
    healthy_rows = jnp.float32(tok_rows * lax.axis_size("dp")) - total_count
    blend_weight = 1.0 - decay_rate
    new_factor_in = decay_rate * factor_in + blend_weight * sum_in / healthy_rows
    new_factor_out = decay_rate * factor_out + blend_weight * sum_out / healthy_rows
    input_eigenvalues = decay_rate * scale_in + blend_weight * in_total / healthy_rows
    lam_out = decay_rate * scale_out + blend_weight * out_total / healthy_rows
    k_start = lax.axis_index("dp") * own_rows
    lam_rows = lax.dynamic_slice_in_dim(input_eigenvalues, k_start, own_rows, 1)
    denominator = lam_rows.T[:, :, None] * lam_out[None, None, :] + damping
    scaled = (grad_rows / healthy_rows / denominator).astype(jnp.bfloat16)
    turned = jnp.einsum(
        "kag,mg->kam", scaled, basis_out, preferred_element_type=jnp.float32
    ).astype(jnp.bfloat16)
    result = jnp.einsum(
        "rak,kam->ram",
        basis_rows,
        lax.all_gather(turned, "dp", axis=0, tiled=True),
        preferred_element_type=jnp.float32,
    )
    return (result.astype(jnp.bfloat16), new_factor_in, new_factor_out)


def solution(mesh):
    in_specs = (
        P("dp", None),
        P("dp", "factor"),
        P("dp", None, "factor"),
        P("factor", None),
        P("dp", None, "factor"),
        P("dp", "factor"),
        P(),
        P("factor"),
        P("dp"),
    )
    out_specs = (P("dp", None, "factor"), P("dp", None, "factor"), P("dp", "factor"))
    return jax.shard_map(
        per_device, mesh=mesh, in_specs=in_specs, out_specs=out_specs, check_vma=False
    )
```

profile of v0, /device:TPU:1, one launch (start us, length us, event | category | flops | bytes accessed | tf_op | source)
XLA Modules:
  0.0 568.1 jit_solution(3520458717240079107)
XLA Ops:
  7.2 0.0 all-gather.4.cloned.1.call-start
  7.2 0.7 all-gather.4.cloned.1.call-update
  7.9 0.0 all-gather.6.cloned.1.call-start
  7.9 0.7 broadcast_compare_fusion
  8.6 3.8 broadcast_select_fusion
  12.4 3.2 copy.20
  15.6 31.0 %all-gather.4.cloned.1.call-done = bf16[1536,2,192]{2,1,0:T(2,128)(2,1)} async-done(((bf16[96,2,192]{2,1,0:T(2,128)(2,1)}), bf16[1536,2,192]{2,1,0:T(2,128)(2,1)}) %all-gather.4.cloned.1.call-update) | async-done | bytes 1179664 | tf_op jit(solution)/shard_map/all_gather | solution.py:37
  46.6 3.0 fusion.12
  49.6 0.0 all-gather.6.cloned.1.call-update
  49.6 0.0 all-reduce.4.cloned.1.call-start
  49.7 6.7 %multiply_reduce_fusion.1 = (f32[1536]{0:T(1024)S(1)}, bf16[512,1536]{1,0:T(8,128)(2,1)}) fusion(bf16[1536,1536]{1,0:T(8,128)(2,1)} %param.12, bf16[512,1536]{1,0:T(8,128)(2,1)} %param.10, pred[512]{0:T(512)(128)(4,1)S(1)} %broadcast_compare_fusion), kind=kOutput, calls=%fused_computation.5 | convolution fusion | flops 2419849728 | bytes 7870976 | tf_op jit(solution)/shard_map/dot_general | solution.py:41
  56.3 55.2 %all-gather.6.cloned.1.call-done = bf16[512,2,1536]{0,2,1:T(8,128)(2,1)} async-done(((bf16[512,2,192]{0,2,1:T(8,128)(2,1)}), bf16[512,2,1536]{0,2,1:T(8,128)(2,1)}) %all-gather.6.cloned.1.call-update) | async-done | bytes 3145744 | tf_op jit(solution)/shard_map/all_gather | solution.py:40
  111.5 9.5 %convolution_convert_fusion = bf16[1536,2,1536]{2,0,1:T(8,128)(2,1)} fusion(bf16[512,2,1536]{0,2,1:T(8,128)(2,1)} %all-gather.6.cloned.1.call-done, bf16[512,1536]{1,0:T(8,128)(2,1)} %get-tuple-element.13), kind=kOutput, calls=%fused_computation | convolution fusion | flops 4836556800 | bytes 14155776 | tf_op jit(solution)/shard_map/tak,tg->kag/dot_general | solution.py:56
  121.0 23.9 %copy.38 = bf16[1536,2,1536]{0,1,2:T(2,128)(2,1)} copy(bf16[1536,2,1536]{2,0,1:T(8,128)(2,1)} %convolution_convert_fusion) | data formatting | bytes 18874368
  145.0 0.0 all-reduce.4.cloned.1.call-update
  145.0 0.0 reduce-scatter.7.cloned.1.call-start
  145.1 2.2 convolution_convert_fusion.3
  147.3 2.5 copy.36
  149.8 0.0 reduce-scatter.7.cloned.1.call-update
  149.8 0.0 reduce-scatter.5.cloned.1.call-start
  149.8 4.8 convolution_convert_fusion.1
  154.6 0.0 reduce-scatter.5.cloned.1.call-update
  154.6 0.0 all-gather.8.cloned.1.call-start
  154.7 0.6 copy-done.7
  155.3 0.6 dynamic-slice
  156.5 0.6 convert_reduce_fusion
  157.1 0.7 multiply_reduce_fusion
  157.8 54.8 %all-reduce.1 = (f32[1536]{0:T(1024)S(1)}, f32[]{:T(128)}, f32[2,1536]{1,0:T(2,128)S(1)}) all-reduce(f32[1536]{0:T(1024)S(1)} %get-tuple-element.12, f32[]{:T(128)} %convert_reduce_fusion, f32[2,1536]{1,0:T(2,128)S(1)} %multiply_reduce_fusion), channel_id=1, replica_groups=mesh['dp'=16,'factor'=8] {'dp'}, use_global_device_ids=true, to_apply=%region_6.7 | all-reduce | flops 4609 | bytes 36872 | tf_op jit(solution)/shard_map/psum | solution.py:46
  213.3 0.8 fusion.19
  214.0 0.1 copy.23
  214.2 145.0 %all-reduce.4.cloned.1.call-done = bf16[1536,2,1536]{2,1,0:T(2,128)(2,1)} async-done(((bf16[1536,2,1536]{2,1,0:T(2,128)(2,1)}), bf16[1536,2,1536]{2,1,0:T(2,128)(2,1)}) %all-reduce.4.cloned.1.call-update) | async-done | bytes 9437200
  359.2 2.2 fusion.15
  361.4 0.0 copy-start.2
  361.4 0.0 copy-start.3
  361.4 0.0 copy-start.1
  361.4 4.9 fusion.2
  366.3 0.0 all-gather.8.cloned.1.call-update
  366.4 0.1 copy.24
  366.5 0.1 copy.26
  366.6 29.9 %all_gather.15 = bf16[96,2,1536]{0,1,2:T(2,128)(2,1)S(1)} all-gather(bf16[96,2,192]{0,1,2:T(2,128)(2,1)S(1)} %copy.24), channel_id=1, replica_groups=mesh['dp'=16,'factor'=8] {'factor'}, dimensions={2}, use_global_device_ids=true | all-gather | bytes 663552 | tf_op jit(solution)/shard_map/all_gather | solution.py:33
  396.6 25.0 %reduce-scatter.7.cloned.1.call-done = bf16[96,384]{1,0:T(8,128)(2,1)} async-done(((bf16[1536,384]{1,0:T(8,128)(2,1)}), bf16[96,384]{1,0:T(8,128)(2,1)}) %reduce-scatter.7.cloned.1.call-update) | async-done | bytes 73744
  421.5 1.0 copy.37
  422.6 0.8 copy.29
  423.4 70.1 %reduce-scatter.5.cloned.1.call-done = bf16[96,1536]{1,0:T(8,128)(2,1)} async-done(((bf16[1536,1536]{1,0:T(8,128)(2,1)}), bf16[96,1536]{1,0:T(8,128)(2,1)}) %reduce-scatter.5.cloned.1.call-update) | async-done | bytes 294928 | tf_op jit(solution)/shard_map/reduce_scatter | solution.py:67
  493.5 1.9 divide_add_fusion
  495.4 59.1 %all-gather.8.cloned.1.call-done = bf16[1536,2,1536]{2,0,1:T(8,128)(2,1)} async-done(((bf16[96,2,1536]{2,0,1:T(8,128)(2,1)}), bf16[1536,2,1536]{2,0,1:T(8,128)(2,1)}) %all-gather.8.cloned.1.call-update) | async-done | bytes 9437200 | tf_op jit(solution)/shard_map/all_gather | solution.py:87
  554.5 5.3 fusion.5
  559.9 1.4 copy.28
  (14 shorter events, 0.1 us)
Async XLA Ops:
  7.2 39.5 %all-gather.4.cloned.1.call-start = ((), (), s32[]{:S(2)}) async-start(), calls=%async_computation.2 | async-start | bytes 1671168 | tf_op jit(solution)/shard_map/all_gather | solution.py:37
  7.9 103.6 %all-gather.6.cloned.1.call-start = ((), (), s32[]{:S(2)}) async-start(), calls=%async_computation.3 | async-start | bytes 3538944 | tf_op jit(solution)/shard_map/all_gather | solution.py:40
  49.6 309.5 %all-reduce.4.cloned.1.call-start = ((), (), s32[]{:S(2)}) async-start(), calls=%async_computation.7 | async-start | bytes 18874368
  145.0 276.5 %reduce-scatter.7.cloned.1.call-start = ((), (), s32[]{:S(2)}) async-start(), calls=%async_computation.6 | async-start | bytes 1253376
  147.3 2.6 copy-start.6
  149.8 343.7 %reduce-scatter.5.cloned.1.call-start = ((), (), s32[]{:S(2)}) async-start(), calls=%async_computation.5 | async-start | bytes 5013504 | tf_op jit(solution)/shard_map/reduce_scatter | solution.py:67
  154.6 0.7 copy-start.7
  154.6 1.9 copy-start.5
  154.6 2.5 copy-start
  154.6 59.5 %copy-start.4 = (f32[1536]{0:T(1024)S(1)}, f32[1536]{0:T(1024)}, u32[]{:S(2)}) copy-start(f32[1536]{0:T(1024)} %param.16) | copy-start | bytes 18436
  154.6 399.9 %all-gather.8.cloned.1.call-start = ((), (), s32[]{:S(2)}) async-start(), calls=%async_computation.4 | async-start | bytes 10027008 | tf_op jit(solution)/shard_map/all_gather | solution.py:87
  361.4 5.0 copy-start.2
  361.4 5.1 copy-start.3
  361.4 132.1 %copy-start.1 = (f32[96,1536]{1,0:T(8,128)S(1)}, f32[96,1536]{1,0:T(8,128)}, u32[]{:S(2)}) copy-start(f32[96,1536]{1,0:T(8,128)} %param.14) | copy-start | bytes 1769476
Sparse Core Ops, SparseCore 0:
  9.7 36.8 all-gather.3
  49.7 61.7 all-gather.5
  145.1 213.9 all-reduce.3
  361.4 60.0 reduce-scatter.6
  423.8 69.6 reduce-scatter.4
  495.6 58.8 all-gather.7
where the time goes:
time: 569 us; the launch traced here: 568 us
  waiting for transfers between devices  386 us (68%)
  blocking collectives  84.8 us (15%)
  matrix products  36.3 us (6%)
  local copies, waits for them, and re-layouts  34.4 us (6%)
  between operations  15.6 us (3%)
  other arithmetic  10.7 us (2%)
    unnamed x8, waiting for transfers between devices  171 us
    reduce_scatter x1, waiting for transfers between devices, per_device(): lax.psum_scatter(cov_out.astype(jnp.bfloat16), 'dp', scatter_dimension=0,...  70.1 us
    all_gather x1, waiting for transfers between devices, per_device(): lax.all_gather(turned, 'dp', axis=0, tiled=True)  59.1 us
    all_gather x1, waiting for transfers between devices, per_device(): eigen_in = lax.all_gather(eigen_part, 'factor', axis=2, tiled=True)  55.2 us
    psum x1, blocking collectives, per_device(): in_total, out_total = lax.psum((in_squares, out_squares), 'dp')  54.8 us
    unnamed x24, local copies, waits for them, and re-layouts  31.1 us
    all_gather x1, waiting for transfers between devices, per_device(): lax.all_gather(basis_in, 'dp', axis=0, tiled=True)  31 us
    all_gather x1, blocking collectives, per_device(): basis_rows = lax.all_gather(basis_in, 'factor', axis=2, tiled=True)  29.9 us
  transfers between devices with their start and end apart: 6, of which 6 were waited for; matrix products, arithmetic and copies ran while one was open for 7% of the time, Pallas kernels for 0%

commit v1 on v0

v1 whole, which is shorter than its diff:
```python
import jax
import jax.numpy as jnp
from jax import lax
from jax.experimental import pallas as pl
from jax.experimental.pallas import tpu as pltpu
from jax.sharding import PartitionSpec as P

decay_rate = 0.9
damping = 0.001
blend_weight = 1.0 - decay_rate

f32 = jnp.float32
bf16 = jnp.bfloat16

CORE = [(i, i ^ 1) for i in range(16)]
XLO = [(i, i ^ 2) for i in range(16)]
XHI = [(j, j ^ 4) for j in range(8)]
SAME_XHI = [[0, 1, 2, 3], [4, 5, 6, 7]]
PARAMS = pltpu.CompilerParams(vmem_limit_bytes=56 * 2**20)


def to_z(s):
    return [(i, ((i >> 2) + s) % 4 * 4 + (i & 3)) for i in range(16)]


def swap_z(bits):
    return [(i, i ^ (bits * 4)) for i in range(16)]


def swap_y(bits):
    return [(j, j ^ bits) for j in range(8)]


UP, DOWN = to_z(1), to_z(3)


def dot(a, b, contract=((1,), (0,)), **kwargs):
    return lax.dot_general(a, b, (contract, ((), ())), preferred_element_type=f32, **kwargs)


def added(*parts):
    total = parts[0].astype(f32)
    for part in parts[1:]:
        total = total + part.astype(f32)
    return total


def after(value, *others):
    return lax.optimization_barrier((value, *others))[0]


def send_z(up, down):
    return lax.ppermute(up, "dp", UP), lax.ppermute(down, "dp", DOWN)


def forward_z(got_up, got_down, first_1, second_3):
    return added(first_1, got_up[0]).astype(bf16), added(second_3, got_down[0]).astype(bf16)


def shape_of(*dims, dtype=bf16):
    return jax.ShapeDtypeStruct(dims, dtype)


def whole(shape):
    return pl.BlockSpec(shape, lambda *_: (0,) * len(shape))


def placed(kernel, place, grid, in_specs, out_shapes, operands, out_specs=None, scratch=()):
    return pl.pallas_call(
        kernel,
        out_shape=out_shapes,
        grid_spec=pltpu.PrefetchScalarGridSpec(
            num_scalar_prefetch=1,
            grid=grid,
            in_specs=in_specs,
            out_specs=out_specs or [whole(s.shape) for s in out_shapes],
            scratch_shapes=list(scratch),
        ),
        compiler_params=PARAMS,
        name=kernel.__name__,
    )(place, *operands)


def healthy(marks):
    return (marks[...] == 0).astype(f32)


def rotate_kernel(place, cot, marks, basis, *refs):
    refs[-1][...] = jnp.swapaxes(dot(cot[...], basis[...]).astype(bf16), 0, 1) * healthy(marks).astype(bf16)


def grad_kernel(place, eigen_0, eigen_1, act_0, act_1, give, keep, up, down, first_1, second_3, own, total):
    chunk, cut = give.shape[1], give.shape[2]
    total[...] = dot(eigen_0[...], act_0[...]) + dot(eigen_1[...], act_1[...])
    outs = ((own, 0, own, 1), (first_1, None, up, 1), (up, 0, down, 0), (down, 1, second_3, None))
    for s in range(4):
        base = (place[0] + s) % 4 * 2 * chunk
        mine = pl.ds(pl.multiple_of(base + place[1] * chunk, 16), chunk)
        other = pl.ds(pl.multiple_of(base + (1 - place[1]) * chunk, 16), chunk)
        give[s] = total[other, :cut].astype(bf16)
        keep[s] = total[mine, :cut].astype(bf16)
        for half in range(2):
            out, at = outs[s][2 * half : 2 * half + 2]
            value = total[pl.ds(pl.multiple_of(base + half * chunk, 16), chunk), cut:].astype(bf16)
            if at is None:
                out[...] = value
            else:
                out[at] = value


def second_kernel(keep, got_a, got_up, got_down, first_1, second_3, up, down, a_first_1, a_second_3, own_a):
    part = own_a.shape[1]
    rest = first_1.shape[1]
    up[:, :rest] = added(first_1[...], got_up[0]).astype(bf16)
    down[:, :rest] = added(second_3[...], got_down[0]).astype(bf16)

    def a_sum(s, half):
        rows = slice(half * part, (half + 1) * part)
        return added(keep[s, rows], got_a[s, rows]).astype(bf16)

    up[:part, rest:] = a_sum(2, 0)
    up[part:, rest:] = a_sum(1, 1)
    down[:part, rest:] = a_sum(2, 1)
    down[part:, rest:] = a_sum(3, 0)
    a_first_1[...] = a_sum(1, 0)
    a_second_3[...] = a_sum(3, 1)
    own_a[0] = a_sum(0, 0)
    own_a[1] = a_sum(0, 1)


def third_kernel(
    place, got_up, got_down, up, down, own_b, a_first_1, a_second_3, own_a, a_up, a_down, give, keep_b, keep_a
):
    part = own_a.shape[1]
    rest = own_b.shape[2]
    a_up[...] = added(a_first_1[...], up[:part, rest:]).astype(bf16)
    a_down[...] = added(a_second_3[...], down[:part, rest:]).astype(bf16)
    first = added(own_b[0], got_down[0], up[:, :rest])
    second = added(own_b[1], got_up[0], down[:, :rest])
    left = place[1] == 0
    give[...] = jnp.where(left, second, first).astype(bf16)
    keep_b[...] = jnp.where(left, first, second)
    keep_a[0] = added(own_a[0], down[part:, rest:])
    keep_a[1] = added(own_a[1], up[part:, rest:])


def cov_kernel(
    place, cot_0, cot_1, marks_0, marks_1, rows_0, rows_1, act_0, act_1, cols_0, cols_1, up, down, rest, turned, mine
):
    places = (((rest, 0), (rest, 2), (up, 0), (down, 1)), ((rest, 1), (up, 1), (down, 0), (rest, 3)))
    tokens = cot_0.shape[0]
    rows = turned.shape[0] // 4
    mask_0, mask_1 = healthy(marks_0).astype(bf16), healthy(marks_1).astype(bf16)
    turned[:, :tokens] = jnp.swapaxes(rows_0[...], 0, 1) * mask_0
    turned[:, tokens:] = jnp.swapaxes(rows_1[...], 0, 1) * mask_1
    for x in range(2):
        mine[x * rows : (x + 1) * rows] = turned[pl.ds(pl.multiple_of((2 * x + place[2]) * rows, 16), rows), :]
    cov_out = dot(mine[:, :tokens], cot_0[...]) + dot(mine[:, tokens:], cot_1[...])
    odd = place[3] % 2
    own = [jnp.where(odd == 0, c[:, : 2 * rows].astype(f32), c[:, 2 * rows :].astype(f32)).astype(bf16) for c in (cols_0, cols_1)]
    cov_in = dot(jnp.swapaxes(act_0[...], 0, 1) * mask_0, own[0])
    cov_in += dot(jnp.swapaxes(act_1[...], 0, 1) * mask_1, own[1])
    for x in range(2):
        low = 2 * x * rows
        pair = jnp.concatenate([cov_in[low : low + rows], cov_in[low + rows : low + 2 * rows]], 1)
        value = jnp.concatenate([cov_out[x * rows : (x + 1) * rows], pair], 1).astype(bf16)
        for s, (out, at) in enumerate(places[x]):

            @pl.when(pl.program_id(0) == s)
            def _():
                out[at] = value


def squares_kernel(place, act_0, act_1, marks_0, marks_1, basis, eigen_0, eigen_1, out_in, out_out):
    total = 0.0
    for act, marks in ((act_0, marks_0), (act_1, marks_1)):
        tokens, columns = act.shape[0], basis.shape[1]
        lanes = min(128, columns)
        square = jnp.square(dot(act[...], basis[...]).astype(bf16).astype(f32))
        mask = jnp.swapaxes(jnp.broadcast_to(healthy(marks), (lanes, tokens)), 0, 1)
        total += jnp.sum(square * jnp.concatenate([mask] * (columns // lanes), 1), axis=0, keepdims=True)
    out_in[...] = total
    width, tokens = eigen_0.shape
    lanes = min(128, tokens)
    for at in range(0, width, width // 4):
        rows = slice(at, at + width // 4)
        square = jnp.square(eigen_0[rows].astype(f32)) + jnp.square(eigen_1[rows].astype(f32))
        square = sum(square[:, i : i + lanes] for i in range(0, tokens, lanes))
        out_out[:, rows] = jnp.sum(jnp.swapaxes(square, 0, 1), axis=0, keepdims=True)


def rows_kernel(place, own, got, out):
    for s in range(4):
        out[(place[0] + s) % 4, place[1]] = own[s]
        out[(place[0] + s) % 4, 1 - place[1]] = got[s]


def turn_kernel(keep_a, via_up, via_down, keep_b, got_b, basis, lam_out, lam_in, damp, out, grad, total):
    y = pl.program_id(0)
    cut = keep_a.shape[2]
    part = keep_a.shape[1]

    @pl.when(y == 0)
    def _():
        grad[:part, :cut] = added(keep_a[0], via_up[...]).astype(bf16)
        grad[part:, :cut] = added(keep_a[1], via_down[...]).astype(bf16)
        grad[:, cut:] = added(keep_b[...], got_b[...]).astype(bf16)
        total[...] = jnp.zeros(total.shape, f32)

    rotated = dot(grad[...], basis[0])
    scaled = (rotated / (lam_out[...] * lam_in[0] + damp[...])).astype(bf16)
    total[...] += dot(basis[0], scaled, ((1,), (1,)))

    @pl.when(y == 3)
    def _():
        out[...] = total[...].astype(bf16)


def last_kernel(spread, basis_out, out):
    chunk = spread.shape[2]
    rows = spread.shape[1]
    total = None
    for z in range(4):
        lhs = jnp.concatenate(
            [jnp.concatenate([spread[4 * z + a], spread[4 * z + 2 + a]], 1) for a in range(2)], 0
        )
        part = dot(lhs, basis_out[:, 2 * z * chunk : 2 * (z + 1) * chunk], ((1,), (1,)))
        total = part if total is None else total + part
    out[0] = total[:rows].astype(bf16)
    out[1] = total[rows:].astype(bf16)


def per_device(
    activations,
    cotangents,
    basis_in,
    basis_out,
    factor_in,
    factor_out,
    scale_in,
    scale_out,
    overflow,
):
    tokens = activations.shape[0]
    width = scale_in.shape[1]
    rows = factor_in.shape[0]
    cols = factor_in.shape[2]
    chunk = width // 8
    wide = width // 4
    cut = width // 3
    dp = lax.axis_index("dp")
    fac = lax.axis_index("factor")
    core, x, z = dp % 2, (dp // 2) % 2, dp // 4
    place = jnp.stack([z, x, core, fac]).astype(jnp.int32)

    basis_keep = lax.dynamic_index_in_dim(basis_in, core, 1, keepdims=False)
    basis_give = lax.dynamic_index_in_dim(basis_in, 1 - core, 1, keepdims=False)
    basis_got = lax.ppermute(basis_give, "dp", CORE)
    marks = overflow.reshape(1, tokens)
    marks_got = lax.ppermute(marks, "dp", CORE)
    cot_got = lax.ppermute(cotangents, "dp", CORE)
    act_give = lax.dynamic_slice_in_dim(activations, (1 - core) * width, width, 1)
    act_got = lax.ppermute(act_give, "dp", CORE)

    def rotate(place, at, before):
        return pl.pallas_call(
            rotate_kernel,
            out_shape=shape_of(width, tokens),
            grid_spec=pltpu.PrefetchScalarGridSpec(
                num_scalar_prefetch=1,
                grid=(2,),
                in_specs=[
                    whole((tokens, width)),
                    whole((1, tokens)),
                    pl.BlockSpec((width, wide), lambda i, p: (0, at + i)),
                ]
                + [pl.BlockSpec(memory_space=pl.ANY)] * len(before),
                out_specs=pl.BlockSpec((wide, tokens), lambda i, p: (at + i, 0)),
            ),
            input_output_aliases={4: 0} if before else {},
            compiler_params=PARAMS,
            name="rotate_kernel",
        )(place, cotangents, marks, basis_out, *before)

    eigen_half = rotate(after(place, act_give, basis_give), 0, ())
    basis_mine = after(basis_keep, eigen_half)
    basis_chip = jnp.where(
        core == 0,
        jnp.concatenate([basis_mine, basis_got], 0),
        jnp.concatenate([basis_got, basis_mine], 0),
    )
    basis_x_hi = lax.ppermute(basis_chip, "factor", XHI)
    eigen = rotate(after(place, basis_chip, marks_got), 2, (eigen_half,))
    eigen_got = lax.ppermute(after(eigen, basis_x_hi), "dp", CORE)
    basis_pair = jnp.concatenate([after(basis_chip, eigen), basis_x_hi], 1)
    basis_z = [lax.ppermute(basis_pair, "dp", to_z(4 - s)) for s in (1, 2, 3)]

    def own_block(n, at):
        return pl.BlockSpec((tokens, n), lambda i, p: (0, at(i, p)))

    columns = width + 2 * cols
    cov_up, cov_down, cov_rest = placed(
        cov_kernel,
        after(place, basis_pair),
        (4,),
        [whole((tokens, width))] * 2
        + [whole((1, tokens))] * 2
        + [own_block(wide, lambda i, p: (p[0] + i) % 4)] * 2
        + [own_block(wide, lambda i, p: p[2] * 4 + (p[0] + i) % 4), own_block(wide, lambda i, p: (p[0] + i) % 4)]
        + [own_block(wide, lambda i, p: p[2] * 4 + p[3] // 2), own_block(wide, lambda i, p: p[3] // 2)],
        [shape_of(n, rows, columns) for n in (2, 2, 4)],
        (cotangents, cot_got, marks, marks_got, cotangents, cot_got, activations, act_got, activations, act_got),
        scratch=[pltpu.VMEM((wide, 2 * tokens), bf16), pltpu.VMEM((wide // 2, 2 * tokens), bf16)],
    )
    cov_got_up, cov_got_down = send_z(cov_up, cov_down)

    basis_four = jnp.stack([after(basis_pair, cov_up), *basis_z])
    basis_x_lo = lax.ppermute(basis_four, "dp", XLO)

    single = shape_of(chunk, width - cut)
    pair = shape_of(2, chunk, width - cut)
    four = shape_of(4, chunk, cut)
    give, keep, up, down, first_1, second_3, own_b = placed(
        grad_kernel,
        after(place, basis_four),
        (1,),
        [whole((width, tokens))] * 2
        + [pl.BlockSpec((tokens, width), lambda i, p: (0, p[2])), whole((tokens, width))],
        [four, four, pair, pair, single, single, pair],
        (eigen, eigen_got, activations, act_got),
        scratch=[pltpu.VMEM((width, width), f32)],
    )
    (basis_rows,) = placed(
        rows_kernel,
        after(place, own_b, cov_got_up, cov_got_down),
        (1,),
        [whole(basis_four.shape)] * 2,
        [shape_of(4, 2, 2 * rows, 2 * cols)],
        (basis_four, basis_x_lo),
    )
    basis_rows = basis_rows.reshape(width, 2 * cols)
    basis_all = lax.all_gather(basis_rows, "factor", axis=0, axis_index_groups=SAME_XHI)
    squares_in, squares_out = placed(
        squares_kernel,
        place,
        (1,),
        [pl.BlockSpec((tokens, width), lambda i, p: (0, p[2])), whole((tokens, width))]
        + [whole((1, tokens))] * 2
        + [whole((width, 2 * cols))]
        + [whole((width, tokens))] * 2,
        [shape_of(1, 2 * cols, dtype=f32), shape_of(1, width, dtype=f32)],
        (activations, act_got, marks, marks_got, basis_rows, eigen, eigen_got),
    )
    by_y = jnp.concatenate([squares_in, lax.ppermute(squares_in, "factor", swap_y(1))], 0)
    by_y = jnp.concatenate([by_y, lax.ppermute(by_y, "factor", swap_y(2))], 0)
    count = jnp.sum((marks + marks_got).astype(f32))
    small = jnp.concatenate([squares_out[0], jnp.full((128,), count), by_y.reshape(width)])
    give, up, down = lax.optimization_barrier((give, up, down, basis_x_lo))[:3]
    got_a = lax.ppermute(give, "dp", XLO)
    got_up, got_down = send_z(up, down)
    part = chunk // 2
    second_up, second_down, a_first_1, a_second_3, own_a = pl.pallas_call(
        second_kernel,
        out_shape=(
            shape_of(chunk, width),
            shape_of(chunk, width),
            shape_of(part, cut),
            shape_of(part, cut),
            shape_of(2, part, cut),
        ),
        compiler_params=PARAMS,
        name="second_kernel",
    )(after(keep, by_y, cov_got_up, cov_got_down), got_a, got_up, got_down, first_1, second_3)
    second_got_up, second_got_down = send_z(second_up, second_down)

    small = after(small, second_up)
    small = small + lax.ppermute(small, "dp", XLO)
    small = small + lax.ppermute(small, "dp", swap_z(1))
    y = fac % 4
    near = pl.BlockSpec((1, chunk, width - cut), lambda i, p: (1, 0, 0))
    third_in = (second_got_up, second_got_down, own_b, a_first_1, a_second_3, own_a)
    third_up, third_down, b_give, b_keep, a_keep = placed(
        third_kernel,
        after(place, small),
        (1,),
        [near, near] + [whole(t.shape) for t in third_in],
        [
            shape_of(part, cut),
            shape_of(part, cut),
            shape_of(chunk, width - cut),
            shape_of(chunk, width - cut, dtype=f32),
            shape_of(2, part, cut, dtype=f32),
        ],
        (got_up, got_down, *third_in),
    )
    b_got = lax.ppermute(b_give, "dp", XLO)
    a_via_up, a_via_down = send_z(third_up, third_down)
    small = after(small, b_give)
    small = small + lax.ppermute(small, "dp", swap_z(3))

    healthy_rows = f32(tokens * lax.axis_size("dp")) - small[width]
    out_total = lax.dynamic_slice_in_dim(small, (z * 2 + x) * chunk, chunk, 0)
    in_total = small[width + 128 :].reshape(2, 2, 2 * cols)
    in_total = jnp.where(y % 2 == 0, in_total, in_total[:, ::-1])
    in_total = jnp.where(y < 2, in_total, in_total[::-1]).reshape(4, 2 * cols)

    cov_next = forward_z(cov_got_up, cov_got_down, cov_rest[2], cov_rest[3])
    cov_next = lax.optimization_barrier((*cov_next, b_give))[:2]
    cov_via_up, cov_via_down = send_z(*cov_next)

    cov_first = added(cov_rest[0], cov_got_down[1], cov_via_up)
    cov_second = added(cov_rest[1], cov_got_up[1], cov_via_down)
    cov_give = jnp.where(x == 0, cov_second, cov_first).astype(bf16)
    cov_keep = jnp.where(x == 0, cov_first, cov_second)
    cov_give = after(cov_give, basis_all)
    cov_sum = added(cov_keep, lax.ppermute(cov_give, "dp", XLO))
    sum_out = cov_sum[:, :width]
    sum_in = cov_sum[:, width:].reshape(rows, 2, cols)
    in_keep = lax.dynamic_index_in_dim(sum_in, core, 1, keepdims=False)
    in_give = lax.dynamic_index_in_dim(sum_in, 1 - core, 1, keepdims=False).astype(bf16)
    in_got = lax.ppermute(in_give, "dp", CORE).astype(f32)

    scale_own = lax.dynamic_index_in_dim(scale_in, core, 0, keepdims=False).reshape(2, 4, cols)
    scale_own = jnp.where(fac // 4 == 0, scale_own, scale_own[::-1])
    scale_own = jnp.concatenate([scale_own[0], scale_own[1]], 1)
    lam_in = decay_rate * scale_own + blend_weight * in_total / healthy_rows
    scale_chip = lax.dynamic_slice_in_dim(scale_out, (z * 2 + x) * chunk, chunk, 0)
    lam_out = decay_rate * scale_chip + blend_weight * out_total / healthy_rows
    lam_out = (lam_out * healthy_rows)[:, None]
    damp = jnp.full((1, 2 * cols), damping * healthy_rows)

    turn_in = (a_keep, a_via_up, a_via_down, b_keep, b_got)
    turned = pl.pallas_call(
        turn_kernel,
        out_shape=shape_of(width, chunk),
        grid=(4,),
        in_specs=[whole(t.shape) for t in turn_in]
        + [pl.BlockSpec((1, width, 2 * cols), lambda i: (i, 0, 0)), whole((chunk, 1))]
        + [pl.BlockSpec((1, 1, 2 * cols), lambda i: (i, 0, 0)), whole((1, 2 * cols))],
        out_specs=whole((width, chunk)),
        scratch_shapes=[pltpu.VMEM((chunk, width), bf16), pltpu.VMEM((width, chunk), f32)],
        compiler_params=PARAMS,
        name="turn_kernel",
    )(*turn_in, basis_all, lam_out, lam_in[:, None], damp)
    spread = lax.all_to_all(turned.reshape(16, rows, chunk), "dp", split_axis=0, concat_axis=0)
    result = pl.pallas_call(
        last_kernel, out_shape=shape_of(2, rows, width), compiler_params=PARAMS, name="last_kernel"
    )(spread, basis_out)

    sum_in = jnp.where(core == 0, jnp.stack([in_keep, in_got], 1), jnp.stack([in_got, in_keep], 1))
    new_factor_in = decay_rate * factor_in + blend_weight * sum_in / healthy_rows
    new_factor_out = decay_rate * factor_out + blend_weight * sum_out / healthy_rows
    return (jnp.swapaxes(result, 0, 1), new_factor_in, new_factor_out)


def solution(mesh):
    in_specs = (
        P("dp", None),
        P("dp", "factor"),
        P("dp", None, "factor"),
        P("factor", None),
        P("dp", None, "factor"),
        P("dp", "factor"),
        P(),
        P("factor"),
        P("dp"),
    )
    out_specs = (P("dp", None, "factor"), P("dp", None, "factor"), P("dp", "factor"))
    return jax.shard_map(
        per_device, mesh=mesh, in_specs=in_specs, out_specs=out_specs, check_vma=False
    )
```

time: 569 us -> 176 us (0.31)
  waiting for transfers between devices: 386 us -> 20.6 us
  blocking collectives: 84.8 us -> 0 us
  Pallas kernels: 0 us -> 62.7 us
  starting transfers between devices: 0.24 us -> 47.1 us
  matrix products: 36.3 us -> 0 us
  local copies, waits for them, and re-layouts: 34.4 us -> 16.7 us
    unnamed x8 -> x1, waiting for transfers between devices: 171 us -> 0.02 us
    all_gather x3 -> x1, waiting for transfers between devices: 145 us -> 0.01 us  [per_device(): lax.all_gather(basis_rows, 'factor', axis=0, axis_index_groups=SAME_XHI)]
    reduce_scatter x1 -> x0, waiting for transfers between devices: 70.1 us -> none  [per_device(): lax.psum_scatter(cov_out.astype(jnp.bfloat16), 'dp', scatter_dimension=0,...]
    pallas_call x0 -> x10, Pallas kernels: none -> 62.7 us  [the longest x5 35.8 us: placed(): pl.pallas_call(kernel, out_shape=out_shapes, grid_spec=pltpu.PrefetchScal...]
    psum x1 -> x0, blocking collectives: 54.8 us -> none  [per_device(): in_total, out_total = lax.psum((in_squares, out_squares), 'dp')]
    dot_general x7 -> x0, matrix products: 36.3 us -> none  [the longest x1 9.51 us: per_device(): jnp.einsum('tak,tg->kag', eigen_in, output_eigenvalues, preferred_element...]
    ppermute x0 -> x29, starting transfers between devices: none -> 36 us  [the longest x10 13.4 us: send_z(): return (lax.ppermute(up, 'dp', UP), lax.ppermute(down, 'dp', DOWN))]
    all_gather x1 -> x0, blocking collectives: 29.9 us -> none  [per_device(): basis_rows = lax.all_gather(basis_in, 'factor', axis=2, tiled=True)]
  transfers between devices with their start and end apart: 6 -> 31, of which waited for: 6 -> 6; matrix products, arithmetic and copies ran while one was open for 7% -> 10% of each run, Pallas kernels for 0% -> 31%
where the time goes in v1:
time: 176 us; the launch traced here: 175 us
  Pallas kernels  62.7 us (36%)
  starting transfers between devices  47.1 us (27%)
  waiting for transfers between devices  20.6 us (12%)
  local copies, waits for them, and re-layouts  16.7 us (9%)
  between operations  15.1 us (9%)
  other arithmetic  12.6 us (7%)
    pallas_call x5, Pallas kernels, placed(): pl.pallas_call(kernel, out_shape=out_shapes, grid_spec=pltpu.PrefetchScal...  35.8 us
    ppermute x10, starting transfers between devices, send_z(): return (lax.ppermute(up, 'dp', UP), lax.ppermute(down, 'dp', DOWN))  13.4 us
    all_to_all x1, starting transfers between devices, per_device(): lax.all_to_all(turned.reshape(16, rows, chunk), 'dp', split_axis=0, conca...  11.1 us
    pallas_call x2, Pallas kernels, rotate(): pl.pallas_call(rotate_kernel, out_shape=shape_of(width, tokens), grid_spe...  10.8 us
    unnamed x66, local copies, waits for them, and re-layouts  9.8 us
    all_to_all x1, waiting for transfers between devices, per_device(): lax.all_to_all(turned.reshape(16, rows, chunk), 'dp', split_axis=0, conca...  7.73 us
    pallas_call x1, Pallas kernels, per_device(): pl.pallas_call(turn_kernel, out_shape=shape_of(width, chunk), grid=(4,),...  7.39 us
    ppermute x1, waiting for transfers between devices, per_device(): small = small + lax.ppermute(small, 'dp', swap_z(1))  6.83 us
  transfers between devices with their start and end apart: 31, of which 6 were waited for; matrix products, arithmetic and copies ran while one was open for 10% of the time, Pallas kernels for 31%

profile of v1, /device:TPU:1, one launch (start us, length us, event | category | flops | bytes accessed | tf_op | source)
XLA Modules:
  0.0 174.8 jit_solution(1231619474870040803)
XLA Ops:
  7.3 2.8 %constant_dynamic-slice_fusion.4 = bf16[512,1536]{1,0:T(8,128)(2,1)} fusion(bf16[512,3072]{1,0:T(8,128)(2,1)} %act_0.5, s32[]{:T(128)S(6)} %select_n.104), kind=kLoop, calls=%fused_computation.42 | loop fusion | bytes 3145732 | tf_op jit(solution)/shard_map/dynamic_slice | solution.py:262
  10.0 1.4 collective-permute-start
  12.9 5.5 %rotate_kernel.2.refs_0_ = bf16[1536,512]{1,0:T(8,128)(2,1)} custom-call(s32[4]{0:T(128)} %pad_add_fusion.place, bf16[512,1536]{1,0:T(8,128)(2,1)} %rows_0.1, s32[1,512]{1,0:T(1,128)} %bitcast.56, bf16[1536,1536]{1,0:T(8,128)(2,1)} %basis_out.1), custom_call_target="tpu_custom_call" | custom-call | tf_op jit(solution)/shard_map/rotate_kernel/pallas_call | solution.py:266
  18.4 2.9 %collective-permute-start.3 = (bf16[192,192]{1,0:T(8,128)(2,1)S(1)}, bf16[192,192]{1,0:T(8,128)(2,1)S(1)}, u32[]{:S(2)}, u32[]{:S(2)}) collective-permute-start(bf16[192,192]{1,0:T(8,128)(2,1)S(1)} %maximum_select_fusion.1), channel_id=1, source_target_pairs={{0,4},{1,5},{2,6},{3,7},{4,0},{5,1},{6,2},{7,3},{8,12},{9,13},{10,... | collective-permute-start | bytes 221192 | tf_op jit(solution)/shard_map/ppermute | solution.py:292
  21.7 0.8 collective-permute-done.1.marks_1
  22.5 5.3 %rotate_kernel.3.eigen_0 = bf16[1536,512]{1,0:T(8,128)(2,1)} custom-call(s32[4]{0:T(128)} %pad_add_fusion.place, bf16[512,1536]{1,0:T(8,128)(2,1)} %rows_0.1, s32[1,512]{1,0:T(1,128)} %bitcast.57, bf16[1536,1536]{1,0:T(8,128)(2,1)} %basis_out.1, bf16[1536,512]{1,0:T(8,128)(2,1)} %rotate_kernel.2.refs_0_), custom_call_target="tpu_custom_call", output_to_operand_aliasing={{}: (4, {})} | custom-call | tf_op jit(solution)/shard_map/rotate_kernel/pallas_call | solution.py:266
  28.4 1.7 collective-permute-start.7
  30.1 3.3 %collective-permute-start.6 = (bf16[192,384]{1,0:T(8,128)(2,1)S(1)}, bf16[192,384]{1,0:T(8,128)(2,1)S(1)}, u32[]{:S(2)}, u32[]{:S(2)}) collective-permute-start(bf16[192,384]{1,0:T(8,128)(2,1)S(1)} %pad_maximum_fusion.1), channel_id=1, source_target_pairs={{0,64},{8,72},{16,80},{24,88},{32,96},{40,104},{48,112},{56,120},{... | collective-permute-start | bytes 442376 | tf_op jit(solution)/shard_map/ppermute | solution.py:296
  33.4 0.7 collective-permute-start.5
  34.6 11.1 %cov_kernel.1 = (bf16[2,96,1920]{2,1,0:T(8,128)(2,1)}, bf16[2,96,1920]{2,1,0:T(8,128)(2,1)}, bf16[4,96,1920]{2,1,0:T(8,128)(2,1)}) custom-call(s32[4]{0:T(128)} %pad_add_fusion.place, bf16[512,1536]{1,0:T(8,128)(2,1)} %rows_0.1, bf16[512,1536]{1,0:T(8,128)(2,1)} %collective-permute-done.4.cot_1.rows_1, s32[1,512]{1,0:T(1,128)} %bitcast.58, ...), custom_call_target="tpu_custom_call" | custom-call | tf_op jit(solution)/shard_map/cov_kernel/pallas_call | solution.py:69
  45.8 2.5 %collective-permute-start.10 = (bf16[2,96,1920]{2,1,0:T(8,128)(2,1)}, bf16[2,96,1920]{2,1,0:T(8,128)(2,1)S(1)}, u32[]{:S(2)}, u32[]{:S(2)}) collective-permute-start(bf16[2,96,1920]{2,1,0:T(8,128)(2,1)} %get-tuple-element.54), channel_id=1, source_target_pairs={{0,96},{8,104},{16,112},{24,120},{32,0},{40,8},{48,16},{56,24},{64... | collective-permute-start | bytes 2211848 | tf_op jit(solution)/shard_map/ppermute | solution.py:53
  48.8 1.2 copy-done.3
  50.0 10.8 %grad_kernel.1 = (bf16[4,192,512]{2,1,0:T(8,128)(2,1)}, bf16[4,192,512]{2,1,0:T(8,128)(2,1)}, bf16[2,192,1024]{2,1,0:T(8,128)(2,1)}, bf16[2,192,1024]{2,1,0:T(8,...) custom-call(s32[4]{0:T(128)} %pad_add_fusion.place, ...), custom_call_target="tpu_custom_call" | custom-call | tf_op jit(solution)/shard_map/grad_kernel/pallas_call | solution.py:69
  60.8 3.5 %collective-permute-done.9 = bf16[2,96,1920]{2,1,0:T(8,128)(2,1)S(1)} collective-permute-done((bf16[2,96,1920]{2,1,0:T(8,128)(2,1)}, bf16[2,96,1920]{2,1,0:T(8,128)(2,1)S(1)}, u32[]{:S(2)}, u32[]{:S(2)}) %collective-permute-start.9) | collective-permute-done | bytes 737312 | tf_op jit(solution)/shard_map/ppermute | solution.py:53
  64.4 0.8 copy-done.16
  65.2 3.1 %rows_kernel.1 = bf16[4,2,192,384]{3,2,1,0:T(8,128)(2,1)} custom-call(s32[4]{0:T(128)} %pad_add_fusion.place, bf16[4,192,384]{2,1,0:T(8,128)(2,1)} %copy-done.8, bf16[4,192,384]{2,1,0:T(8,128)(2,1)} %copy-done.16), custom_call_target="tpu_custom_call" | custom-call | tf_op jit(solution)/shard_map/rows_kernel/pallas_call | solution.py:69
  68.9 2.7 %collective-permute-start.16 = (bf16[2,192,1024]{2,1,0:T(8,128)(2,1)}, bf16[2,192,1024]{2,1,0:T(8,128)(2,1)S(1)}, u32[]{:S(2)}, u32[]{:S(2)}) collective-permute-start(bf16[2,192,1024]{2,1,0:T(8,128)(2,1)} %get-tuple-element.65), channel_id=1, source_target_pairs={{0,96},{8,104},{16,112},{24,120},{32,0},{40,8},{48,16},{56,24},{64... | collective-permute-start | bytes 2359304 | tf_op jit(solution)/shard_map/ppermute | solution.py:53
  71.6 6.7 %squares_kernel.1 = (f32[1,384]{1,0:T(1,128)}, f32[1,1536]{1,0:T(1,128)}) custom-call(s32[4]{0:T(128)} %pad_add_fusion.place, bf16[512,3072]{1,0:T(8,128)(2,1)} %act_0.5, bf16[512,1536]{1,0:T(8,128)(2,1)} %copy-done.2, s32[1,512]{1,0:T(1,128)} %bitcast.59, s32[1,512]{1,0:T(1,128)} %copy-done.26, bf16[1536,384]{1,0:T(8,128)(2,1)} %bitcast.48, ...), custom_call_target="tpu_custom_call" | custom-call | tf_op jit(solution)/shard_map/squares_kernel/pallas_call | solution.py:69
  78.3 1.3 collective-permute-start.12
  79.8 1.4 collective-permute-done.12
  81.2 0.7 pad_maximum_fusion.4
  81.9 2.8 %collective-permute-start.13 = (f32[2,384]{1,0:T(2,128)S(1)}, f32[2,384]{1,0:T(2,128)S(1)}, u32[]{:S(2)}, u32[]{:S(2)}) collective-permute-start(f32[2,384]{1,0:T(2,128)S(1)} %pad_maximum_fusion.4), channel_id=1, source_target_pairs={{0,2},{1,3},{2,0},{3,1},{4,6},{5,7},{6,4},{7,5},{8,10},{9,11},{10,... | collective-permute-start | bytes 9224 | tf_op jit(solution)/shard_map/ppermute | solution.py:355
  85.3 0.7 reduce
  86.0 0.7 pad_maximum_fusion.3
  88.8 3.5 %second_kernel.1 = (bf16[192,1536]{1,0:T(8,128)(2,1)}, bf16[192,1536]{1,0:T(8,128)(2,1)}, bf16[96,512]{1,0:T(8,128)(2,1)}, bf16[96,512]{1,0:T(8,128)(2,1)}, bf16[2,96,512]{2,1,0:T(8,128)(2,1)}) custom-call(bf16[4,192,512]{2,1,0:T(8,128)(2,1)} %get-tuple-element.59.keep, bf16[4,192,512]{2,1,0:T(8,128)(2,1)} %copy-done.15, bf16[2,192,1024]{2,1,0:T(8,128)(2,1)} %copy-done.6, ...), custom_call_target="tpu_custom_call" | custom-call | tf_op jit(solution)/shard_map/second_kernel/pallas_call | solution.py:362
  92.3 1.2 collective-permute-start.17
  93.5 2.7 %collective-permute-start.20 = (bf16[192,1536]{1,0:T(8,128)(2,1)}, bf16[192,1536]{1,0:T(8,128)(2,1)S(1)}, u32[]{:S(2)}, u32[]{:S(2)}) collective-permute-start(bf16[192,1536]{1,0:T(8,128)(2,1)} %get-tuple-element.71), channel_id=1, source_target_pairs={{0,96},{8,104},{16,112},{24,120},{32,0},{40,8},{48,16},{56,24},{64... | collective-permute-start | bytes 1769480 | tf_op jit(solution)/shard_map/ppermute | solution.py:53
  96.4 1.1 fusion.3
  97.5 6.8 %collective-permute-done.18 = f32[3200]{0:T(1024)S(1)} collective-permute-done((f32[3200]{0:T(1024)S(1)}, f32[3200]{0:T(1024)S(1)}, u32[]{:S(2)}, u32[]{:S(2)}) %collective-permute-start.18) | collective-permute-done | bytes 12832 | tf_op jit(solution)/shard_map/ppermute | solution.py:378
  104.4 0.8 copy-done.17
  105.3 4.2 %third_kernel.1 = (bf16[96,512]{1,0:T(8,128)(2,1)}, bf16[96,512]{1,0:T(8,128)(2,1)}, bf16[192,1024]{1,0:T(8,128)(2,1)}, f32[192,1024]{1,0:T(8,128)}, f32[2,96,512]{2,1,0:T(8,128)}) custom-call(s32[4]{0:T(128)} %pad_add_fusion.place, bf16[2,192,1024]{2,1,0:T(8,128)(2,1)} %copy-done.6, bf16[2,192,1024]{2,1,0:T(8,128)(2,1)} %copy-done.7, ...), custom_call_target="tpu_custom_call" | custom-call | tf_op jit(solution)/shard_map/third_kernel/pallas_call | solution.py:69
  109.5 3.0 %collective-permute-start.24 = (f32[3200]{0:T(1024)S(1)}, f32[3200]{0:T(1024)S(1)}, u32[]{:S(2)}, u32[]{:S(2)}) collective-permute-start(f32[3200]{0:T(1024)S(1)} %add.109), channel_id=1, source_target_pairs={{0,96},{8,104},{16,112},{24,120},{32,64},{40,72},{48,80},{56,88},{... | collective-permute-start | bytes 38408 | tf_op jit(solution)/shard_map/ppermute | solution.py:399
  112.7 2.5 %collective-permute-start.26 = (bf16[96,1920]{1,0:T(8,128)(2,1)}, bf16[96,1920]{1,0:T(8,128)(2,1)}, u32[]{:S(2)}, u32[]{:S(2)}) collective-permute-start(bf16[96,1920]{1,0:T(8,128)(2,1)} %get-tuple-element.83), channel_id=1, source_target_pairs={{0,96},{8,104},{16,112},{24,120},{32,0},{40,8},{48,16},{56,24},{64... | collective-permute-start | bytes 1105928 | tf_op jit(solution)/shard_map/ppermute | solution.py:53
  116.7 2.7 %collective-permute-start.22 = (bf16[96,512]{1,0:T(8,128)(2,1)}, bf16[96,512]{1,0:T(8,128)(2,1)S(1)}, u32[]{:S(2)}, u32[]{:S(2)}) collective-permute-start(bf16[96,512]{1,0:T(8,128)(2,1)} %get-tuple-element.77), channel_id=1, source_target_pairs={{0,96},{8,104},{16,112},{24,120},{32,0},{40,8},{48,16},{56,24},{64... | collective-permute-start | bytes 294920 | tf_op jit(solution)/shard_map/ppermute | solution.py:53
  119.4 0.7 add.112
  121.6 2.1 %select_convert_fusion = bf16[96,1920]{1,0:T(8,128)(2,1)} fusion(bf16[96,1920]{1,0:T(8,128)(2,1)S(1)} %collective-permute-done.25, bf16[96,1920]{1,0:T(8,128)(2,1)} %collective-permute-done.26, pred[]{:T(512)S(6)} %eq.22, bf16[2,96,1920]{2,1,0:T(8,128)(2,1)S(1)} %copy-done.11, bf16[2,96,1920]{2,1,0:T(8,128)(2,1)S(1)} %copy-done.14, ...), kind=kLoop, calls=%fused_computation.3 | loop fusion | flops 2211840 | bytes 2580481 | tf_op jit(solution)/shard_map/convert_element_type | solution.py:413
  123.7 1.2 collective-permute-start.27
  125.5 0.8 fusion.11
  126.3 0.8 copy.29.lam_out
  127.8 7.4 %turn_kernel.1 = bf16[1536,192]{1,0:T(8,128)(2,1)} custom-call(f32[2,96,512]{2,1,0:T(8,128)} %get-tuple-element.75.keep_a, bf16[96,512]{1,0:T(8,128)(2,1)} %copy-done.21, bf16[96,512]{1,0:T(8,128)(2,1)} %copy-done.22, f32[192,1024]{1,0:T(8,128)} %get-tuple-element.78.keep_b, bf16[192,1024]{1,0:T(8,128)(2,1)} %collective-permute-done.23.got_b, ...), custom_call_target="tpu_custom_call" | custom-call | tf_op jit(solution)/shard_map/turn_kernel/pallas_call | solution.py:433
  135.2 11.1 %all-to-all-start = ((bf16[16,96,192]{2,1,0:T(8,128)(2,1)}), bf16[16,96,192]{2,1,0:T(8,128)(2,1)S(1)}, u32[]{:S(2)}, u32[]{:S(2)}) async-start(bf16[16,96,192]{2,1,0:T(8,128)(2,1)} %bitcast.49), calls=%async_computation | async-start | bytes 1572864 | tf_op jit(solution)/shard_map/all_to_all | solution.py:445
  146.3 1.7 convert_add_fusion
  148.6 2.0 %fusion.1 = f32[96,1536]{1,0:T(8,128)} fusion(f32[96,1920]{1,0:T(8,128)S(1)} %convert_add_fusion, f32[96,1536]{1,0:T(8,128)} %param.14, f32[]{:T(128)} %bitcast.13), kind=kLoop, calls=%fused_computation.8 | loop fusion | flops 589824 | bytes 1769476 | tf_op jit(solution)/shard_map/add | solution.py:452
  150.8 0.8 copy.34
  151.6 7.7 %all-to-all-done.spread = bf16[16,96,192]{2,1,0:T(8,128)(2,1)S(1)} async-done(((bf16[16,96,192]{2,1,0:T(8,128)(2,1)}), bf16[16,96,192]{2,1,0:T(8,128)(2,1)S(1)}, u32[]{:S(2)}, u32[]{:S(2)}) %all-to-all-start) | async-done | bytes 589856 | tf_op jit(solution)/shard_map/all_to_all | solution.py:445
  159.3 0.9 copy-done.5
  160.3 5.2 %last_kernel.1 = bf16[2,96,1536]{2,1,0:T(8,128)(2,1)} custom-call(bf16[16,96,192]{2,1,0:T(8,128)(2,1)} %copy-done.5, bf16[1536,1536]{1,0:T(8,128)(2,1)} %basis_out.1), custom_call_target="tpu_custom_call" | custom-call | tf_op jit(solution)/shard_map/last_kernel/pallas_call | solution.py:446
  165.5 2.5 %copy.33 = bf16[96,2,1536]{2,1,0:T(2,128)(2,1)} copy(bf16[96,2,1536]{2,0,1:T(8,128)(2,1)} %bitcast.50) | data formatting | bytes 1179648
  (134 shorter events, 12.0 us)
Async XLA Ops:
  7.2 72.4 %copy-start = (f32[2,1536]{1,0:T(2,128)S(1)}, f32[2,1536]{1,0:T(2,128)}, u32[]{:S(2)}) copy-start(f32[2,1536]{1,0:T(2,128)} %param.15) | copy-start | bytes 36868
  7.2 116.5 %all-gather.2.cloned.1.call-start = ((), (), s32[]{:S(2)}) async-start(), calls=%async_computation.1 | async-start | bytes 5898240 | tf_op jit(solution)/shard_map/all_gather | solution.py:342
  7.2 4.2 %copy-start.1 = (bf16[512,1536]{1,0:T(8,128)(2,1)S(1)}, bf16[512,1536]{1,0:T(8,128)(2,1)}, u32[]{:S(2)}) copy-start(bf16[512,1536]{1,0:T(8,128)(2,1)} %rows_0.1) | copy-start | bytes 4718596
  7.3 4.2 %copy-start.19 = (bf16[96,2,192]{2,1,0:T(2,128)(2,1)S(1)}, bf16[96,2,192]{2,1,0:T(2,128)(2,1)}, u32[]{:S(2)}) copy-start(bf16[96,2,192]{2,1,0:T(2,128)(2,1)} %param.11) | copy-start | bytes 221188
  10.0 23.3 %collective-permute-start = (bf16[512,1536]{1,0:T(8,128)(2,1)}, bf16[512,1536]{1,0:T(8,128)(2,1)S(1)}, u32[]{:S(2)}, u32[]{:S(2)}) collective-permute-start(bf16[512,1536]{1,0:T(8,128)(2,1)} %constant_dynamic-slice_fusion.4), channel_id=1, source_target_pairs={{0,8},{8,0},{16,24},{24,16},{32,40},{40,32},{48,56},{56,48},{64,72... | collective-permute-start | bytes 4718600 | tf_op jit(solution)/shard_map/ppermute | solution.py:263
  11.5 22.6 %collective-permute-start.4 = (bf16[512,1536]{1,0:T(8,128)(2,1)S(1)}, bf16[512,1536]{1,0:T(8,128)(2,1)}, u32[]{:S(2)}, u32[]{:S(2)}) collective-permute-start(bf16[512,1536]{1,0:T(8,128)(2,1)S(1)} %copy-done.1), channel_id=1, source_target_pairs={{0,8},{8,0},{16,24},{24,16},{32,40},{40,32},{48,56},{56,48},{64,72... | collective-permute-start | bytes 4718600 | tf_op jit(solution)/shard_map/ppermute | solution.py:261
  11.7 6.7 %collective-permute-start.2 = (bf16[96,192]{1,0:T(8,128)(2,1)S(1)}, bf16[96,192]{1,0:T(8,128)(2,1)S(1)}, u32[]{:S(2)}, u32[]{:S(2)}) collective-permute-start(bf16[96,192]{1,0:T(8,128)(2,1)S(1)} %bitcast.62), channel_id=1, source_target_pairs={{0,8},{8,0},{16,24},{24,16},{32,40},{40,32},{48,56},{56,48},{64,72... | collective-permute-start | bytes 110600 | tf_op jit(solution)/shard_map/ppermute | solution.py:258
  12.9 8.4 %copy-start.23 = (s32[512]{0:T(512)S(1)}, s32[512]{0:T(512)}, u32[]{:S(2)}) copy-start(s32[512]{0:T(512)} %param.17) | copy-start | bytes 6148
  18.4 9.4 %collective-permute-start.3 = (bf16[192,192]{1,0:T(8,128)(2,1)S(1)}, bf16[192,192]{1,0:T(8,128)(2,1)S(1)}, u32[]{:S(2)}, u32[]{:S(2)}) collective-permute-start(bf16[192,192]{1,0:T(8,128)(2,1)S(1)} %maximum_select_fusion.1), channel_id=1, source_target_pairs={{0,4},{1,5},{2,6},{3,7},{4,0},{5,1},{6,2},{7,3},{8,12},{9,13},{10,... | collective-permute-start | bytes 221192 | tf_op jit(solution)/shard_map/ppermute | solution.py:292
  21.3 1.2 collective-permute-start.1
  22.5 5.3 %copy-start.26 = (s32[1,512]{1,0:T(1,128)}, s32[1,512]{1,0:T(1,128)S(1)}, u32[]{:S(2)}) copy-start(s32[1,512]{1,0:T(1,128)S(1)} %collective-permute-done.1.marks_1) | copy-start | bytes 6148
  27.8 21.0 %collective-permute-start.8 = (bf16[1536,512]{1,0:T(8,128)(2,1)}, bf16[1536,512]{1,0:T(8,128)(2,1)S(1)}, u32[]{:S(2)}, u32[]{:S(2)}) collective-permute-start(bf16[1536,512]{1,0:T(8,128)(2,1)} %rotate_kernel.3.eigen_0), channel_id=1, source_target_pairs={{0,8},{8,0},{16,24},{24,16},{32,40},{40,32},{48,56},{56,48},{64,72... | collective-permute-start | bytes 4718600 | tf_op jit(solution)/shard_map/ppermute | solution.py:294
  28.4 17.5 %collective-permute-start.7 = (bf16[192,384]{1,0:T(8,128)(2,1)S(1)}, bf16[192,384]{1,0:T(8,128)(2,1)S(1)}, u32[]{:S(2)}, u32[]{:S(2)}) collective-permute-start(bf16[192,384]{1,0:T(8,128)(2,1)S(1)} %pad_maximum_fusion.1), channel_id=1, source_target_pairs={{0,32},{8,40},{16,48},{24,56},{32,64},{40,72},{48,80},{56,88},{64,... | collective-permute-start | bytes 442376 | tf_op jit(solution)/shard_map/ppermute | solution.py:296
  30.1 18.2 %collective-permute-start.6 = (bf16[192,384]{1,0:T(8,128)(2,1)S(1)}, bf16[192,384]{1,0:T(8,128)(2,1)S(1)}, u32[]{:S(2)}, u32[]{:S(2)}) collective-permute-start(bf16[192,384]{1,0:T(8,128)(2,1)S(1)} %pad_maximum_fusion.1), channel_id=1, source_target_pairs={{0,64},{8,72},{16,80},{24,88},{32,96},{40,104},{48,112},{56,120},{... | collective-permute-start | bytes 442376 | tf_op jit(solution)/shard_map/ppermute | solution.py:296
  33.4 14.9 %collective-permute-start.5 = (bf16[192,384]{1,0:T(8,128)(2,1)S(1)}, bf16[192,384]{1,0:T(8,128)(2,1)S(1)}, u32[]{:S(2)}, u32[]{:S(2)}) collective-permute-start(bf16[192,384]{1,0:T(8,128)(2,1)S(1)} %pad_maximum_fusion.1), channel_id=1, source_target_pairs={{0,96},{8,104},{16,112},{24,120},{32,0},{40,8},{48,16},{56,24},{64... | collective-permute-start | bytes 442376 | tf_op jit(solution)/shard_map/ppermute | solution.py:296
  45.6 18.7 %collective-permute-start.9 = (bf16[2,96,1920]{2,1,0:T(8,128)(2,1)}, bf16[2,96,1920]{2,1,0:T(8,128)(2,1)S(1)}, u32[]{:S(2)}, u32[]{:S(2)}) collective-permute-start(bf16[2,96,1920]{2,1,0:T(8,128)(2,1)} %get-tuple-element.49), channel_id=1, source_target_pairs={{0,32},{8,40},{16,48},{24,56},{32,64},{40,72},{48,80},{56,88},{64,... | collective-permute-start | bytes 2211848 | tf_op jit(solution)/shard_map/ppermute | solution.py:53
  45.8 18.5 %collective-permute-start.10 = (bf16[2,96,1920]{2,1,0:T(8,128)(2,1)}, bf16[2,96,1920]{2,1,0:T(8,128)(2,1)S(1)}, u32[]{:S(2)}, u32[]{:S(2)}) collective-permute-start(bf16[2,96,1920]{2,1,0:T(8,128)(2,1)} %get-tuple-element.54), channel_id=1, source_target_pairs={{0,96},{8,104},{16,112},{24,120},{32,0},{40,8},{48,16},{56,24},{64... | collective-permute-start | bytes 2211848 | tf_op jit(solution)/shard_map/ppermute | solution.py:53
  48.4 16.0 %copy-start.8 = (bf16[4,192,384]{2,1,0:T(8,128)(2,1)}, bf16[4,192,384]{2,1,0:T(8,128)(2,1)S(1)}, u32[]{:S(2)}) copy-start(bf16[4,192,384]{2,1,0:T(8,128)(2,1)S(1)} %pad_maximum_fusion.own) | copy-start | bytes 1769476
  48.4 16.0 %collective-permute-start.11 = (bf16[4,192,384]{2,1,0:T(8,128)(2,1)S(1)}, bf16[4,192,384]{2,1,0:T(8,128)(2,1)S(1)}, u32[]{:S(2)}, u32[]{:S(2)}) collective-permute-start(bf16[4,192,384]{2,1,0:T(8,128)(2,1)S(1)} %pad_maximum_fusion.own), channel_id=1, source_target_pairs={{0,16},{8,24},{16,0},{24,8},{32,48},{40,56},{48,32},{56,40},{64,80... | collective-permute-start | bytes 1769480 | tf_op jit(solution)/shard_map/ppermute | solution.py:318
  64.4 3.9 %copy-start.9 = (bf16[2,96,1920]{2,1,0:T(8,128)(2,1)}, bf16[2,96,1920]{2,1,0:T(8,128)(2,1)S(1)}, u32[]{:S(2)}) copy-start(bf16[2,96,1920]{2,1,0:T(8,128)(2,1)S(1)} %collective-permute-done.9) | copy-start | bytes 2211844
  64.4 3.9 %copy-start.12 = (bf16[2,96,1920]{2,1,0:T(8,128)(2,1)}, bf16[2,96,1920]{2,1,0:T(8,128)(2,1)S(1)}, u32[]{:S(2)}) copy-start(bf16[2,96,1920]{2,1,0:T(8,128)(2,1)S(1)} %collective-permute-done.10) | copy-start | bytes 2211844
  68.3 19.1 %collective-permute-start.14 = (bf16[4,192,512]{2,1,0:T(8,128)(2,1)}, bf16[4,192,512]{2,1,0:T(8,128)(2,1)S(1)}, u32[]{:S(2)}, u32[]{:S(2)}) collective-permute-start(bf16[4,192,512]{2,1,0:T(8,128)(2,1)} %get-tuple-element.63), channel_id=1, source_target_pairs={{0,16},{8,24},{16,0},{24,8},{32,48},{40,56},{48,32},{56,40},{64,80... | collective-permute-start | bytes 2359304 | tf_op jit(solution)/shard_map/ppermute | solution.py:359
  68.9 18.7 %collective-permute-start.15 = (bf16[2,192,1024]{2,1,0:T(8,128)(2,1)}, bf16[2,192,1024]{2,1,0:T(8,128)(2,1)S(1)}, u32[]{:S(2)}, u32[]{:S(2)}) collective-permute-start(bf16[2,192,1024]{2,1,0:T(8,128)(2,1)} %get-tuple-element.64), channel_id=1, source_target_pairs={{0,32},{8,40},{16,48},{24,56},{32,64},{40,72},{48,80},{56,88},{64,... | collective-permute-start | bytes 2359304 | tf_op jit(solution)/shard_map/ppermute | solution.py:53
  68.9 18.7 %collective-permute-start.16 = (bf16[2,192,1024]{2,1,0:T(8,128)(2,1)}, bf16[2,192,1024]{2,1,0:T(8,128)(2,1)S(1)}, u32[]{:S(2)}, u32[]{:S(2)}) collective-permute-start(bf16[2,192,1024]{2,1,0:T(8,128)(2,1)} %get-tuple-element.65), channel_id=1, source_target_pairs={{0,96},{8,104},{16,112},{24,120},{32,0},{40,8},{48,16},{56,24},{64... | collective-permute-start | bytes 2359304 | tf_op jit(solution)/shard_map/ppermute | solution.py:53
  71.6 13.1 %copy-start.24 = (s32[512]{0:T(512)S(1)}, s32[512]{0:T(512)}, u32[]{:S(2)}) copy-start(s32[512]{0:T(512)} %param.17) | copy-start | bytes 6148
  71.6 13.1 %copy-start.27 = (s32[1,512]{1,0:T(1,128)S(1)}, s32[1,512]{1,0:T(1,128)}, u32[]{:S(2)}) copy-start(s32[1,512]{1,0:T(1,128)} %copy-done.26) | copy-start | bytes 6148
  78.3 2.9 %collective-permute-start.12 = (f32[1,384]{1,0:T(1,128)}, f32[1,384]{1,0:T(1,128)S(1)}, u32[]{:S(2)}, u32[]{:S(2)}) collective-permute-start(f32[1,384]{1,0:T(1,128)} %get-tuple-element.57), channel_id=1, source_target_pairs={{0,1},{1,0},{2,3},{3,2},{4,5},{5,4},{6,7},{7,6},{8,9},{9,8},{10,11... | collective-permute-start | bytes 4616 | tf_op jit(solution)/shard_map/ppermute | solution.py:354
  81.9 4.1 %collective-permute-start.13 = (f32[2,384]{1,0:T(2,128)S(1)}, f32[2,384]{1,0:T(2,128)S(1)}, u32[]{:S(2)}, u32[]{:S(2)}) collective-permute-start(f32[2,384]{1,0:T(2,128)S(1)} %pad_maximum_fusion.4), channel_id=1, source_target_pairs={{0,2},{1,3},{2,0},{3,1},{4,6},{5,7},{6,4},{7,5},{8,10},{9,11},{10,... | collective-permute-start | bytes 9224 | tf_op jit(solution)/shard_map/ppermute | solution.py:355
  88.8 7.6 %copy-start.4 = (bf16[4,96,1920]{2,1,0:T(8,128)(2,1)S(1)}, bf16[4,96,1920]{2,1,0:T(8,128)(2,1)}, u32[]{:S(2)}) copy-start(bf16[4,96,1920]{2,1,0:T(8,128)(2,1)} %get-tuple-element.81) | copy-start | bytes 4423684
  88.8 7.6 %copy-start.10 = (bf16[2,96,1920]{2,1,0:T(8,128)(2,1)S(1)}, bf16[2,96,1920]{2,1,0:T(8,128)(2,1)}, u32[]{:S(2)}) copy-start(bf16[2,96,1920]{2,1,0:T(8,128)(2,1)} %copy-done.9) | copy-start | bytes 2211844
  88.8 7.6 %copy-start.13 = (bf16[2,96,1920]{2,1,0:T(8,128)(2,1)S(1)}, bf16[2,96,1920]{2,1,0:T(8,128)(2,1)}, u32[]{:S(2)}) copy-start(bf16[2,96,1920]{2,1,0:T(8,128)(2,1)} %copy-done.12) | copy-start | bytes 2211844
  92.3 12.0 %collective-permute-start.19 = (bf16[192,1536]{1,0:T(8,128)(2,1)}, bf16[192,1536]{1,0:T(8,128)(2,1)S(1)}, u32[]{:S(2)}, u32[]{:S(2)}) collective-permute-start(bf16[192,1536]{1,0:T(8,128)(2,1)} %get-tuple-element.68), channel_id=1, source_target_pairs={{0,32},{8,40},{16,48},{24,56},{32,64},{40,72},{48,80},{56,88},{64,... | collective-permute-start | bytes 1769480 | tf_op jit(solution)/shard_map/ppermute | solution.py:53
  92.3 3.8 %collective-permute-start.17 = (f32[3200]{0:T(1024)S(1)}, f32[3200]{0:T(1024)S(1)}, u32[]{:S(2)}, u32[]{:S(2)}) collective-permute-start(f32[3200]{0:T(1024)S(1)} %pad_maximum_fusion.2), channel_id=1, source_target_pairs={{0,16},{8,24},{16,0},{24,8},{32,48},{40,56},{48,32},{56,40},{64,80... | collective-permute-start | bytes 38408 | tf_op jit(solution)/shard_map/ppermute | solution.py:377
  93.5 10.8 %collective-permute-start.20 = (bf16[192,1536]{1,0:T(8,128)(2,1)}, bf16[192,1536]{1,0:T(8,128)(2,1)S(1)}, u32[]{:S(2)}, u32[]{:S(2)}) collective-permute-start(bf16[192,1536]{1,0:T(8,128)(2,1)} %get-tuple-element.71), channel_id=1, source_target_pairs={{0,96},{8,104},{16,112},{24,120},{32,0},{40,8},{48,16},{56,24},{64... | collective-permute-start | bytes 1769480 | tf_op jit(solution)/shard_map/ppermute | solution.py:53
  96.2 8.1 %collective-permute-start.18 = (f32[3200]{0:T(1024)S(1)}, f32[3200]{0:T(1024)S(1)}, u32[]{:S(2)}, u32[]{:S(2)}) collective-permute-start(f32[3200]{0:T(1024)S(1)} %add.108), channel_id=1, source_target_pairs={{0,32},{8,40},{16,48},{24,56},{32,0},{40,8},{48,16},{56,24},{64,96... | collective-permute-start | bytes 38408 | tf_op jit(solution)/shard_map/ppermute | solution.py:378
  105.3 16.2 %copy-start.11 = (bf16[2,96,1920]{2,1,0:T(8,128)(2,1)S(1)}, bf16[2,96,1920]{2,1,0:T(8,128)(2,1)}, u32[]{:S(2)}) copy-start(bf16[2,96,1920]{2,1,0:T(8,128)(2,1)} %copy-done.9) | copy-start | bytes 2211844
  105.3 16.2 %copy-start.14 = (bf16[2,96,1920]{2,1,0:T(8,128)(2,1)S(1)}, bf16[2,96,1920]{2,1,0:T(8,128)(2,1)}, u32[]{:S(2)}) copy-start(bf16[2,96,1920]{2,1,0:T(8,128)(2,1)} %copy-done.12) | copy-start | bytes 2211844
  109.5 6.6 %collective-permute-start.24 = (f32[3200]{0:T(1024)S(1)}, f32[3200]{0:T(1024)S(1)}, u32[]{:S(2)}, u32[]{:S(2)}) collective-permute-start(f32[3200]{0:T(1024)S(1)} %add.109), channel_id=1, source_target_pairs={{0,96},{8,104},{16,112},{24,120},{32,64},{40,72},{48,80},{56,88},{... | collective-permute-start | bytes 38408 | tf_op jit(solution)/shard_map/ppermute | solution.py:399
  112.5 9.0 %collective-permute-start.25 = (bf16[96,1920]{1,0:T(8,128)(2,1)}, bf16[96,1920]{1,0:T(8,128)(2,1)S(1)}, u32[]{:S(2)}, u32[]{:S(2)}) collective-permute-start(bf16[96,1920]{1,0:T(8,128)(2,1)} %get-tuple-element.82), channel_id=1, source_target_pairs={{0,32},{8,40},{16,48},{24,56},{32,64},{40,72},{48,80},{56,88},{64,... | collective-permute-start | bytes 1105928 | tf_op jit(solution)/shard_map/ppermute | solution.py:53
  112.7 8.9 %collective-permute-start.26 = (bf16[96,1920]{1,0:T(8,128)(2,1)}, bf16[96,1920]{1,0:T(8,128)(2,1)}, u32[]{:S(2)}, u32[]{:S(2)}) collective-permute-start(bf16[96,1920]{1,0:T(8,128)(2,1)} %get-tuple-element.83), channel_id=1, source_target_pairs={{0,96},{8,104},{16,112},{24,120},{32,0},{40,8},{48,16},{56,24},{64... | collective-permute-start | bytes 1105928 | tf_op jit(solution)/shard_map/ppermute | solution.py:53
  115.8 11.3 %collective-permute-start.23 = (bf16[192,1024]{1,0:T(8,128)(2,1)}, bf16[192,1024]{1,0:T(8,128)(2,1)}, u32[]{:S(2)}, u32[]{:S(2)}) collective-permute-start(bf16[192,1024]{1,0:T(8,128)(2,1)} %get-tuple-element.79), channel_id=1, source_target_pairs={{0,16},{8,24},{16,0},{24,8},{32,48},{40,56},{48,32},{56,40},{64,80... | collective-permute-start | bytes 1179656 | tf_op jit(solution)/shard_map/ppermute | solution.py:396
  116.1 11.0 %collective-permute-start.21 = (bf16[96,512]{1,0:T(8,128)(2,1)}, bf16[96,512]{1,0:T(8,128)(2,1)S(1)}, u32[]{:S(2)}, u32[]{:S(2)}) collective-permute-start(bf16[96,512]{1,0:T(8,128)(2,1)} %get-tuple-element.76), channel_id=1, source_target_pairs={{0,32},{8,40},{16,48},{24,56},{32,64},{40,72},{48,80},{56,88},{64,... | collective-permute-start | bytes 294920 | tf_op jit(solution)/shard_map/ppermute | solution.py:53
  116.7 10.4 %collective-permute-start.22 = (bf16[96,512]{1,0:T(8,128)(2,1)}, bf16[96,512]{1,0:T(8,128)(2,1)S(1)}, u32[]{:S(2)}, u32[]{:S(2)}) collective-permute-start(bf16[96,512]{1,0:T(8,128)(2,1)} %get-tuple-element.77), channel_id=1, source_target_pairs={{0,96},{8,104},{16,112},{24,120},{32,0},{40,8},{48,16},{56,24},{64... | collective-permute-start | bytes 294920 | tf_op jit(solution)/shard_map/ppermute | solution.py:53
  121.5 3.3 %copy-start.29 = (f32[4,1,192]{2,1,0:T(1,128)S(1)}, f32[4,1,192]{2,1,0:T(1,128)}, u32[]{:S(2)}) copy-start(f32[4,1,192]{2,1,0:T(1,128)} %get-tuple-element.99) | copy-start | bytes 9220
  123.7 22.6 %collective-permute-start.27 = (bf16[96,1920]{1,0:T(8,128)(2,1)}, bf16[96,1920]{1,0:T(8,128)(2,1)}, u32[]{:S(2)}, u32[]{:S(2)}) collective-permute-start(bf16[96,1920]{1,0:T(8,128)(2,1)} %select_convert_fusion), channel_id=1, source_target_pairs={{0,16},{8,24},{16,0},{24,8},{32,48},{40,56},{48,32},{56,40},{64,80... | collective-permute-start | bytes 1105928 | tf_op jit(solution)/shard_map/ppermute | solution.py:416
  135.2 24.2 %all-to-all-start = ((bf16[16,96,192]{2,1,0:T(8,128)(2,1)}), bf16[16,96,192]{2,1,0:T(8,128)(2,1)S(1)}, u32[]{:S(2)}, u32[]{:S(2)}) async-start(bf16[16,96,192]{2,1,0:T(8,128)(2,1)} %bitcast.49), calls=%async_computation | async-start | bytes 1572864 | tf_op jit(solution)/shard_map/all_to_all | solution.py:445
  148.0 2.7 %copy-start.20 = (f32[96,2,192]{2,1,0:T(2,128)S(1)}, f32[96,2,192]{2,1,0:T(2,128)}, u32[]{:S(2)}) copy-start(f32[96,2,192]{2,1,0:T(2,128)} %param.13) | copy-start | bytes 442372
  148.3 2.4 %collective-permute-start.28 = (bf16[96,192]{1,0:T(8,128)(2,1)S(1)}, bf16[96,192]{1,0:T(8,128)(2,1)S(1)}, u32[]{:S(2)}, u32[]{:S(2)}) collective-permute-start(bf16[96,192]{1,0:T(8,128)(2,1)S(1)} %bitcast.63), channel_id=1, source_target_pairs={{0,8},{8,0},{16,24},{24,16},{32,40},{40,32},{48,56},{56,48},{64,72... | collective-permute-start | bytes 110600 | tf_op jit(solution)/shard_map/ppermute | solution.py:421
  (13 other events, 11.6 us)
Sparse Core Ops, SparseCore 0:
  68.5 52.9 all-gather.1

commit v2 on v1

--- a/solution.py
+++ b/solution.py
@@ -1,3 +1,5 @@
+import functools
+
 import jax
 import jax.numpy as jnp
 from jax import lax
@@ -65,7 +67,7 @@
     return pl.BlockSpec(shape, lambda *_: (0,) * len(shape))
 
 
-def placed(kernel, place, grid, in_specs, out_shapes, operands, out_specs=None, scratch=()):
+def placed(kernel, place, grid, in_specs, out_shapes, operands, out_specs=None, scratch=(), name=None):
     return pl.pallas_call(
         kernel,
         out_shape=out_shapes,
@@ -77,7 +79,7 @@
             scratch_shapes=list(scratch),
         ),
         compiler_params=PARAMS,
-        name=kernel.__name__,
+        name=name or kernel.__name__,
     )(place, *operands)
 
 
@@ -145,30 +147,33 @@
 
 
 def cov_kernel(
-    place, cot_0, cot_1, marks_0, marks_1, rows_0, rows_1, act_0, act_1, cols_0, cols_1, up, down, rest, turned, mine
+    place, cot_0, cot_1, marks_0, marks_1, act_0, act_1, cols_0, cols_1, up, down, rest, turned, mine, cov_out, cov_in
 ):
-    places = (((rest, 0), (rest, 2), (up, 0), (down, 1)), ((rest, 1), (up, 1), (down, 0), (rest, 3)))
+    places = ((rest, 0, rest, 1), (rest, 2, up, 1), (up, 0, down, 0), (down, 1, rest, 3))
     tokens = cot_0.shape[0]
-    rows = turned.shape[0] // 4
+    rows = mine.shape[0] // 8
     mask_0, mask_1 = healthy(marks_0).astype(bf16), healthy(marks_1).astype(bf16)
-    turned[:, :tokens] = jnp.swapaxes(rows_0[...], 0, 1) * mask_0
-    turned[:, tokens:] = jnp.swapaxes(rows_1[...], 0, 1) * mask_1
-    for x in range(2):
-        mine[x * rows : (x + 1) * rows] = turned[pl.ds(pl.multiple_of((2 * x + place[2]) * rows, 16), rows), :]
-    cov_out = dot(mine[:, :tokens], cot_0[...]) + dot(mine[:, tokens:], cot_1[...])
+    turned[:, :tokens] = jnp.swapaxes(cot_0[...], 0, 1) * mask_0
+    turned[:, tokens:] = jnp.swapaxes(cot_1[...], 0, 1) * mask_1
+    for s in range(4):
+        for x in range(2):
+            base = ((place[0] + s) % 4 * 4 + 2 * x + place[2]) * rows
+            at = (2 * s + x) * rows
+            mine[at : at + rows] = turned[pl.ds(pl.multiple_of(base, 16), rows), :]
+    cov_out[...] = dot(mine[:, :tokens], cot_0[...]) + dot(mine[:, tokens:], cot_1[...])
     odd = place[3] % 2
-    own = [jnp.where(odd == 0, c[:, : 2 * rows].astype(f32), c[:, 2 * rows :].astype(f32)).astype(bf16) for c in (cols_0, cols_1)]
-    cov_in = dot(jnp.swapaxes(act_0[...], 0, 1) * mask_0, own[0])
-    cov_in += dot(jnp.swapaxes(act_1[...], 0, 1) * mask_1, own[1])
-    for x in range(2):
-        low = 2 * x * rows
-        pair = jnp.concatenate([cov_in[low : low + rows], cov_in[low + rows : low + 2 * rows]], 1)
-        value = jnp.concatenate([cov_out[x * rows : (x + 1) * rows], pair], 1).astype(bf16)
-        for s, (out, at) in enumerate(places[x]):
-
-            @pl.when(pl.program_id(0) == s)
-            def _():
-                out[at] = value
+    side = 0.0
+    for cols, mask, act in ((cols_0, mask_0, act_0), (cols_1, mask_1, act_1)):
+        own = jnp.where(odd == 0, cols[:, : 2 * rows].astype(f32), cols[:, 2 * rows :].astype(f32)).astype(bf16)
+        side += dot(jnp.swapaxes(own, 0, 1) * mask, act[...])
+    cov_in[...] = jnp.swapaxes(side, 0, 1)
+    for s in range(4):
+        for x in range(2):
+            base = ((place[0] + s) % 4 * 4 + 2 * x) * rows
+            pair = [cov_in[pl.ds(pl.multiple_of(base + k * rows, 16), rows), :] for k in range(2)]
+            at = (2 * s + x) * rows
+            out, index = places[s][2 * x : 2 * x + 2]
+            out[index] = jnp.concatenate([cov_out[at : at + rows], *pair], 1).astype(bf16)
 
 
 def squares_kernel(place, act_0, act_1, marks_0, marks_1, basis, eigen_0, eigen_1, out_in, out_out):
@@ -182,11 +187,13 @@
     out_in[...] = total
     width, tokens = eigen_0.shape
     lanes = min(128, tokens)
+    count = jnp.sum(2.0 - healthy(marks_0) - healthy(marks_1), axis=1, keepdims=True)
+    out_out[4:5, :] = jnp.broadcast_to(count, (1, width // 4))
     for at in range(0, width, width // 4):
         rows = slice(at, at + width // 4)
         square = jnp.square(eigen_0[rows].astype(f32)) + jnp.square(eigen_1[rows].astype(f32))
         square = sum(square[:, i : i + lanes] for i in range(0, tokens, lanes))
-        out_out[:, rows] = jnp.sum(jnp.swapaxes(square, 0, 1), axis=0, keepdims=True)
+        out_out[at // (width // 4) : at // (width // 4) + 1, :] = jnp.sum(jnp.swapaxes(square, 0, 1), axis=0, keepdims=True)
 
 
 def rows_kernel(place, own, got, out):
@@ -195,10 +202,14 @@
         out[(place[0] + s) % 4, 1 - place[1]] = got[s]
 
 
-def turn_kernel(keep_a, via_up, via_down, keep_b, got_b, basis, lam_out, lam_in, damp, out, grad, total):
+def turn_kernel(
+    place, keep_a, via_up, via_down, keep_b, got_b, basis, small, scale_in, scale_out, out, grad, total, lam_out, rows_all
+):
     y = pl.program_id(0)
     cut = keep_a.shape[2]
     part = keep_a.shape[1]
+    chunk = 2 * part
+    healthy_rows = rows_all - small[8:9, 0:1]
 
     @pl.when(y == 0)
     def _():
@@ -206,9 +217,13 @@
         grad[part:, :cut] = added(keep_a[1], via_down[...]).astype(bf16)
         grad[:, cut:] = added(keep_b[...], got_b[...]).astype(bf16)
         total[...] = jnp.zeros(total.shape, f32)
-
+        lam = decay_rate * scale_out[pl.ds(place[0], 1), :] + blend_weight * small[pl.ds(place[0], 1), :] / healthy_rows
+        lam = jnp.where(place[1] == 0, lam[:, :chunk], lam[:, chunk:]) * healthy_rows
+        lam_out[...] = jnp.swapaxes(jnp.broadcast_to(lam, (lam_out.shape[1], chunk)), 0, 1)
+
+    lam_in = decay_rate * scale_in[pl.ds(y, 1), :] + blend_weight * small[pl.ds(4 + y, 1), :] / healthy_rows
     rotated = dot(grad[...], basis[0])
-    scaled = (rotated / (lam_out[...] * lam_in[0] + damp[...])).astype(bf16)
+    scaled = (rotated / (lam_out[:, :1] * lam_in + damping * healthy_rows)).astype(bf16)
     total[...] += dot(basis[0], scaled, ((1,), (1,)))
 
     @pl.when(y == 3)
@@ -302,15 +317,19 @@
     cov_up, cov_down, cov_rest = placed(
         cov_kernel,
         after(place, basis_pair),
-        (4,),
+        (1,),
         [whole((tokens, width))] * 2
         + [whole((1, tokens))] * 2
-        + [own_block(wide, lambda i, p: (p[0] + i) % 4)] * 2
-        + [own_block(wide, lambda i, p: p[2] * 4 + (p[0] + i) % 4), own_block(wide, lambda i, p: (p[0] + i) % 4)]
+        + [own_block(width, lambda i, p: p[2]), whole((tokens, width))]
         + [own_block(wide, lambda i, p: p[2] * 4 + p[3] // 2), own_block(wide, lambda i, p: p[3] // 2)],
         [shape_of(n, rows, columns) for n in (2, 2, 4)],
-        (cotangents, cot_got, marks, marks_got, cotangents, cot_got, activations, act_got, activations, act_got),
-        scratch=[pltpu.VMEM((wide, 2 * tokens), bf16), pltpu.VMEM((wide // 2, 2 * tokens), bf16)],
+        (cotangents, cot_got, marks, marks_got, activations, act_got, activations, act_got),
+        scratch=[
+            pltpu.VMEM((width, 2 * tokens), bf16),
+            pltpu.VMEM((8 * rows, 2 * tokens), bf16),
+            pltpu.VMEM((8 * rows, width), f32),
+            pltpu.VMEM((width, cols), f32),
+        ],
     )
     cov_got_up, cov_got_down = send_z(cov_up, cov_down)
 
@@ -348,13 +367,17 @@
         + [whole((1, tokens))] * 2
         + [whole((width, 2 * cols))]
         + [whole((width, tokens))] * 2,
-        [shape_of(1, 2 * cols, dtype=f32), shape_of(1, width, dtype=f32)],
+        [shape_of(1, 2 * cols, dtype=f32), shape_of(5, wide, dtype=f32)],
         (activations, act_got, marks, marks_got, basis_rows, eigen, eigen_got),
     )
-    by_y = jnp.concatenate([squares_in, lax.ppermute(squares_in, "factor", swap_y(1))], 0)
-    by_y = jnp.concatenate([by_y, lax.ppermute(by_y, "factor", swap_y(2))], 0)
-    count = jnp.sum((marks + marks_got).astype(f32))
-    small = jnp.concatenate([squares_out[0], jnp.full((128,), count), by_y.reshape(width)])
+    y = fac % 4
+
+    def pair_y(own, got, first):
+        return jnp.where(first, jnp.concatenate([own, got], 0), jnp.concatenate([got, own], 0))
+
+    by_y = pair_y(squares_in, lax.ppermute(squares_in, "factor", swap_y(1)), y % 2 == 0)
+    by_y = pair_y(by_y, lax.ppermute(by_y, "factor", swap_y(2)), y < 2)
+    small = jnp.concatenate([squares_out[:4], by_y, squares_out[4:]], 0)
     give, up, down = lax.optimization_barrier((give, up, down, basis_x_lo))[:3]
     got_a = lax.ppermute(give, "dp", XLO)
     got_up, got_down = send_z(up, down)
@@ -370,18 +393,22 @@
         ),
         compiler_params=PARAMS,
         name="second_kernel",
-    )(after(keep, by_y, cov_got_up, cov_got_down), got_a, got_up, got_down, first_1, second_3)
+    )(after(keep, by_y), got_a, got_up, got_down, first_1, second_3)
     second_got_up, second_got_down = send_z(second_up, second_down)
 
     small = after(small, second_up)
     small = small + lax.ppermute(small, "dp", XLO)
-    small = small + lax.ppermute(small, "dp", swap_z(1))
-    y = fac % 4
+    small = added(small, *[lax.ppermute(small, "dp", to_z(i)) for i in (1, 3, 2)])
+    scale_own = lax.dynamic_index_in_dim(scale_in, core, 0, keepdims=False).reshape(2, 4, cols)
+    scale_own = jnp.where(fac // 4 == 0, scale_own, scale_own[::-1])
+    scale_own = jnp.concatenate([scale_own[0], scale_own[1]], 1)
+    scale_own, scale_chip = lax.optimization_barrier((scale_own, scale_out.reshape(4, wide), second_up))[:2]
+
     near = pl.BlockSpec((1, chunk, width - cut), lambda i, p: (1, 0, 0))
     third_in = (second_got_up, second_got_down, own_b, a_first_1, a_second_3, own_a)
     third_up, third_down, b_give, b_keep, a_keep = placed(
         third_kernel,
-        after(place, small),
+        after(place, small, scale_own, scale_chip),
         (1,),
         [near, near] + [whole(t.shape) for t in third_in],
         [
@@ -395,24 +422,35 @@
     )
     b_got = lax.ppermute(b_give, "dp", XLO)
     a_via_up, a_via_down = send_z(third_up, third_down)
-    small = after(small, b_give)
-    small = small + lax.ppermute(small, "dp", swap_z(3))
-
-    healthy_rows = f32(tokens * lax.axis_size("dp")) - small[width]
-    out_total = lax.dynamic_slice_in_dim(small, (z * 2 + x) * chunk, chunk, 0)
-    in_total = small[width + 128 :].reshape(2, 2, 2 * cols)
-    in_total = jnp.where(y % 2 == 0, in_total, in_total[:, ::-1])
-    in_total = jnp.where(y < 2, in_total, in_total[::-1]).reshape(4, 2 * cols)
+
+    healthy_rows = f32(tokens * lax.axis_size("dp")) - small[8, 0]
 
     cov_next = forward_z(cov_got_up, cov_got_down, cov_rest[2], cov_rest[3])
-    cov_next = lax.optimization_barrier((*cov_next, b_give))[:2]
+    cov_next = lax.optimization_barrier((*cov_next, b_got, a_via_up, a_via_down))[:2]
     cov_via_up, cov_via_down = send_z(*cov_next)
 
+    turn_in = (a_keep, a_via_up, a_via_down, b_keep, b_got)
+    (turned,) = placed(
+        functools.partial(turn_kernel, rows_all=float(tokens * lax.axis_size("dp"))),
+        place,
+        (4,),
+        [whole(t.shape) for t in turn_in]
+        + [pl.BlockSpec((1, width, 2 * cols), lambda i, p: (i, 0, 0))]
+        + [whole((9, wide)), whole((4, wide)), whole((4, wide))],
+        [shape_of(width, chunk)],
+        (*turn_in, basis_all, small, scale_own, scale_chip),
+        scratch=[
+            pltpu.VMEM((chunk, width), bf16),
+            pltpu.VMEM((width, chunk), f32),
+            pltpu.VMEM((chunk, 128), f32),
+        ],
+        name="turn_kernel",
+    )
+    cov_rest = after(cov_rest, turned)
     cov_first = added(cov_rest[0], cov_got_down[1], cov_via_up)
     cov_second = added(cov_rest[1], cov_got_up[1], cov_via_down)
     cov_give = jnp.where(x == 0, cov_second, cov_first).astype(bf16)
     cov_keep = jnp.where(x == 0, cov_first, cov_second)
-    cov_give = after(cov_give, basis_all)
     cov_sum = added(cov_keep, lax.ppermute(cov_give, "dp", XLO))
     sum_out = cov_sum[:, :width]
     sum_in = cov_sum[:, width:].reshape(rows, 2, cols)
@@ -420,28 +458,6 @@
     in_give = lax.dynamic_index_in_dim(sum_in, 1 - core, 1, keepdims=False).astype(bf16)
     in_got = lax.ppermute(in_give, "dp", CORE).astype(f32)
 
-    scale_own = lax.dynamic_index_in_dim(scale_in, core, 0, keepdims=False).reshape(2, 4, cols)
-    scale_own = jnp.where(fac // 4 == 0, scale_own, scale_own[::-1])
-    scale_own = jnp.concatenate([scale_own[0], scale_own[1]], 1)
-    lam_in = decay_rate * scale_own + blend_weight * in_total / healthy_rows
-    scale_chip = lax.dynamic_slice_in_dim(scale_out, (z * 2 + x) * chunk, chunk, 0)
-    lam_out = decay_rate * scale_chip + blend_weight * out_total / healthy_rows
-    lam_out = (lam_out * healthy_rows)[:, None]
-    damp = jnp.full((1, 2 * cols), damping * healthy_rows)
-
-    turn_in = (a_keep, a_via_up, a_via_down, b_keep, b_got)
-    turned = pl.pallas_call(
-        turn_kernel,
-        out_shape=shape_of(width, chunk),
-        grid=(4,),
-        in_specs=[whole(t.shape) for t in turn_in]
-        + [pl.BlockSpec((1, width, 2 * cols), lambda i: (i, 0, 0)), whole((chunk, 1))]
-        + [pl.BlockSpec((1, 1, 2 * cols), lambda i: (i, 0, 0)), whole((1, 2 * cols))],
-        out_specs=whole((width, chunk)),
-        scratch_shapes=[pltpu.VMEM((chunk, width), bf16), pltpu.VMEM((width, chunk), f32)],
-        compiler_params=PARAMS,
-        name="turn_kernel",
-    )(*turn_in, basis_all, lam_out, lam_in[:, None], damp)
     spread = lax.all_to_all(turned.reshape(16, rows, chunk), "dp", split_axis=0, concat_axis=0)
     result = pl.pallas_call(
         last_kernel, out_shape=shape_of(2, rows, width), compiler_params=PARAMS, name="last_kernel"

time: 176 us -> 174 us (0.989)
  waiting for transfers between devices: 20.6 us -> 24.3 us
  other arithmetic: 12.6 us -> 9.71 us
    pallas_call x1 -> x0, Pallas kernels: 7.39 us -> none  [per_device(): pl.pallas_call(turn_kernel, out_shape=shape_of(width, chunk), grid=(4,),...]
    pallas_call x5 -> x6, Pallas kernels: 35.8 us -> 42.6 us  [placed(): pl.pallas_call(kernel, out_shape=out_shapes, grid_spec=pltpu.PrefetchScal...]
    ppermute x10, waiting for transfers between devices: 3.72 us -> 7.9 us  [send_z(): return (lax.ppermute(up, 'dp', UP), lax.ppermute(down, 'dp', DOWN))]
    ppermute x3 -> x4, waiting for transfers between devices: 6.84 us -> 4.59 us  [the longest x3 4.59 us: per_device(): lax.ppermute(small, 'dp', to_z(i))]
    slice x2 -> x3, local copies, waits for them, and re-layouts: 0.52 us -> 2.61 us  [the longest x2 1.42 us: per_device(): small = jnp.concatenate([squares_out[:4], by_y, squares_out[4:]], 0)]
    broadcast_in_dim x3 -> x0, local copies, waits for them, and re-layouts: 2.04 us -> none  [the longest x1 0.77 us: per_device(): lam_out = (lam_out * healthy_rows)[:, None]]
    ppermute x1, waiting for transfers between devices: 0.01 us -> 1.89 us  [per_device(): small = small + lax.ppermute(small, 'dp', XLO)]
    unnamed x66 -> x50, local copies, waits for them, and re-layouts: 9.8 us -> 9.31 us
  transfers between devices with their start and end apart: 31 -> 32, of which waited for: 6 -> 11; matrix products, arithmetic and copies ran while one was open for 10% -> 7% of each run, Pallas kernels for 31% -> 31%
where the time goes in v2:
time: 174 us
  Pallas kernels  62.1 us (36%)
  starting transfers between devices  46.6 us (27%)
  waiting for transfers between devices  24.3 us (14%)
  local copies, waits for them, and re-layouts  16 us (9%)
  between operations  15 us (9%)
  other arithmetic  9.71 us (6%)
    pallas_call x6, Pallas kernels, placed(): pl.pallas_call(kernel, out_shape=out_shapes, grid_spec=pltpu.PrefetchScal...  42.6 us
    ppermute x10, starting transfers between devices, send_z(): return (lax.ppermute(up, 'dp', UP), lax.ppermute(down, 'dp', DOWN))  12.2 us
    pallas_call x2, Pallas kernels, rotate(): pl.pallas_call(rotate_kernel, out_shape=shape_of(width, tokens), grid_spe...  10.8 us
    all_to_all x1, starting transfers between devices, per_device(): lax.all_to_all(turned.reshape(16, rows, chunk), 'dp', split_axis=0, conca...  10.8 us
    unnamed x50, local copies, waits for them, and re-layouts  9.31 us
    ppermute x10, waiting for transfers between devices, send_z(): return (lax.ppermute(up, 'dp', UP), lax.ppermute(down, 'dp', DOWN))  7.9 us
    all_to_all x1, waiting for transfers between devices, per_device(): lax.all_to_all(turned.reshape(16, rows, chunk), 'dp', split_axis=0, conca...  6.67 us
    pallas_call x1, Pallas kernels, per_device(): pl.pallas_call(last_kernel, out_shape=shape_of(2, rows, width), compiler_...  5.19 us
  transfers between devices with their start and end apart: 32, of which 11 were waited for; matrix products, arithmetic and copies ran while one was open for 7% of the time, Pallas kernels for 31%

profile of v2, /device:TPU:1, one launch (start us, length us, event | category | flops | bytes accessed | tf_op | source)
XLA Modules:
  0.0 173.7 jit_solution(13120210239178691442)
XLA Ops:
  7.3 2.8 %constant_dynamic-slice_fusion.4 = bf16[512,1536]{1,0:T(8,128)(2,1)} fusion(bf16[512,3072]{1,0:T(8,128)(2,1)} %act_0.5, s32[]{:T(128)S(6)} %select_n.100), kind=kLoop, calls=%fused_computation.37 | loop fusion | bytes 3145732 | tf_op jit(solution)/shard_map/dynamic_slice | solution.py:277
  10.0 1.4 collective-permute-start
  12.9 5.5 %rotate_kernel.2.refs_0_ = bf16[1536,512]{1,0:T(8,128)(2,1)} custom-call(s32[4]{0:T(128)} %pad_add_fusion.place, bf16[512,1536]{1,0:T(8,128)(2,1)} %cot_0.1, s32[1,512]{1,0:T(1,128)} %bitcast.56, bf16[1536,1536]{1,0:T(8,128)(2,1)} %basis_out.1), custom_call_target="tpu_custom_call" | custom-call | tf_op jit(solution)/shard_map/rotate_kernel/pallas_call | solution.py:281
  18.4 2.9 %collective-permute-start.3 = (bf16[192,192]{1,0:T(8,128)(2,1)S(1)}, bf16[192,192]{1,0:T(8,128)(2,1)S(1)}, u32[]{:S(2)}, u32[]{:S(2)}) collective-permute-start(bf16[192,192]{1,0:T(8,128)(2,1)S(1)} %maximum_select_fusion.1), channel_id=1, source_target_pairs={{0,4},{1,5},{2,6},{3,7},{4,0},{5,1},{6,2},{7,3},{8,12},{9,13},{10,... | collective-permute-start | bytes 221192 | tf_op jit(solution)/shard_map/ppermute | solution.py:307
  22.5 5.3 %rotate_kernel.3.eigen_0 = bf16[1536,512]{1,0:T(8,128)(2,1)} custom-call(s32[4]{0:T(128)} %pad_add_fusion.place, bf16[512,1536]{1,0:T(8,128)(2,1)} %cot_0.1, s32[1,512]{1,0:T(1,128)} %bitcast.57, bf16[1536,1536]{1,0:T(8,128)(2,1)} %basis_out.1, bf16[1536,512]{1,0:T(8,128)(2,1)} %rotate_kernel.2.refs_0_), custom_call_target="tpu_custom_call", output_to_operand_aliasing={{}: (4, {})} | custom-call | tf_op jit(solution)/shard_map/rotate_kernel/pallas_call | solution.py:281
  28.4 1.7 collective-permute-start.7
  30.1 2.2 %collective-permute-start.5 = (bf16[192,384]{1,0:T(8,128)(2,1)S(1)}, bf16[192,384]{1,0:T(8,128)(2,1)S(1)}, u32[]{:S(2)}, u32[]{:S(2)}) collective-permute-start(bf16[192,384]{1,0:T(8,128)(2,1)S(1)} %pad_maximum_fusion.1), channel_id=1, source_target_pairs={{0,96},{8,104},{16,112},{24,120},{32,0},{40,8},{48,16},{56,24},{64... | collective-permute-start | bytes 442376 | tf_op jit(solution)/shard_map/ppermute | solution.py:311
  32.3 1.2 collective-permute-start.6
  33.5 9.8 %cov_kernel.1 = (bf16[2,96,1920]{2,1,0:T(8,128)(2,1)}, bf16[2,96,1920]{2,1,0:T(8,128)(2,1)}, bf16[4,96,1920]{2,1,0:T(8,128)(2,1)}) custom-call(s32[4]{0:T(128)} %pad_add_fusion.place, bf16[512,1536]{1,0:T(8,128)(2,1)} %cot_0.1, bf16[512,1536]{1,0:T(8,128)(2,1)} %collective-permute-done.4.cot_1, s32[1,512]{1,0:T(1,128)} %bitcast.58, s32[1,512]{1,0:T(1,128)} %copy-done.21, ...), custom_call_target="tpu_custom_call" | custom-call | tf_op jit(solution)/shard_map/cov_kernel/pallas_call | solution.py:71
  43.3 1.3 collective-permute-start.10
  45.5 1.2 copy-done.3
  46.7 10.9 %grad_kernel.1 = (bf16[4,192,512]{2,1,0:T(8,128)(2,1)}, bf16[4,192,512]{2,1,0:T(8,128)(2,1)}, bf16[2,192,1024]{2,1,0:T(8,128)(2,1)}, bf16[2,192,1024]{2,1,0:T(8,...) custom-call(s32[4]{0:T(128)} %pad_add_fusion.place, ...), custom_call_target="tpu_custom_call" | custom-call | tf_op jit(solution)/shard_map/grad_kernel/pallas_call | solution.py:71
  57.6 2.9 %collective-permute-done.10 = bf16[2,96,1920]{2,1,0:T(8,128)(2,1)S(1)} collective-permute-done((bf16[2,96,1920]{2,1,0:T(8,128)(2,1)}, bf16[2,96,1920]{2,1,0:T(8,128)(2,1)S(1)}, u32[]{:S(2)}, u32[]{:S(2)}) %collective-permute-start.10) | collective-permute-done | bytes 737312 | tf_op jit(solution)/shard_map/ppermute | solution.py:55
  60.5 2.6 %collective-permute-done.9 = bf16[2,96,1920]{2,1,0:T(8,128)(2,1)S(1)} collective-permute-done((bf16[2,96,1920]{2,1,0:T(8,128)(2,1)}, bf16[2,96,1920]{2,1,0:T(8,128)(2,1)S(1)}, u32[]{:S(2)}, u32[]{:S(2)}) %collective-permute-start.9) | collective-permute-done | bytes 737312 | tf_op jit(solution)/shard_map/ppermute | solution.py:55
  63.9 3.1 %rows_kernel.1 = bf16[4,2,192,384]{3,2,1,0:T(8,128)(2,1)} custom-call(s32[4]{0:T(128)} %pad_add_fusion.place, bf16[4,192,384]{2,1,0:T(8,128)(2,1)} %copy-done.8, bf16[4,192,384]{2,1,0:T(8,128)(2,1)} %copy-done.11), custom_call_target="tpu_custom_call" | custom-call | tf_op jit(solution)/shard_map/rows_kernel/pallas_call | solution.py:71
  67.4 2.7 %collective-permute-start.16 = (bf16[2,192,1024]{2,1,0:T(8,128)(2,1)}, bf16[2,192,1024]{2,1,0:T(8,128)(2,1)S(1)}, u32[]{:S(2)}, u32[]{:S(2)}) collective-permute-start(bf16[2,192,1024]{2,1,0:T(8,128)(2,1)} %get-tuple-element.66), channel_id=1, source_target_pairs={{0,96},{8,104},{16,112},{24,120},{32,0},{40,8},{48,16},{56,24},{64... | collective-permute-start | bytes 2359304 | tf_op jit(solution)/shard_map/ppermute | solution.py:55
  70.0 6.5 %squares_kernel.1 = (f32[1,384]{1,0:T(1,128)}, f32[5,384]{1,0:T(8,128)}) custom-call(s32[4]{0:T(128)} %pad_add_fusion.place, bf16[512,3072]{1,0:T(8,128)(2,1)} %act_0.5, bf16[512,1536]{1,0:T(8,128)(2,1)} %copy-done.1, s32[1,512]{1,0:T(1,128)} %bitcast.59, s32[1,512]{1,0:T(1,128)} %copy-done.21, bf16[1536,384]{1,0:T(8,128)(2,1)} %bitcast.47, ...), custom_call_target="tpu_custom_call" | custom-call | tf_op jit(solution)/shard_map/squares_kernel/pallas_call | solution.py:71
  76.6 1.3 collective-permute-start.12
  78.0 1.6 collective-permute-done.12
  80.4 3.0 %collective-permute-start.13 = (f32[2,384]{1,0:T(2,128)S(1)}, f32[2,384]{1,0:T(2,128)S(1)}, u32[]{:S(2)}, u32[]{:S(2)}) collective-permute-start(f32[2,384]{1,0:T(2,128)S(1)} %maximum_select_fusion.3), channel_id=1, source_target_pairs={{0,2},{1,3},{2,0},{3,1},{4,6},{5,7},{6,4},{7,5},{8,10},{9,11},{10,... | collective-permute-start | bytes 9224 | tf_op jit(solution)/shard_map/ppermute | solution.py:379
  85.7 0.9 copy-done.6
  86.9 3.4 %second_kernel.1 = (bf16[192,1536]{1,0:T(8,128)(2,1)}, bf16[192,1536]{1,0:T(8,128)(2,1)}, bf16[96,512]{1,0:T(8,128)(2,1)}, bf16[96,512]{1,0:T(8,128)(2,1)}, bf16[2,96,512]{2,1,0:T(8,128)(2,1)}) custom-call(bf16[4,192,512]{2,1,0:T(8,128)(2,1)} %get-tuple-element.60.keep, bf16[4,192,512]{2,1,0:T(8,128)(2,1)} %collective-permute-done.14.got_a, ...), custom_call_target="tpu_custom_call" | custom-call | tf_op jit(solution)/shard_map/second_kernel/pallas_call | solution.py:385
  90.3 2.7 %collective-permute-start.22 = (bf16[192,1536]{1,0:T(8,128)(2,1)}, bf16[192,1536]{1,0:T(8,128)(2,1)S(1)}, u32[]{:S(2)}, u32[]{:S(2)}) collective-permute-start(bf16[192,1536]{1,0:T(8,128)(2,1)} %get-tuple-element.74), channel_id=1, source_target_pairs={{0,96},{8,104},{16,112},{24,120},{32,0},{40,8},{48,16},{56,24},{64... | collective-permute-start | bytes 1769480 | tf_op jit(solution)/shard_map/ppermute | solution.py:55
  93.0 1.3 collective-permute-start.17
  94.2 1.9 %collective-permute-done.17 = f32[9,384]{1,0:T(8,128)S(1)} collective-permute-done((f32[9,384]{1,0:T(8,128)S(1)}, f32[9,384]{1,0:T(8,128)S(1)}, u32[]{:S(2)}, u32[]{:S(2)}) %collective-permute-start.17) | collective-permute-done | bytes 13856 | tf_op jit(solution)/shard_map/ppermute | solution.py:400
  96.1 2.7 %collective-permute-start.19 = (f32[9,384]{1,0:T(8,128)S(1)}, f32[9,384]{1,0:T(8,128)S(1)}, u32[]{:S(2)}, u32[]{:S(2)}) collective-permute-start(f32[9,384]{1,0:T(8,128)S(1)} %add.86), channel_id=1, source_target_pairs={{0,96},{8,104},{16,112},{24,120},{32,0},{40,8},{48,16},{56,24},{64... | collective-permute-start | bytes 41480 | tf_op jit(solution)/shard_map/ppermute | solution.py:401
  100.1 2.8 %collective-permute-done.18 = f32[9,384]{1,0:T(8,128)S(1)} collective-permute-done((f32[9,384]{1,0:T(8,128)S(1)}, f32[9,384]{1,0:T(8,128)S(1)}, u32[]{:S(2)}, u32[]{:S(2)}) %collective-permute-start.18) | collective-permute-done | bytes 13856 | tf_op jit(solution)/shard_map/ppermute | solution.py:401
  102.9 1.8 %collective-permute-done.20 = f32[9,384]{1,0:T(8,128)S(1)} collective-permute-done((f32[9,384]{1,0:T(8,128)S(1)}, f32[9,384]{1,0:T(8,128)S(1)}, u32[]{:S(2)}, u32[]{:S(2)}) %collective-permute-start.20) | collective-permute-done | bytes 13856 | tf_op jit(solution)/shard_map/ppermute | solution.py:401
  106.3 4.2 %third_kernel.1 = (bf16[96,512]{1,0:T(8,128)(2,1)}, bf16[96,512]{1,0:T(8,128)(2,1)}, bf16[192,1024]{1,0:T(8,128)(2,1)}, f32[192,1024]{1,0:T(8,128)}, f32[2,96,512]{2,1,0:T(8,128)}) custom-call(s32[4]{0:T(128)} %pad_add_fusion.place, bf16[2,192,1024]{2,1,0:T(8,128)(2,1)} %copy-done.6, bf16[2,192,1024]{2,1,0:T(8,128)(2,1)} %copy-done.7, ...), custom_call_target="tpu_custom_call" | custom-call | tf_op jit(solution)/shard_map/third_kernel/pallas_call | solution.py:71
  110.5 1.2 collective-permute-start.25
  111.7 1.0 collective-permute-start.23
  112.6 1.7 collective-permute-start.24
  114.4 1.1 fusion.3
  115.4 1.6 collective-permute-done.23.via_up
  118.5 1.0 collective-permute-start.26
  119.4 1.7 collective-permute-start.27
  121.2 8.2 %turn_kernel.1 = bf16[1536,192]{1,0:T(8,128)(2,1)} custom-call(s32[4]{0:T(128)} %pad_add_fusion.place, f32[2,96,512]{2,1,0:T(8,128)} %get-tuple-element.78.keep_a, bf16[96,512]{1,0:T(8,128)(2,1)} %copy-done.17, bf16[96,512]{1,0:T(8,128)(2,1)} %copy-done.18, f32[192,1024]{1,0:T(8,128)} %get-tuple-element.81.keep_b, bf16[192,1024]{1,0:T(8,128)(2,1)} %copy-done.14, ...), custom_call_target="tpu_custom_call" | custom-call | tf_op jit(solution)/shard_map/turn_kernel/pallas_call | solution.py:71
  129.4 2.0 %select_convert_fusion = bf16[96,1920]{1,0:T(8,128)(2,1)} fusion(bf16[96,1920]{1,0:T(8,128)(2,1)S(1)} %collective-permute-done.26, bf16[96,1920]{1,0:T(8,128)(2,1)} %collective-permute-done.27, pred[]{:T(512)S(6)} %eq.22, bf16[2,96,1920]{2,1,0:T(8,128)(2,1)S(1)} %collective-permute-done.9, bf16[2,96,1920]{2,1,0:T(8,128)(2,1)S(1)} %collective-permute-done.10, ...), kind=kLoop, calls=%fused_computation.3 | loop fusion | flops 2211840 | bytes 2580481 | tf_op jit(solution)/shard_map/convert_element_type | solution.py:452
  131.4 1.2 collective-permute-start.28
  132.6 1.2 slice.67
  134.5 10.8 %all-to-all-start = ((bf16[16,96,192]{2,1,0:T(8,128)(2,1)}), bf16[16,96,192]{2,1,0:T(8,128)(2,1)S(1)}, u32[]{:S(2)}, u32[]{:S(2)}) async-start(bf16[16,96,192]{2,1,0:T(8,128)(2,1)} %bitcast.15), calls=%async_computation | async-start | bytes 1572864 | tf_op jit(solution)/shard_map/all_to_all | solution.py:461
  145.2 1.7 convert_add_fusion
  147.2 1.3 collective-permute-start.29
  148.5 2.0 %fusion.1 = f32[96,1536]{1,0:T(8,128)} fusion(f32[96,1920]{1,0:T(8,128)S(1)} %convert_add_fusion, f32[96,1536]{1,0:T(8,128)} %param.14, f32[]{:T(128)} %bitcast.24), kind=kLoop, calls=%fused_computation.8 | loop fusion | flops 589824 | bytes 1769476 | tf_op jit(solution)/shard_map/add | solution.py:468
  151.5 6.7 %all-to-all-done.spread = bf16[16,96,192]{2,1,0:T(8,128)(2,1)S(1)} async-done(((bf16[16,96,192]{2,1,0:T(8,128)(2,1)}), bf16[16,96,192]{2,1,0:T(8,128)(2,1)S(1)}, u32[]{:S(2)}, u32[]{:S(2)}) %all-to-all-start) | async-done | bytes 589856 | tf_op jit(solution)/shard_map/all_to_all | solution.py:461
  158.2 0.9 copy-done.5
  159.1 5.2 %last_kernel.1 = bf16[2,96,1536]{2,1,0:T(8,128)(2,1)} custom-call(bf16[16,96,192]{2,1,0:T(8,128)(2,1)} %copy-done.5, bf16[1536,1536]{1,0:T(8,128)(2,1)} %basis_out.1), custom_call_target="tpu_custom_call" | custom-call | tf_op jit(solution)/shard_map/last_kernel/pallas_call | solution.py:462
  164.3 2.5 %copy.27 = bf16[96,2,1536]{2,1,0:T(2,128)(2,1)} copy(bf16[96,2,1536]{2,0,1:T(8,128)(2,1)} %bitcast.48) | data formatting | bytes 1179648
  (107 shorter events, 14.4 us)
Async XLA Ops:
  7.2 70.7 %copy-start = (f32[2,1536]{1,0:T(2,128)S(1)}, f32[2,1536]{1,0:T(2,128)}, u32[]{:S(2)}) copy-start(f32[2,1536]{1,0:T(2,128)} %param.15) | copy-start | bytes 36868
  7.2 114.0 %all-gather.2.cloned.1.call-start = ((), (), s32[]{:S(2)}) async-start(), calls=%async_computation.1 | async-start | bytes 5898240 | tf_op jit(solution)/shard_map/all_gather | solution.py:361
  7.2 4.2 %copy-start.2 = (bf16[512,1536]{1,0:T(8,128)(2,1)S(1)}, bf16[512,1536]{1,0:T(8,128)(2,1)}, u32[]{:S(2)}) copy-start(bf16[512,1536]{1,0:T(8,128)(2,1)} %cot_0.1) | copy-start | bytes 4718596
  7.3 4.2 %copy-start.15 = (bf16[96,2,192]{2,1,0:T(2,128)(2,1)S(1)}, bf16[96,2,192]{2,1,0:T(2,128)(2,1)}, u32[]{:S(2)}) copy-start(bf16[96,2,192]{2,1,0:T(2,128)(2,1)} %param.11) | copy-start | bytes 221188
  10.0 22.3 %collective-permute-start = (bf16[512,1536]{1,0:T(8,128)(2,1)}, bf16[512,1536]{1,0:T(8,128)(2,1)S(1)}, u32[]{:S(2)}, u32[]{:S(2)}) collective-permute-start(bf16[512,1536]{1,0:T(8,128)(2,1)} %constant_dynamic-slice_fusion.4), channel_id=1, source_target_pairs={{0,8},{8,0},{16,24},{24,16},{32,40},{40,32},{48,56},{56,48},{64,72... | collective-permute-start | bytes 4718600 | tf_op jit(solution)/shard_map/ppermute | solution.py:278
  11.5 22.1 %collective-permute-start.4 = (bf16[512,1536]{1,0:T(8,128)(2,1)S(1)}, bf16[512,1536]{1,0:T(8,128)(2,1)}, u32[]{:S(2)}, u32[]{:S(2)}) collective-permute-start(bf16[512,1536]{1,0:T(8,128)(2,1)S(1)} %copy-done.2), channel_id=1, source_target_pairs={{0,8},{8,0},{16,24},{24,16},{32,40},{40,32},{48,56},{56,48},{64,72... | collective-permute-start | bytes 4718600 | tf_op jit(solution)/shard_map/ppermute | solution.py:276
  11.7 6.7 %collective-permute-start.2 = (bf16[96,192]{1,0:T(8,128)(2,1)S(1)}, bf16[96,192]{1,0:T(8,128)(2,1)S(1)}, u32[]{:S(2)}, u32[]{:S(2)}) collective-permute-start(bf16[96,192]{1,0:T(8,128)(2,1)S(1)} %bitcast.54), channel_id=1, source_target_pairs={{0,8},{8,0},{16,24},{24,16},{32,40},{40,32},{48,56},{56,48},{64,72... | collective-permute-start | bytes 110600 | tf_op jit(solution)/shard_map/ppermute | solution.py:273
  12.9 8.4 %copy-start.19 = (s32[512]{0:T(512)S(1)}, s32[512]{0:T(512)}, u32[]{:S(2)}) copy-start(s32[512]{0:T(512)} %param.17) | copy-start | bytes 6148
  18.4 9.4 %collective-permute-start.3 = (bf16[192,192]{1,0:T(8,128)(2,1)S(1)}, bf16[192,192]{1,0:T(8,128)(2,1)S(1)}, u32[]{:S(2)}, u32[]{:S(2)}) collective-permute-start(bf16[192,192]{1,0:T(8,128)(2,1)S(1)} %maximum_select_fusion.1), channel_id=1, source_target_pairs={{0,4},{1,5},{2,6},{3,7},{4,0},{5,1},{6,2},{7,3},{8,12},{9,13},{10,... | collective-permute-start | bytes 221192 | tf_op jit(solution)/shard_map/ppermute | solution.py:307
  21.3 1.2 collective-permute-start.1
  22.5 5.4 %copy-start.21 = (s32[1,512]{1,0:T(1,128)}, s32[1,512]{1,0:T(1,128)S(1)}, u32[]{:S(2)}) copy-start(s32[1,512]{1,0:T(1,128)S(1)} %collective-permute-done.1.marks_1) | copy-start | bytes 6148
  27.9 17.6 %collective-permute-start.8 = (bf16[1536,512]{1,0:T(8,128)(2,1)}, bf16[1536,512]{1,0:T(8,128)(2,1)S(1)}, u32[]{:S(2)}, u32[]{:S(2)}) collective-permute-start(bf16[1536,512]{1,0:T(8,128)(2,1)} %rotate_kernel.3.eigen_0), channel_id=1, source_target_pairs={{0,8},{8,0},{16,24},{24,16},{32,40},{40,32},{48,56},{56,48},{64,72... | collective-permute-start | bytes 4718600 | tf_op jit(solution)/shard_map/ppermute | solution.py:309
  28.4 16.3 %collective-permute-start.7 = (bf16[192,384]{1,0:T(8,128)(2,1)S(1)}, bf16[192,384]{1,0:T(8,128)(2,1)S(1)}, u32[]{:S(2)}, u32[]{:S(2)}) collective-permute-start(bf16[192,384]{1,0:T(8,128)(2,1)S(1)} %pad_maximum_fusion.1), channel_id=1, source_target_pairs={{0,32},{8,40},{16,48},{24,56},{32,64},{40,72},{48,80},{56,88},{64,... | collective-permute-start | bytes 442376 | tf_op jit(solution)/shard_map/ppermute | solution.py:311
  30.1 14.7 %collective-permute-start.5 = (bf16[192,384]{1,0:T(8,128)(2,1)S(1)}, bf16[192,384]{1,0:T(8,128)(2,1)S(1)}, u32[]{:S(2)}, u32[]{:S(2)}) collective-permute-start(bf16[192,384]{1,0:T(8,128)(2,1)S(1)} %pad_maximum_fusion.1), channel_id=1, source_target_pairs={{0,96},{8,104},{16,112},{24,120},{32,0},{40,8},{48,16},{56,24},{64... | collective-permute-start | bytes 442376 | tf_op jit(solution)/shard_map/ppermute | solution.py:311
  32.3 1.2 copy-start.1
  32.3 12.5 %collective-permute-start.6 = (bf16[192,384]{1,0:T(8,128)(2,1)S(1)}, bf16[192,384]{1,0:T(8,128)(2,1)S(1)}, u32[]{:S(2)}, u32[]{:S(2)}) collective-permute-start(bf16[192,384]{1,0:T(8,128)(2,1)S(1)} %pad_maximum_fusion.1), channel_id=1, source_target_pairs={{0,64},{8,72},{16,80},{24,88},{32,96},{40,104},{48,112},{56,120},{... | collective-permute-start | bytes 442376 | tf_op jit(solution)/shard_map/ppermute | solution.py:311
  43.3 17.2 %collective-permute-start.10 = (bf16[2,96,1920]{2,1,0:T(8,128)(2,1)}, bf16[2,96,1920]{2,1,0:T(8,128)(2,1)S(1)}, u32[]{:S(2)}, u32[]{:S(2)}) collective-permute-start(bf16[2,96,1920]{2,1,0:T(8,128)(2,1)} %get-tuple-element.55), channel_id=1, source_target_pairs={{0,96},{8,104},{16,112},{24,120},{32,0},{40,8},{48,16},{56,24},{64... | collective-permute-start | bytes 2211848 | tf_op jit(solution)/shard_map/ppermute | solution.py:55
  44.6 18.4 %collective-permute-start.9 = (bf16[2,96,1920]{2,1,0:T(8,128)(2,1)}, bf16[2,96,1920]{2,1,0:T(8,128)(2,1)S(1)}, u32[]{:S(2)}, u32[]{:S(2)}) collective-permute-start(bf16[2,96,1920]{2,1,0:T(8,128)(2,1)} %get-tuple-element.50), channel_id=1, source_target_pairs={{0,32},{8,40},{16,48},{24,56},{32,64},{40,72},{48,80},{56,88},{64,... | collective-permute-start | bytes 2211848 | tf_op jit(solution)/shard_map/ppermute | solution.py:55
  44.9 18.2 %copy-start.8 = (bf16[4,192,384]{2,1,0:T(8,128)(2,1)}, bf16[4,192,384]{2,1,0:T(8,128)(2,1)S(1)}, u32[]{:S(2)}) copy-start(bf16[4,192,384]{2,1,0:T(8,128)(2,1)S(1)} %pad_maximum_fusion.own) | copy-start | bytes 1769476
  44.9 18.1 %collective-permute-start.11 = (bf16[4,192,384]{2,1,0:T(8,128)(2,1)S(1)}, bf16[4,192,384]{2,1,0:T(8,128)(2,1)S(1)}, u32[]{:S(2)}, u32[]{:S(2)}) collective-permute-start(bf16[4,192,384]{2,1,0:T(8,128)(2,1)S(1)} %pad_maximum_fusion.own), channel_id=1, source_target_pairs={{0,16},{8,24},{16,0},{24,8},{32,48},{40,56},{48,32},{56,40},{64,80... | collective-permute-start | bytes 1769480 | tf_op jit(solution)/shard_map/ppermute | solution.py:337
  45.5 1.2 copy-start.3
  60.5 68.9 %copy-start.9 = (bf16[2,96,1920]{2,1,0:T(8,128)(2,1)}, bf16[2,96,1920]{2,1,0:T(8,128)(2,1)S(1)}, u32[]{:S(2)}) copy-start(bf16[2,96,1920]{2,1,0:T(8,128)(2,1)S(1)} %collective-permute-done.10) | copy-start | bytes 2211844
  63.0 66.4 %copy-start.10 = (bf16[2,96,1920]{2,1,0:T(8,128)(2,1)}, bf16[2,96,1920]{2,1,0:T(8,128)(2,1)S(1)}, u32[]{:S(2)}) copy-start(bf16[2,96,1920]{2,1,0:T(8,128)(2,1)S(1)} %collective-permute-done.9) | copy-start | bytes 2211844
  67.0 17.8 %collective-permute-start.14 = (bf16[4,192,512]{2,1,0:T(8,128)(2,1)}, bf16[4,192,512]{2,1,0:T(8,128)(2,1)}, u32[]{:S(2)}, u32[]{:S(2)}) collective-permute-start(bf16[4,192,512]{2,1,0:T(8,128)(2,1)} %get-tuple-element.64), channel_id=1, source_target_pairs={{0,16},{8,24},{16,0},{24,8},{32,48},{40,56},{48,32},{56,40},{64,80... | collective-permute-start | bytes 2359304 | tf_op jit(solution)/shard_map/ppermute | solution.py:382
  67.4 18.3 %collective-permute-start.15 = (bf16[2,192,1024]{2,1,0:T(8,128)(2,1)}, bf16[2,192,1024]{2,1,0:T(8,128)(2,1)S(1)}, u32[]{:S(2)}, u32[]{:S(2)}) collective-permute-start(bf16[2,192,1024]{2,1,0:T(8,128)(2,1)} %get-tuple-element.65), channel_id=1, source_target_pairs={{0,32},{8,40},{16,48},{24,56},{32,64},{40,72},{48,80},{56,88},{64,... | collective-permute-start | bytes 2359304 | tf_op jit(solution)/shard_map/ppermute | solution.py:55
  67.4 18.3 %collective-permute-start.16 = (bf16[2,192,1024]{2,1,0:T(8,128)(2,1)}, bf16[2,192,1024]{2,1,0:T(8,128)(2,1)S(1)}, u32[]{:S(2)}, u32[]{:S(2)}) collective-permute-start(bf16[2,192,1024]{2,1,0:T(8,128)(2,1)} %get-tuple-element.66), channel_id=1, source_target_pairs={{0,96},{8,104},{16,112},{24,120},{32,0},{40,8},{48,16},{56,24},{64... | collective-permute-start | bytes 2359304 | tf_op jit(solution)/shard_map/ppermute | solution.py:55
  76.6 3.0 %collective-permute-start.12 = (f32[1,384]{1,0:T(1,128)}, f32[1,384]{1,0:T(1,128)S(1)}, u32[]{:S(2)}, u32[]{:S(2)}) collective-permute-start(f32[1,384]{1,0:T(1,128)} %get-tuple-element.58), channel_id=1, source_target_pairs={{0,1},{1,0},{2,3},{3,2},{4,5},{5,4},{6,7},{7,6},{8,9},{9,8},{10,11... | collective-permute-start | bytes 4616 | tf_op jit(solution)/shard_map/ppermute | solution.py:378
  80.4 4.4 %collective-permute-start.13 = (f32[2,384]{1,0:T(2,128)S(1)}, f32[2,384]{1,0:T(2,128)S(1)}, u32[]{:S(2)}, u32[]{:S(2)}) collective-permute-start(f32[2,384]{1,0:T(2,128)S(1)} %maximum_select_fusion.3), channel_id=1, source_target_pairs={{0,2},{1,3},{2,0},{3,1},{4,6},{5,7},{6,4},{7,5},{8,10},{9,11},{10,... | collective-permute-start | bytes 9224 | tf_op jit(solution)/shard_map/ppermute | solution.py:379
  85.7 1.1 copy-start.7
  86.9 12.6 %copy-start.20 = (f32[1536]{0:T(1024)S(1)}, f32[1536]{0:T(1024)}, u32[]{:S(2)}) copy-start(f32[1536]{0:T(1024)} %param.16) | copy-start | bytes 18436
  90.3 15.0 %collective-permute-start.21 = (bf16[192,1536]{1,0:T(8,128)(2,1)}, bf16[192,1536]{1,0:T(8,128)(2,1)S(1)}, u32[]{:S(2)}, u32[]{:S(2)}) collective-permute-start(bf16[192,1536]{1,0:T(8,128)(2,1)} %get-tuple-element.69), channel_id=1, source_target_pairs={{0,32},{8,40},{16,48},{24,56},{32,64},{40,72},{48,80},{56,88},{64,... | collective-permute-start | bytes 1769480 | tf_op jit(solution)/shard_map/ppermute | solution.py:55
  90.3 15.0 %collective-permute-start.22 = (bf16[192,1536]{1,0:T(8,128)(2,1)}, bf16[192,1536]{1,0:T(8,128)(2,1)S(1)}, u32[]{:S(2)}, u32[]{:S(2)}) collective-permute-start(bf16[192,1536]{1,0:T(8,128)(2,1)} %get-tuple-element.74), channel_id=1, source_target_pairs={{0,96},{8,104},{16,112},{24,120},{32,0},{40,8},{48,16},{56,24},{64... | collective-permute-start | bytes 1769480 | tf_op jit(solution)/shard_map/ppermute | solution.py:55
  93.0 3.2 %collective-permute-start.17 = (f32[9,384]{1,0:T(8,128)S(1)}, f32[9,384]{1,0:T(8,128)S(1)}, u32[]{:S(2)}, u32[]{:S(2)}) collective-permute-start(f32[9,384]{1,0:T(8,128)S(1)} %pad_maximum_fusion.2), channel_id=1, source_target_pairs={{0,16},{8,24},{16,0},{24,8},{32,48},{40,56},{48,32},{56,40},{64,80... | collective-permute-start | bytes 41480 | tf_op jit(solution)/shard_map/ppermute | solution.py:400
  96.1 6.8 %collective-permute-start.18 = (f32[9,384]{1,0:T(8,128)S(1)}, f32[9,384]{1,0:T(8,128)S(1)}, u32[]{:S(2)}, u32[]{:S(2)}) collective-permute-start(f32[9,384]{1,0:T(8,128)S(1)} %add.86), channel_id=1, source_target_pairs={{0,32},{8,40},{16,48},{24,56},{32,64},{40,72},{48,80},{56,88},{64,... | collective-permute-start | bytes 41480 | tf_op jit(solution)/shard_map/ppermute | solution.py:401
  96.1 6.8 %collective-permute-start.19 = (f32[9,384]{1,0:T(8,128)S(1)}, f32[9,384]{1,0:T(8,128)S(1)}, u32[]{:S(2)}, u32[]{:S(2)}) collective-permute-start(f32[9,384]{1,0:T(8,128)S(1)} %add.86), channel_id=1, source_target_pairs={{0,96},{8,104},{16,112},{24,120},{32,0},{40,8},{48,16},{56,24},{64... | collective-permute-start | bytes 41480 | tf_op jit(solution)/shard_map/ppermute | solution.py:401
  98.8 5.9 %collective-permute-start.20 = (f32[9,384]{1,0:T(8,128)S(1)}, f32[9,384]{1,0:T(8,128)S(1)}, u32[]{:S(2)}, u32[]{:S(2)}) collective-permute-start(f32[9,384]{1,0:T(8,128)S(1)} %add.86), channel_id=1, source_target_pairs={{0,64},{8,72},{16,80},{24,88},{32,96},{40,104},{48,112},{56,120},{... | collective-permute-start | bytes 41480 | tf_op jit(solution)/shard_map/ppermute | solution.py:401
  106.3 8.1 %copy-start.4 = (bf16[4,96,1920]{2,1,0:T(8,128)(2,1)S(1)}, bf16[4,96,1920]{2,1,0:T(8,128)(2,1)}, u32[]{:S(2)}) copy-start(bf16[4,96,1920]{2,1,0:T(8,128)(2,1)} %get-tuple-element.84) | copy-start | bytes 4423684
  110.5 7.2 %collective-permute-start.25 = (bf16[192,1024]{1,0:T(8,128)(2,1)}, bf16[192,1024]{1,0:T(8,128)(2,1)S(1)}, u32[]{:S(2)}, u32[]{:S(2)}) collective-permute-start(bf16[192,1024]{1,0:T(8,128)(2,1)} %get-tuple-element.82), channel_id=1, source_target_pairs={{0,16},{8,24},{16,0},{24,8},{32,48},{40,56},{48,32},{56,40},{64,80... | collective-permute-start | bytes 1179656 | tf_op jit(solution)/shard_map/ppermute | solution.py:423
  111.7 5.3 %collective-permute-start.23 = (bf16[96,512]{1,0:T(8,128)(2,1)}, bf16[96,512]{1,0:T(8,128)(2,1)S(1)}, u32[]{:S(2)}, u32[]{:S(2)}) collective-permute-start(bf16[96,512]{1,0:T(8,128)(2,1)} %get-tuple-element.79), channel_id=1, source_target_pairs={{0,32},{8,40},{16,48},{24,56},{32,64},{40,72},{48,80},{56,88},{64,... | collective-permute-start | bytes 294920 | tf_op jit(solution)/shard_map/ppermute | solution.py:55
  112.6 4.3 %collective-permute-start.24 = (bf16[96,512]{1,0:T(8,128)(2,1)}, bf16[96,512]{1,0:T(8,128)(2,1)S(1)}, u32[]{:S(2)}, u32[]{:S(2)}) collective-permute-start(bf16[96,512]{1,0:T(8,128)(2,1)} %get-tuple-element.80), channel_id=1, source_target_pairs={{0,96},{8,104},{16,112},{24,120},{32,0},{40,8},{48,16},{56,24},{64... | collective-permute-start | bytes 294920 | tf_op jit(solution)/shard_map/ppermute | solution.py:55
  117.0 4.2 %copy-start.17 = (bf16[96,512]{1,0:T(8,128)(2,1)}, bf16[96,512]{1,0:T(8,128)(2,1)S(1)}, u32[]{:S(2)}) copy-start(bf16[96,512]{1,0:T(8,128)(2,1)S(1)} %collective-permute-done.23.via_up) | copy-start | bytes 294916
  117.0 4.2 %copy-start.18 = (bf16[96,512]{1,0:T(8,128)(2,1)}, bf16[96,512]{1,0:T(8,128)(2,1)S(1)}, u32[]{:S(2)}) copy-start(bf16[96,512]{1,0:T(8,128)(2,1)S(1)} %collective-permute-done.24.via_down) | copy-start | bytes 294916
  118.5 10.9 %collective-permute-start.26 = (bf16[96,1920]{1,0:T(8,128)(2,1)}, bf16[96,1920]{1,0:T(8,128)(2,1)S(1)}, u32[]{:S(2)}, u32[]{:S(2)}) collective-permute-start(bf16[96,1920]{1,0:T(8,128)(2,1)} %get-tuple-element.85), channel_id=1, source_target_pairs={{0,32},{8,40},{16,48},{24,56},{32,64},{40,72},{48,80},{56,88},{64,... | collective-permute-start | bytes 1105928 | tf_op jit(solution)/shard_map/ppermute | solution.py:55
  119.4 9.9 %collective-permute-start.27 = (bf16[96,1920]{1,0:T(8,128)(2,1)}, bf16[96,1920]{1,0:T(8,128)(2,1)}, u32[]{:S(2)}, u32[]{:S(2)}) collective-permute-start(bf16[96,1920]{1,0:T(8,128)(2,1)} %get-tuple-element.86), channel_id=1, source_target_pairs={{0,96},{8,104},{16,112},{24,120},{32,0},{40,8},{48,16},{56,24},{64... | collective-permute-start | bytes 1105928 | tf_op jit(solution)/shard_map/ppermute | solution.py:55
  131.4 13.8 %collective-permute-start.28 = (bf16[96,1920]{1,0:T(8,128)(2,1)}, bf16[96,1920]{1,0:T(8,128)(2,1)}, u32[]{:S(2)}, u32[]{:S(2)}) collective-permute-start(bf16[96,1920]{1,0:T(8,128)(2,1)} %select_convert_fusion), channel_id=1, source_target_pairs={{0,16},{8,24},{16,0},{24,8},{32,48},{40,56},{48,32},{56,40},{64,80... | collective-permute-start | bytes 1105928 | tf_op jit(solution)/shard_map/ppermute | solution.py:454
  134.5 23.7 %all-to-all-start = ((bf16[16,96,192]{2,1,0:T(8,128)(2,1)}), bf16[16,96,192]{2,1,0:T(8,128)(2,1)S(1)}, u32[]{:S(2)}, u32[]{:S(2)}) async-start(bf16[16,96,192]{2,1,0:T(8,128)(2,1)} %bitcast.15), calls=%async_computation | async-start | bytes 1572864 | tf_op jit(solution)/shard_map/all_to_all | solution.py:461
  146.9 3.7 %copy-start.16 = (f32[96,2,192]{2,1,0:T(2,128)S(1)}, f32[96,2,192]{2,1,0:T(2,128)}, u32[]{:S(2)}) copy-start(f32[96,2,192]{2,1,0:T(2,128)} %param.13) | copy-start | bytes 442372
  147.2 3.4 %collective-permute-start.29 = (bf16[96,192]{1,0:T(8,128)(2,1)S(1)}, bf16[96,192]{1,0:T(8,128)(2,1)S(1)}, u32[]{:S(2)}, u32[]{:S(2)}) collective-permute-start(bf16[96,192]{1,0:T(8,128)(2,1)S(1)} %bitcast.55), channel_id=1, source_target_pairs={{0,8},{8,0},{16,24},{24,16},{32,40},{40,32},{48,56},{56,48},{64,72... | collective-permute-start | bytes 110600 | tf_op jit(solution)/shard_map/ppermute | solution.py:459
  (6 other events, 5.2 us)
Sparse Core Ops, SparseCore 0:
  67.1 50.9 all-gather.1

commit v3 on v2

--- a/solution.py
+++ b/solution.py
@@ -18,7 +18,7 @@
 XLO = [(i, i ^ 2) for i in range(16)]
 XHI = [(j, j ^ 4) for j in range(8)]
 SAME_XHI = [[0, 1, 2, 3], [4, 5, 6, 7]]
-PARAMS = pltpu.CompilerParams(vmem_limit_bytes=56 * 2**20)
+PARAMS = pltpu.CompilerParams(vmem_limit_bytes=64 * 2**20)
 
 
 def to_z(s):
@@ -228,21 +228,38 @@
 
     @pl.when(y == 3)
     def _():
-        out[...] = total[...].astype(bf16)
-
-
-def last_kernel(spread, basis_out, out):
-    chunk = spread.shape[2]
-    rows = spread.shape[1]
-    total = None
-    for z in range(4):
-        lhs = jnp.concatenate(
-            [jnp.concatenate([spread[4 * z + a], spread[4 * z + 2 + a]], 1) for a in range(2)], 0
-        )
-        part = dot(lhs, basis_out[:, 2 * z * chunk : 2 * (z + 1) * chunk], ((1,), (1,)))
-        total = part if total is None else total + part
-    out[0] = total[:rows].astype(bf16)
-    out[1] = total[rows:].astype(bf16)
+        rows, main = out.shape[1] * 2 // 3, out.shape[2]
+        for d in range(16):
+            block = total[d * rows : (d + 1) * rows, :]
+            out[d, :rows, :] = block[:, :main].astype(bf16)
+            side = block[:, main:]
+            out[d, rows:, :] = jnp.concatenate([side[: rows // 2], side[rows // 2 :]], 1).astype(bf16)
+
+
+def last_kernel(spread, basis_out, out, total):
+    z = pl.program_id(0)
+    rows, main = out.shape[1], spread.shape[2]
+
+    def block(at):
+        side = spread[at, rows:, :]
+        side = jnp.concatenate([side[:, : main // 2], side[:, main // 2 :]], 0)
+        return jnp.concatenate([spread[at, :rows, :], side], 1)
+
+    lhs = [jnp.concatenate([block(4 * z + a), block(4 * z + 2 + a)], 1) for a in range(2)]
+    part = dot(jnp.concatenate(lhs, 0), basis_out[...], ((1,), (1,)))
+
+    @pl.when(z == 0)
+    def _():
+        total[...] = part
+
+    @pl.when(z > 0)
+    def _():
+        total[...] += part
+
+    @pl.when(z == 3)
+    def _():
+        out[0] = total[:rows].astype(bf16)
+        out[1] = total[rows:].astype(bf16)
 
 
 def per_device(
@@ -426,7 +443,7 @@
     healthy_rows = f32(tokens * lax.axis_size("dp")) - small[8, 0]
 
     cov_next = forward_z(cov_got_up, cov_got_down, cov_rest[2], cov_rest[3])
-    cov_next = lax.optimization_barrier((*cov_next, b_got, a_via_up, a_via_down))[:2]
+    cov_next = lax.optimization_barrier((*cov_next, b_got, a_via_up, a_via_down, healthy_rows))[:2]
     cov_via_up, cov_via_down = send_z(*cov_next)
 
     turn_in = (a_keep, a_via_up, a_via_down, b_keep, b_got)
@@ -437,7 +454,7 @@
         [whole(t.shape) for t in turn_in]
         + [pl.BlockSpec((1, width, 2 * cols), lambda i, p: (i, 0, 0))]
         + [whole((9, wide)), whole((4, wide)), whole((4, wide))],
-        [shape_of(width, chunk)],
+        [shape_of(16, rows * 3 // 2, chunk * 2 // 3)],
         (*turn_in, basis_all, small, scale_own, scale_chip),
         scratch=[
             pltpu.VMEM((chunk, width), bf16),
@@ -458,9 +475,16 @@
     in_give = lax.dynamic_index_in_dim(sum_in, 1 - core, 1, keepdims=False).astype(bf16)
     in_got = lax.ppermute(in_give, "dp", CORE).astype(f32)
 
-    spread = lax.all_to_all(turned.reshape(16, rows, chunk), "dp", split_axis=0, concat_axis=0)
+    spread = lax.all_to_all(turned, "dp", split_axis=0, concat_axis=0)
     result = pl.pallas_call(
-        last_kernel, out_shape=shape_of(2, rows, width), compiler_params=PARAMS, name="last_kernel"
+        last_kernel,
+        out_shape=shape_of(2, rows, width),
+        grid=(4,),
+        in_specs=[whole(spread.shape), pl.BlockSpec((width, wide), lambda i: (0, i))],
+        out_specs=whole((2, rows, width)),
+        scratch_shapes=[pltpu.VMEM((2 * rows, width), f32)],
+        compiler_params=PARAMS,
+        name="last_kernel",
     )(spread, basis_out)
 
     sum_in = jnp.where(core == 0, jnp.stack([in_keep, in_got], 1), jnp.stack([in_got, in_keep], 1))

time: 174 us -> 173 us (level)
  waiting for transfers between devices: 24.3 us -> 14.2 us
  other arithmetic: 9.71 us -> 16.9 us
  starting transfers between devices: 46.6 us -> 49 us
    unnamed x50 -> x14, local copies, waits for them, and re-layouts: 9.31 us -> 4.6 us
    all_to_all x1, waiting for transfers between devices: 6.67 us -> 3.06 us  [per_device(): spread = lax.all_to_all(turned, 'dp', split_axis=0, concat_axis=0)]
    ppermute x10, waiting for transfers between devices: 7.9 us -> 4.33 us  [send_z(): return (lax.ppermute(up, 'dp', UP), lax.ppermute(down, 'dp', DOWN))]
    all_to_all x1, starting transfers between devices: 10.8 us -> 12.8 us  [per_device(): spread = lax.all_to_all(turned, 'dp', split_axis=0, concat_axis=0)]
    ppermute x3, waiting for transfers between devices: 4.59 us -> 2.58 us  [per_device(): lax.ppermute(small, 'dp', to_z(i))]
    another operation x1, other arithmetic: 0.09 us -> 2.03 us  [per_device(): basis_four = jnp.stack([after(basis_pair, cov_up), *basis_z])]
  transfers between devices with their start and end apart: 32 -> 32, of which waited for: 11 -> 9; matrix products, arithmetic and copies ran while one was open for 7% -> 14% of each run, Pallas kernels for 31% -> 31%
where the time goes in v3:
time: 173 us; the launch traced here: 172 us
  Pallas kernels  62.1 us (36%)
  starting transfers between devices  49 us (28%)
  other arithmetic  16.9 us (10%)
  between operations  14.9 us (9%)
  local copies, waits for them, and re-layouts  14.4 us (8%)
  waiting for transfers between devices  14.2 us (8%)
    pallas_call x6, Pallas kernels, placed(): pl.pallas_call(kernel, out_shape=out_shapes, grid_spec=pltpu.PrefetchScal...  42.3 us
    all_to_all x1, starting transfers between devices, per_device(): spread = lax.all_to_all(turned, 'dp', split_axis=0, concat_axis=0)  12.8 us
    ppermute x10, starting transfers between devices, send_z(): return (lax.ppermute(up, 'dp', UP), lax.ppermute(down, 'dp', DOWN))  12.5 us
    pallas_call x2, Pallas kernels, rotate(): pl.pallas_call(rotate_kernel, out_shape=shape_of(width, tokens), grid_spe...  10.7 us
    pallas_call x1, Pallas kernels, per_device(): pl.pallas_call(last_kernel, out_shape=shape_of(2, rows, width), grid=(4,)...  5.67 us
    ppermute x3, starting transfers between devices, per_device(): basis_z = [lax.ppermute(basis_pair, 'dp', to_z(4 - s)) for s in (1, 2, 3)]  5.06 us
    unnamed x14, local copies, waits for them, and re-layouts  4.6 us
    ppermute x10, waiting for transfers between devices, send_z(): return (lax.ppermute(up, 'dp', UP), lax.ppermute(down, 'dp', DOWN))  4.33 us
  transfers between devices with their start and end apart: 32, of which 9 were waited for; matrix products, arithmetic and copies ran while one was open for 14% of the time, Pallas kernels for 31%

profile of v3, /device:TPU:1, one launch (start us, length us, event | category | flops | bytes accessed | tf_op | source)
XLA Modules:
  0.0 171.6 jit_solution(6503981418883081727)
XLA Ops:
  7.2 2.7 %constant_dynamic-slice_fusion.4 = bf16[512,1536]{1,0:T(8,128)(2,1)} fusion(bf16[512,3072]{1,0:T(8,128)(2,1)} %act_0.5, s32[]{:T(128)S(6)} %select_n.100), kind=kLoop, calls=%fused_computation.37 | loop fusion | bytes 3145732 | tf_op jit(solution)/shard_map/dynamic_slice | solution.py:294
  9.9 1.4 collective-permute-start
  14.0 5.4 %rotate_kernel.2.refs_0_ = bf16[1536,512]{1,0:T(8,128)(2,1)} custom-call(s32[4]{0:T(128)} %pad_add_fusion.place, bf16[512,1536]{1,0:T(8,128)(2,1)} %cot_0.1, s32[1,512]{1,0:T(1,128)} %bitcast.50, bf16[1536,1536]{1,0:T(8,128)(2,1)} %basis_out.1), custom_call_target="tpu_custom_call" | custom-call | tf_op jit(solution)/shard_map/rotate_kernel/pallas_call | solution.py:298
  19.4 1.6 maximum_select_fusion.1
  20.9 2.8 %collective-permute-start.3 = (bf16[192,192]{1,0:T(8,128)(2,1)}, bf16[192,192]{1,0:T(8,128)(2,1)}, u32[]{:S(2)}, u32[]{:S(2)}) collective-permute-start(bf16[192,192]{1,0:T(8,128)(2,1)} %maximum_select_fusion.1), channel_id=1, source_target_pairs={{0,4},{1,5},{2,6},{3,7},{4,0},{5,1},{6,2},{7,3},{8,12},{9,13},{10,... | collective-permute-start | bytes 221192 | tf_op jit(solution)/shard_map/ppermute | solution.py:324
  24.0 1.2 collective-permute-done.1.marks_1
  25.2 5.4 %rotate_kernel.3.eigen_0 = bf16[1536,512]{1,0:T(8,128)(2,1)} custom-call(s32[4]{0:T(128)} %pad_add_fusion.place, bf16[512,1536]{1,0:T(8,128)(2,1)} %cot_0.1, s32[1,512]{1,0:T(1,128)} %bitcast.52, bf16[1536,1536]{1,0:T(8,128)(2,1)} %basis_out.1, bf16[1536,512]{1,0:T(8,128)(2,1)} %rotate_kernel.2.refs_0_), custom_call_target="tpu_custom_call", output_to_operand_aliasing={{}: (4, {})} | custom-call | tf_op jit(solution)/shard_map/rotate_kernel/pallas_call | solution.py:298
  30.9 1.7 pad_maximum_fusion.1
  32.6 1.6 collective-permute-start.7
  34.2 2.1 %collective-permute-start.5 = (bf16[192,384]{1,0:T(8,128)(2,1)}, bf16[192,384]{1,0:T(8,128)(2,1)}, u32[]{:S(2)}, u32[]{:S(2)}) collective-permute-start(bf16[192,384]{1,0:T(8,128)(2,1)} %pad_maximum_fusion.1), channel_id=1, source_target_pairs={{0,96},{8,104},{16,112},{24,120},{32,0},{40,8},{48,16},{56,24},{64... | collective-permute-start | bytes 442376 | tf_op jit(solution)/shard_map/ppermute | solution.py:328
  36.4 1.3 collective-permute-start.6
  37.7 9.7 %cov_kernel.1 = (bf16[2,96,1920]{2,1,0:T(8,128)(2,1)}, bf16[2,96,1920]{2,1,0:T(8,128)(2,1)}, bf16[4,96,1920]{2,1,0:T(8,128)(2,1)}) custom-call(s32[4]{0:T(128)} %pad_add_fusion.place, bf16[512,1536]{1,0:T(8,128)(2,1)} %cot_0.1, bf16[512,1536]{1,0:T(8,128)(2,1)} %collective-permute-done.4.cot_1, s32[1,512]{1,0:T(1,128)} %bitcast.53, ...), custom_call_target="tpu_custom_call" | custom-call | tf_op jit(solution)/shard_map/cov_kernel/pallas_call | solution.py:71
  48.0 0.9 collective-permute-start.9
  48.9 2.0 %pad_maximum_fusion.own = bf16[4,192,384]{2,1,0:T(8,128)(2,1)} fusion(bf16[1,192,384]{2,1,0:T(8,128)(2,1)} %bitcast.10, bf16[1,192,384]{2,1,0:T(8,128)(2,1)} %bitcast.9, bf16[1,192,384]{2,1,0:T(8,128)(2,1)} %bitcast.8, bf16[1,192,384]{2,1,0:T(8,128)(2,1)} %bitcast.7), kind=kLoop, calls=%fused_computation.9 | loop fusion | flops 884736 | bytes 1179648 | tf_op jit(solution)/shard_map/stack | solution.py:353
  51.2 10.8 %grad_kernel.1 = (bf16[4,192,512]{2,1,0:T(8,128)(2,1)}, bf16[4,192,512]{2,1,0:T(8,128)(2,1)}, bf16[2,192,1024]{2,1,0:T(8,128)(2,1)}, bf16[2,192,1024]{2,1,0:T(8,...) custom-call(s32[4]{0:T(128)} %pad_add_fusion.place, ...), custom_call_target="tpu_custom_call" | custom-call | tf_op jit(solution)/shard_map/grad_kernel/pallas_call | solution.py:71
  62.0 2.6 %collective-permute-done.10 = bf16[2,96,1920]{2,1,0:T(8,128)(2,1)} collective-permute-done((bf16[2,96,1920]{2,1,0:T(8,128)(2,1)}, bf16[2,96,1920]{2,1,0:T(8,128)(2,1)}, u32[]{:S(2)}, u32[]{:S(2)}) %collective-permute-start.10) | collective-permute-done | bytes 737312 | tf_op jit(solution)/shard_map/ppermute | solution.py:55
  64.6 1.7 %collective-permute-done.9 = bf16[2,96,1920]{2,1,0:T(8,128)(2,1)} collective-permute-done((bf16[2,96,1920]{2,1,0:T(8,128)(2,1)}, bf16[2,96,1920]{2,1,0:T(8,128)(2,1)}, u32[]{:S(2)}, u32[]{:S(2)}) %collective-permute-start.9) | collective-permute-done | bytes 737312 | tf_op jit(solution)/shard_map/ppermute | solution.py:55
  66.3 3.1 %rows_kernel.1 = bf16[4,2,192,384]{3,2,1,0:T(8,128)(2,1)} custom-call(s32[4]{0:T(128)} %pad_add_fusion.place, bf16[4,192,384]{2,1,0:T(8,128)(2,1)} %pad_maximum_fusion.own, bf16[4,192,384]{2,1,0:T(8,128)(2,1)} %collective-permute-done.11.got), custom_call_target="tpu_custom_call" | custom-call | tf_op jit(solution)/shard_map/rows_kernel/pallas_call | solution.py:71
  69.8 2.7 %collective-permute-start.16 = (bf16[2,192,1024]{2,1,0:T(8,128)(2,1)}, bf16[2,192,1024]{2,1,0:T(8,128)(2,1)}, u32[]{:S(2)}, u32[]{:S(2)}) collective-permute-start(bf16[2,192,1024]{2,1,0:T(8,128)(2,1)} %get-tuple-element.66), channel_id=1, source_target_pairs={{0,96},{8,104},{16,112},{24,120},{32,0},{40,8},{48,16},{56,24},{64... | collective-permute-start | bytes 2359304 | tf_op jit(solution)/shard_map/ppermute | solution.py:55
  72.5 6.5 %squares_kernel.1 = (f32[1,384]{1,0:T(1,128)}, f32[5,384]{1,0:T(8,128)}) custom-call(s32[4]{0:T(128)} %pad_add_fusion.place, bf16[512,3072]{1,0:T(8,128)(2,1)} %act_0.5, bf16[512,1536]{1,0:T(8,128)(2,1)} %collective-permute-done.act_1.cols_1, s32[1,512]{1,0:T(1,128)} %bitcast.54, s32[1,512]{1,0:T(1,128)} %collective-permute-done.1.marks_1, ...), custom_call_target="tpu_custom_call" | custom-call | tf_op jit(solution)/shard_map/squares_kernel/pallas_call | solution.py:71
  79.0 1.3 collective-permute-start.12
  81.1 0.9 collective-permute-done.12
  82.8 3.0 %collective-permute-start.13 = (f32[2,384]{1,0:T(2,128)S(1)}, f32[2,384]{1,0:T(2,128)S(1)}, u32[]{:S(2)}, u32[]{:S(2)}) collective-permute-start(f32[2,384]{1,0:T(2,128)S(1)} %maximum_select_fusion.3), channel_id=1, source_target_pairs={{0,2},{1,3},{2,0},{3,1},{4,6},{5,7},{6,4},{7,5},{8,10},{9,11},{10,... | collective-permute-start | bytes 9224 | tf_op jit(solution)/shard_map/ppermute | solution.py:396
  86.4 1.3 slice.45
  87.7 1.3 slice.46
  89.6 3.4 %second_kernel.1 = (bf16[192,1536]{1,0:T(8,128)(2,1)}, bf16[192,1536]{1,0:T(8,128)(2,1)}, bf16[96,512]{1,0:T(8,128)(2,1)}, bf16[96,512]{1,0:T(8,128)(2,1)}, bf16[2,96,512]{2,1,0:T(8,128)(2,1)}) custom-call(bf16[4,192,512]{2,1,0:T(8,128)(2,1)} %get-tuple-element.60.keep, bf16[4,192,512]{2,1,0:T(8,128)(2,1)} %collective-permute-done.14.got_a, ...), custom_call_target="tpu_custom_call" | custom-call | tf_op jit(solution)/shard_map/second_kernel/pallas_call | solution.py:402
  93.0 2.7 %collective-permute-start.22 = (bf16[192,1536]{1,0:T(8,128)(2,1)}, bf16[192,1536]{1,0:T(8,128)(2,1)}, u32[]{:S(2)}, u32[]{:S(2)}) collective-permute-start(bf16[192,1536]{1,0:T(8,128)(2,1)} %get-tuple-element.74), channel_id=1, source_target_pairs={{0,96},{8,104},{16,112},{24,120},{32,0},{40,8},{48,16},{56,24},{64... | collective-permute-start | bytes 1769480 | tf_op jit(solution)/shard_map/ppermute | solution.py:55
  96.4 1.2 collective-permute-start.17
  98.3 1.3 collective-permute-done.17
  99.6 2.7 %collective-permute-start.19 = (f32[9,384]{1,0:T(8,128)S(1)}, f32[9,384]{1,0:T(8,128)S(1)}, u32[]{:S(2)}, u32[]{:S(2)}) collective-permute-start(f32[9,384]{1,0:T(8,128)S(1)} %add.86), channel_id=1, source_target_pairs={{0,96},{8,104},{16,112},{24,120},{32,0},{40,8},{48,16},{56,24},{64... | collective-permute-start | bytes 41480 | tf_op jit(solution)/shard_map/ppermute | solution.py:418
  103.0 1.3 reshape.42.scale_out
  104.2 1.1 collective-permute-done.18
  105.4 1.4 collective-permute-done.20
  107.5 4.0 %third_kernel.1 = (bf16[96,512]{1,0:T(8,128)(2,1)}, bf16[96,512]{1,0:T(8,128)(2,1)}, bf16[192,1024]{1,0:T(8,128)(2,1)}, f32[192,1024]{1,0:T(8,128)}, f32[2,96,512]{2,1,0:T(8,128)}) custom-call(s32[4]{0:T(128)} %pad_add_fusion.place, bf16[2,192,1024]{2,1,0:T(8,128)(2,1)} %collective-permute-done.15.got_up, ...), custom_call_target="tpu_custom_call" | custom-call | tf_op jit(solution)/shard_map/third_kernel/pallas_call | solution.py:71
  111.4 1.2 collective-permute-start.25
  112.6 2.7 %collective-permute-start.24 = (bf16[96,512]{1,0:T(8,128)(2,1)}, bf16[96,512]{1,0:T(8,128)(2,1)}, u32[]{:S(2)}, u32[]{:S(2)}) collective-permute-start(bf16[96,512]{1,0:T(8,128)(2,1)} %get-tuple-element.80), channel_id=1, source_target_pairs={{0,96},{8,104},{16,112},{24,120},{32,0},{40,8},{48,16},{56,24},{64... | collective-permute-start | bytes 294920 | tf_op jit(solution)/shard_map/ppermute | solution.py:55
  115.3 2.4 %fusion.3 = (bf16[96,1920]{1,0:T(8,128)(2,1)}, bf16[96,1920]{1,0:T(8,128)(2,1)}) fusion(bf16[2,96,1920]{2,1,0:T(8,128)(2,1)} %collective-permute-done.10, bf16[4,96,1920]{2,1,0:T(8,128)(2,1)} %get-tuple-element.84, bf16[2,96,1920]{2,1,0:T(8,128)(2,1)} %collective-permute-done.9), kind=kLoop, calls=%fused_computation.11 | loop fusion | flops 1474560 | bytes 2211840 | tf_op jit(solution)/shard_map/convert_element_type | solution.py:59
  117.7 1.2 slice.65
  119.8 2.7 %collective-permute-start.27 = (bf16[96,1920]{1,0:T(8,128)(2,1)}, bf16[96,1920]{1,0:T(8,128)(2,1)}, u32[]{:S(2)}, u32[]{:S(2)}) collective-permute-start(bf16[96,1920]{1,0:T(8,128)(2,1)} %get-tuple-element.86), channel_id=1, source_target_pairs={{0,96},{8,104},{16,112},{24,120},{32,0},{40,8},{48,16},{56,24},{64... | collective-permute-start | bytes 1105928 | tf_op jit(solution)/shard_map/ppermute | solution.py:55
  122.5 8.2 %turn_kernel.1 = bf16[16,144,128]{2,1,0:T(8,128)(2,1)} custom-call(s32[4]{0:T(128)} %pad_add_fusion.place, f32[2,96,512]{2,1,0:T(8,128)} %get-tuple-element.78.keep_a, bf16[96,512]{1,0:T(8,128)(2,1)} %collective-permute-done.23.via_up, bf16[96,512]{1,0:T(8,128)(2,1)} %collective-permute-done.24.via_down, f32[192,1024]{1,0:T(8,128)} %get-tuple-element.81.keep_b, ...), custom_call_target="tpu_custom_call" | custom-call | tf_op jit(solution)/shard_map/turn_kernel/pallas_call | solution.py:71
  130.7 1.9 %select_convert_fusion = bf16[96,1920]{1,0:T(8,128)(2,1)S(1)} fusion(bf16[96,1920]{1,0:T(8,128)(2,1)} %collective-permute-done.26, bf16[96,1920]{1,0:T(8,128)(2,1)} %collective-permute-done.27, pred[]{:T(512)S(6)} %eq.22, bf16[2,96,1920]{2,1,0:T(8,128)(2,1)} %collective-permute-done.9, bf16[2,96,1920]{2,1,0:T(8,128)(2,1)} %collective-permute-done.10, ...), kind=kLoop, calls=%fused_computation.3 | loop fusion | flops 2211840 | bytes 2580481 | tf_op jit(solution)/shard_map/convert_element_type | solution.py:469
  133.0 12.8 %all-to-all-start = ((bf16[16,144,128]{2,1,0:T(8,128)(2,1)}), bf16[16,144,128]{2,1,0:T(8,128)(2,1)}, u32[]{:S(2)}, u32[]{:S(2)}) async-start(bf16[16,144,128]{2,1,0:T(8,128)(2,1)} %turn_kernel.1), calls=%async_computation | async-start | bytes 1179648 | tf_op jit(solution)/shard_map/all_to_all | solution.py:478
  145.9 1.7 convert_add_fusion
  147.6 0.9 fusion.1
  148.8 2.9 %collective-permute-start.29 = (bf16[96,192]{1,0:T(8,128)(2,1)S(1)}, bf16[96,192]{1,0:T(8,128)(2,1)S(1)}, u32[]{:S(2)}, u32[]{:S(2)}) collective-permute-start(bf16[96,192]{1,0:T(8,128)(2,1)S(1)} %bitcast.49), channel_id=1, source_target_pairs={{0,8},{8,0},{16,24},{24,16},{32,40},{40,32},{48,56},{56,48},{64,72... | collective-permute-start | bytes 110600 | tf_op jit(solution)/shard_map/ppermute | solution.py:476
  153.5 3.1 %all-to-all-done.spread = bf16[16,144,128]{2,1,0:T(8,128)(2,1)} async-done(((bf16[16,144,128]{2,1,0:T(8,128)(2,1)}), bf16[16,144,128]{2,1,0:T(8,128)(2,1)}, u32[]{:S(2)}, u32[]{:S(2)}) %all-to-all-start) | async-done | bytes 589856 | tf_op jit(solution)/shard_map/all_to_all | solution.py:478
  156.6 5.7 %last_kernel.1 = bf16[2,96,1536]{2,1,0:T(8,128)(2,1)} custom-call(bf16[16,144,128]{2,1,0:T(8,128)(2,1)} %all-to-all-done.spread, bf16[1536,1536]{1,0:T(8,128)(2,1)} %basis_out.1), custom_call_target="tpu_custom_call" | custom-call | tf_op jit(solution)/shard_map/last_kernel/pallas_call | solution.py:479
  162.2 2.5 %copy.27 = bf16[96,2,1536]{2,1,0:T(2,128)(2,1)} copy(bf16[96,2,1536]{2,0,1:T(8,128)(2,1)} %bitcast.47) | data formatting | bytes 1179648
  (71 shorter events, 12.8 us)
Async XLA Ops:
  7.2 115.3 %all-gather.2.cloned.1.call-start = ((), (), s32[]{:S(2)}) async-start(), calls=%async_computation.1 | async-start | bytes 5898240 | tf_op jit(solution)/shard_map/all_gather | solution.py:378
  7.2 4.1 %copy-start.2 = (bf16[96,2,192]{2,1,0:T(2,128)(2,1)S(1)}, bf16[96,2,192]{2,1,0:T(2,128)(2,1)}, u32[]{:S(2)}) copy-start(bf16[96,2,192]{2,1,0:T(2,128)(2,1)} %param.11) | copy-start | bytes 221188
  9.9 26.4 %collective-permute-start = (bf16[512,1536]{1,0:T(8,128)(2,1)}, bf16[512,1536]{1,0:T(8,128)(2,1)}, u32[]{:S(2)}, u32[]{:S(2)}) collective-permute-start(bf16[512,1536]{1,0:T(8,128)(2,1)} %constant_dynamic-slice_fusion.4), channel_id=1, source_target_pairs={{0,8},{8,0},{16,24},{24,16},{32,40},{40,32},{48,56},{56,48},{64,72... | collective-permute-start | bytes 4718600 | tf_op jit(solution)/shard_map/ppermute | solution.py:295
  11.4 26.3 %collective-permute-start.4 = (bf16[512,1536]{1,0:T(8,128)(2,1)}, bf16[512,1536]{1,0:T(8,128)(2,1)}, u32[]{:S(2)}, u32[]{:S(2)}) collective-permute-start(bf16[512,1536]{1,0:T(8,128)(2,1)} %cot_0.1), channel_id=1, source_target_pairs={{0,8},{8,0},{16,24},{24,16},{32,40},{40,32},{48,56},{56,48},{64,72... | collective-permute-start | bytes 4718600 | tf_op jit(solution)/shard_map/ppermute | solution.py:293
  12.2 7.1 %collective-permute-start.2 = (bf16[96,192]{1,0:T(8,128)(2,1)}, bf16[96,192]{1,0:T(8,128)(2,1)}, u32[]{:S(2)}, u32[]{:S(2)}) collective-permute-start(bf16[96,192]{1,0:T(8,128)(2,1)} %bitcast.43), channel_id=1, source_target_pairs={{0,8},{8,0},{16,24},{24,16},{32,40},{40,32},{48,56},{56,48},{64,72... | collective-permute-start | bytes 110600 | tf_op jit(solution)/shard_map/ppermute | solution.py:290
  20.9 9.7 %collective-permute-start.3 = (bf16[192,192]{1,0:T(8,128)(2,1)}, bf16[192,192]{1,0:T(8,128)(2,1)}, u32[]{:S(2)}, u32[]{:S(2)}) collective-permute-start(bf16[192,192]{1,0:T(8,128)(2,1)} %maximum_select_fusion.1), channel_id=1, source_target_pairs={{0,4},{1,5},{2,6},{3,7},{4,0},{5,1},{6,2},{7,3},{8,12},{9,13},{10,... | collective-permute-start | bytes 221192 | tf_op jit(solution)/shard_map/ppermute | solution.py:324
  23.7 1.5 collective-permute-start.1
  30.6 20.6 %collective-permute-start.8 = (bf16[1536,512]{1,0:T(8,128)(2,1)}, bf16[1536,512]{1,0:T(8,128)(2,1)}, u32[]{:S(2)}, u32[]{:S(2)}) collective-permute-start(bf16[1536,512]{1,0:T(8,128)(2,1)} %rotate_kernel.3.eigen_0), channel_id=1, source_target_pairs={{0,8},{8,0},{16,24},{24,16},{32,40},{40,32},{48,56},{56,48},{64,72... | collective-permute-start | bytes 4718600 | tf_op jit(solution)/shard_map/ppermute | solution.py:326
  32.6 15.4 %collective-permute-start.7 = (bf16[192,384]{1,0:T(8,128)(2,1)}, bf16[192,384]{1,0:T(8,128)(2,1)}, u32[]{:S(2)}, u32[]{:S(2)}) collective-permute-start(bf16[192,384]{1,0:T(8,128)(2,1)} %pad_maximum_fusion.1), channel_id=1, source_target_pairs={{0,32},{8,40},{16,48},{24,56},{32,64},{40,72},{48,80},{56,88},{64,... | collective-permute-start | bytes 442376 | tf_op jit(solution)/shard_map/ppermute | solution.py:328
  34.2 14.6 %collective-permute-start.5 = (bf16[192,384]{1,0:T(8,128)(2,1)}, bf16[192,384]{1,0:T(8,128)(2,1)}, u32[]{:S(2)}, u32[]{:S(2)}) collective-permute-start(bf16[192,384]{1,0:T(8,128)(2,1)} %pad_maximum_fusion.1), channel_id=1, source_target_pairs={{0,96},{8,104},{16,112},{24,120},{32,0},{40,8},{48,16},{56,24},{64... | collective-permute-start | bytes 442376 | tf_op jit(solution)/shard_map/ppermute | solution.py:328
  36.4 12.5 %collective-permute-start.6 = (bf16[192,384]{1,0:T(8,128)(2,1)}, bf16[192,384]{1,0:T(8,128)(2,1)}, u32[]{:S(2)}, u32[]{:S(2)}) collective-permute-start(bf16[192,384]{1,0:T(8,128)(2,1)} %pad_maximum_fusion.1), channel_id=1, source_target_pairs={{0,64},{8,72},{16,80},{24,88},{32,96},{40,104},{48,112},{56,120},{... | collective-permute-start | bytes 442376 | tf_op jit(solution)/shard_map/ppermute | solution.py:328
  47.4 17.2 %collective-permute-start.10 = (bf16[2,96,1920]{2,1,0:T(8,128)(2,1)}, bf16[2,96,1920]{2,1,0:T(8,128)(2,1)}, u32[]{:S(2)}, u32[]{:S(2)}) collective-permute-start(bf16[2,96,1920]{2,1,0:T(8,128)(2,1)} %get-tuple-element.55), channel_id=1, source_target_pairs={{0,96},{8,104},{16,112},{24,120},{32,0},{40,8},{48,16},{56,24},{64... | collective-permute-start | bytes 2211848 | tf_op jit(solution)/shard_map/ppermute | solution.py:55
  48.0 18.3 %collective-permute-start.9 = (bf16[2,96,1920]{2,1,0:T(8,128)(2,1)}, bf16[2,96,1920]{2,1,0:T(8,128)(2,1)}, u32[]{:S(2)}, u32[]{:S(2)}) collective-permute-start(bf16[2,96,1920]{2,1,0:T(8,128)(2,1)} %get-tuple-element.50), channel_id=1, source_target_pairs={{0,32},{8,40},{16,48},{24,56},{32,64},{40,72},{48,80},{56,88},{64,... | collective-permute-start | bytes 2211848 | tf_op jit(solution)/shard_map/ppermute | solution.py:55
  50.9 15.4 %collective-permute-start.11 = (bf16[4,192,384]{2,1,0:T(8,128)(2,1)}, bf16[4,192,384]{2,1,0:T(8,128)(2,1)}, u32[]{:S(2)}, u32[]{:S(2)}) collective-permute-start(bf16[4,192,384]{2,1,0:T(8,128)(2,1)} %pad_maximum_fusion.own), channel_id=1, source_target_pairs={{0,16},{8,24},{16,0},{24,8},{32,48},{40,56},{48,32},{56,40},{64,80... | collective-permute-start | bytes 1769480 | tf_op jit(solution)/shard_map/ppermute | solution.py:354
  69.4 20.2 %collective-permute-start.14 = (bf16[4,192,512]{2,1,0:T(8,128)(2,1)}, bf16[4,192,512]{2,1,0:T(8,128)(2,1)}, u32[]{:S(2)}, u32[]{:S(2)}) collective-permute-start(bf16[4,192,512]{2,1,0:T(8,128)(2,1)} %get-tuple-element.64), channel_id=1, source_target_pairs={{0,16},{8,24},{16,0},{24,8},{32,48},{40,56},{48,32},{56,40},{64,80... | collective-permute-start | bytes 2359304 | tf_op jit(solution)/shard_map/ppermute | solution.py:399
  69.8 19.8 %collective-permute-start.15 = (bf16[2,192,1024]{2,1,0:T(8,128)(2,1)}, bf16[2,192,1024]{2,1,0:T(8,128)(2,1)}, u32[]{:S(2)}, u32[]{:S(2)}) collective-permute-start(bf16[2,192,1024]{2,1,0:T(8,128)(2,1)} %get-tuple-element.65), channel_id=1, source_target_pairs={{0,32},{8,40},{16,48},{24,56},{32,64},{40,72},{48,80},{56,88},{64,... | collective-permute-start | bytes 2359304 | tf_op jit(solution)/shard_map/ppermute | solution.py:55
  69.8 19.8 %collective-permute-start.16 = (bf16[2,192,1024]{2,1,0:T(8,128)(2,1)}, bf16[2,192,1024]{2,1,0:T(8,128)(2,1)}, u32[]{:S(2)}, u32[]{:S(2)}) collective-permute-start(bf16[2,192,1024]{2,1,0:T(8,128)(2,1)} %get-tuple-element.66), channel_id=1, source_target_pairs={{0,96},{8,104},{16,112},{24,120},{32,0},{40,8},{48,16},{56,24},{64... | collective-permute-start | bytes 2359304 | tf_op jit(solution)/shard_map/ppermute | solution.py:55
  79.0 3.0 %collective-permute-start.12 = (f32[1,384]{1,0:T(1,128)}, f32[1,384]{1,0:T(1,128)S(1)}, u32[]{:S(2)}, u32[]{:S(2)}) collective-permute-start(f32[1,384]{1,0:T(1,128)} %get-tuple-element.58), channel_id=1, source_target_pairs={{0,1},{1,0},{2,3},{3,2},{4,5},{5,4},{6,7},{7,6},{8,9},{9,8},{10,11... | collective-permute-start | bytes 4616 | tf_op jit(solution)/shard_map/ppermute | solution.py:395
  82.8 6.2 %collective-permute-start.13 = (f32[2,384]{1,0:T(2,128)S(1)}, f32[2,384]{1,0:T(2,128)S(1)}, u32[]{:S(2)}, u32[]{:S(2)}) collective-permute-start(f32[2,384]{1,0:T(2,128)S(1)} %maximum_select_fusion.3), channel_id=1, source_target_pairs={{0,2},{1,3},{2,0},{3,1},{4,6},{5,7},{6,4},{7,5},{8,10},{9,11},{10,... | collective-permute-start | bytes 9224 | tf_op jit(solution)/shard_map/ppermute | solution.py:396
  93.0 14.4 %collective-permute-start.21 = (bf16[192,1536]{1,0:T(8,128)(2,1)}, bf16[192,1536]{1,0:T(8,128)(2,1)}, u32[]{:S(2)}, u32[]{:S(2)}) collective-permute-start(bf16[192,1536]{1,0:T(8,128)(2,1)} %get-tuple-element.69), channel_id=1, source_target_pairs={{0,32},{8,40},{16,48},{24,56},{32,64},{40,72},{48,80},{56,88},{64,... | collective-permute-start | bytes 1769480 | tf_op jit(solution)/shard_map/ppermute | solution.py:55
  93.0 14.4 %collective-permute-start.22 = (bf16[192,1536]{1,0:T(8,128)(2,1)}, bf16[192,1536]{1,0:T(8,128)(2,1)}, u32[]{:S(2)}, u32[]{:S(2)}) collective-permute-start(bf16[192,1536]{1,0:T(8,128)(2,1)} %get-tuple-element.74), channel_id=1, source_target_pairs={{0,96},{8,104},{16,112},{24,120},{32,0},{40,8},{48,16},{56,24},{64... | collective-permute-start | bytes 1769480 | tf_op jit(solution)/shard_map/ppermute | solution.py:55
  96.4 3.2 %collective-permute-start.17 = (f32[9,384]{1,0:T(8,128)S(1)}, f32[9,384]{1,0:T(8,128)S(1)}, u32[]{:S(2)}, u32[]{:S(2)}) collective-permute-start(f32[9,384]{1,0:T(8,128)S(1)} %pad_maximum_fusion.2), channel_id=1, source_target_pairs={{0,16},{8,24},{16,0},{24,8},{32,48},{40,56},{48,32},{56,40},{64,80... | collective-permute-start | bytes 41480 | tf_op jit(solution)/shard_map/ppermute | solution.py:417
  99.6 5.8 %collective-permute-start.18 = (f32[9,384]{1,0:T(8,128)S(1)}, f32[9,384]{1,0:T(8,128)S(1)}, u32[]{:S(2)}, u32[]{:S(2)}) collective-permute-start(f32[9,384]{1,0:T(8,128)S(1)} %add.86), channel_id=1, source_target_pairs={{0,32},{8,40},{16,48},{24,56},{32,64},{40,72},{48,80},{56,88},{64,... | collective-permute-start | bytes 41480 | tf_op jit(solution)/shard_map/ppermute | solution.py:418
  99.6 5.8 %collective-permute-start.19 = (f32[9,384]{1,0:T(8,128)S(1)}, f32[9,384]{1,0:T(8,128)S(1)}, u32[]{:S(2)}, u32[]{:S(2)}) collective-permute-start(f32[9,384]{1,0:T(8,128)S(1)} %add.86), channel_id=1, source_target_pairs={{0,96},{8,104},{16,112},{24,120},{32,0},{40,8},{48,16},{56,24},{64... | collective-permute-start | bytes 41480 | tf_op jit(solution)/shard_map/ppermute | solution.py:418
  102.3 4.6 %collective-permute-start.20 = (f32[9,384]{1,0:T(8,128)S(1)}, f32[9,384]{1,0:T(8,128)S(1)}, u32[]{:S(2)}, u32[]{:S(2)}) collective-permute-start(f32[9,384]{1,0:T(8,128)S(1)} %add.86), channel_id=1, source_target_pairs={{0,64},{8,72},{16,80},{24,88},{32,96},{40,104},{48,112},{56,120},{... | collective-permute-start | bytes 41480 | tf_op jit(solution)/shard_map/ppermute | solution.py:418
  111.4 8.1 %collective-permute-start.25 = (bf16[192,1024]{1,0:T(8,128)(2,1)}, bf16[192,1024]{1,0:T(8,128)(2,1)}, u32[]{:S(2)}, u32[]{:S(2)}) collective-permute-start(bf16[192,1024]{1,0:T(8,128)(2,1)} %get-tuple-element.82), channel_id=1, source_target_pairs={{0,16},{8,24},{16,0},{24,8},{32,48},{40,56},{48,32},{56,40},{64,80... | collective-permute-start | bytes 1179656 | tf_op jit(solution)/shard_map/ppermute | solution.py:440
  112.6 6.9 %collective-permute-start.23 = (bf16[96,512]{1,0:T(8,128)(2,1)}, bf16[96,512]{1,0:T(8,128)(2,1)}, u32[]{:S(2)}, u32[]{:S(2)}) collective-permute-start(bf16[96,512]{1,0:T(8,128)(2,1)} %get-tuple-element.79), channel_id=1, source_target_pairs={{0,32},{8,40},{16,48},{24,56},{32,64},{40,72},{48,80},{56,88},{64,... | collective-permute-start | bytes 294920 | tf_op jit(solution)/shard_map/ppermute | solution.py:55
  112.6 6.9 %collective-permute-start.24 = (bf16[96,512]{1,0:T(8,128)(2,1)}, bf16[96,512]{1,0:T(8,128)(2,1)}, u32[]{:S(2)}, u32[]{:S(2)}) collective-permute-start(bf16[96,512]{1,0:T(8,128)(2,1)} %get-tuple-element.80), channel_id=1, source_target_pairs={{0,96},{8,104},{16,112},{24,120},{32,0},{40,8},{48,16},{56,24},{64... | collective-permute-start | bytes 294920 | tf_op jit(solution)/shard_map/ppermute | solution.py:55
  119.5 11.1 %collective-permute-start.26 = (bf16[96,1920]{1,0:T(8,128)(2,1)}, bf16[96,1920]{1,0:T(8,128)(2,1)}, u32[]{:S(2)}, u32[]{:S(2)}) collective-permute-start(bf16[96,1920]{1,0:T(8,128)(2,1)} %get-tuple-element.85), channel_id=1, source_target_pairs={{0,32},{8,40},{16,48},{24,56},{32,64},{40,72},{48,80},{56,88},{64,... | collective-permute-start | bytes 1105928 | tf_op jit(solution)/shard_map/ppermute | solution.py:55
  119.8 10.8 %collective-permute-start.27 = (bf16[96,1920]{1,0:T(8,128)(2,1)}, bf16[96,1920]{1,0:T(8,128)(2,1)}, u32[]{:S(2)}, u32[]{:S(2)}) collective-permute-start(bf16[96,1920]{1,0:T(8,128)(2,1)} %get-tuple-element.86), channel_id=1, source_target_pairs={{0,96},{8,104},{16,112},{24,120},{32,0},{40,8},{48,16},{56,24},{64... | collective-permute-start | bytes 1105928 | tf_op jit(solution)/shard_map/ppermute | solution.py:55
  130.7 15.2 %copy-start = (bf16[4,96,1920]{2,1,0:T(8,128)(2,1)S(1)}, bf16[4,96,1920]{2,1,0:T(8,128)(2,1)}, u32[]{:S(2)}) copy-start(bf16[4,96,1920]{2,1,0:T(8,128)(2,1)} %get-tuple-element.84) | copy-start | bytes 4423684
  132.6 13.2 %collective-permute-start.28 = (bf16[96,1920]{1,0:T(8,128)(2,1)S(1)}, bf16[96,1920]{1,0:T(8,128)(2,1)S(1)}, u32[]{:S(2)}, u32[]{:S(2)}) collective-permute-start(bf16[96,1920]{1,0:T(8,128)(2,1)S(1)} %select_convert_fusion), channel_id=1, source_target_pairs={{0,16},{8,24},{16,0},{24,8},{32,48},{40,56},{48,32},{56,40},{64,80... | collective-permute-start | bytes 1105928 | tf_op jit(solution)/shard_map/ppermute | solution.py:471
  133.0 23.5 %all-to-all-start = ((bf16[16,144,128]{2,1,0:T(8,128)(2,1)}), bf16[16,144,128]{2,1,0:T(8,128)(2,1)}, u32[]{:S(2)}, u32[]{:S(2)}) async-start(bf16[16,144,128]{2,1,0:T(8,128)(2,1)} %turn_kernel.1), calls=%async_computation | async-start | bytes 1179648 | tf_op jit(solution)/shard_map/all_to_all | solution.py:478
  145.8 1.7 %copy-start.1 = (f32[96,1536]{1,0:T(8,128)S(1)}, f32[96,1536]{1,0:T(8,128)}, u32[]{:S(2)}) copy-start(f32[96,1536]{1,0:T(8,128)} %param.14) | copy-start | bytes 1769476
  147.6 5.0 %copy-start.3 = (f32[96,2,192]{2,1,0:T(2,128)S(1)}, f32[96,2,192]{2,1,0:T(2,128)}, u32[]{:S(2)}) copy-start(f32[96,2,192]{2,1,0:T(2,128)} %param.13) | copy-start | bytes 442372
  148.8 3.8 %collective-permute-start.29 = (bf16[96,192]{1,0:T(8,128)(2,1)S(1)}, bf16[96,192]{1,0:T(8,128)(2,1)S(1)}, u32[]{:S(2)}, u32[]{:S(2)}) collective-permute-start(bf16[96,192]{1,0:T(8,128)(2,1)S(1)} %bitcast.49), channel_id=1, source_target_pairs={{0,8},{8,0},{16,24},{24,16},{32,40},{40,32},{48,56},{56,48},{64,72... | collective-permute-start | bytes 110600 | tf_op jit(solution)/shard_map/ppermute | solution.py:476
Sparse Core Ops, SparseCore 0:
  69.5 51.5 all-gather.1

commit v4 on v3

--- a/solution.py
+++ b/solution.py
@@ -19,6 +19,7 @@
 XHI = [(j, j ^ 4) for j in range(8)]
 SAME_XHI = [[0, 1, 2, 3], [4, 5, 6, 7]]
 PARAMS = pltpu.CompilerParams(vmem_limit_bytes=64 * 2**20)
+EARLY = pltpu.CompilerParams(vmem_limit_bytes=56 * 2**20)
 
 
 def to_z(s):
@@ -67,7 +68,7 @@
     return pl.BlockSpec(shape, lambda *_: (0,) * len(shape))
 
 
-def placed(kernel, place, grid, in_specs, out_shapes, operands, out_specs=None, scratch=(), name=None):
+def placed(kernel, place, grid, in_specs, out_shapes, operands, out_specs=None, scratch=(), name=None, params=PARAMS):
     return pl.pallas_call(
         kernel,
         out_shape=out_shapes,
@@ -78,7 +79,7 @@
             out_specs=out_specs or [whole(s.shape) for s in out_shapes],
             scratch_shapes=list(scratch),
         ),
-        compiler_params=PARAMS,
+        compiler_params=params,
         name=name or kernel.__name__,
     )(place, *operands)
 
@@ -203,13 +204,13 @@
 
 
 def turn_kernel(
-    place, keep_a, via_up, via_down, keep_b, got_b, basis, small, scale_in, scale_out, out, grad, total, lam_out, rows_all
+    place, keep_a, via_up, via_down, keep_b, got_b, basis, small, scale_in, scale_out, out, grad, total, lam_out, scales, rows_all
 ):
     y = pl.program_id(0)
     cut = keep_a.shape[2]
     part = keep_a.shape[1]
     chunk = 2 * part
-    healthy_rows = rows_all - small[8:9, 0:1]
+    healthy_rows = rows_all - small[4:5, 0:1]
 
     @pl.when(y == 0)
     def _():
@@ -217,11 +218,18 @@
         grad[part:, :cut] = added(keep_a[1], via_down[...]).astype(bf16)
         grad[:, cut:] = added(keep_b[...], got_b[...]).astype(bf16)
         total[...] = jnp.zeros(total.shape, f32)
-        lam = decay_rate * scale_out[pl.ds(place[0], 1), :] + blend_weight * small[pl.ds(place[0], 1), :] / healthy_rows
+        wide = 2 * chunk
+        scale = scale_out[:, pl.ds(pl.multiple_of(place[0] * wide, wide), wide)]
+        lam = decay_rate * scale + blend_weight * small[pl.ds(place[0], 1), :] / healthy_rows
         lam = jnp.where(place[1] == 0, lam[:, :chunk], lam[:, chunk:]) * healthy_rows
+        row = scale_in[pl.ds(place[2], 1), :]
+        for k in range(4):
+            halves = [row[:, i : i + chunk] for i in (k * chunk, (4 + k) * chunk)]
+            swapped = jnp.concatenate(halves[::-1], 1)
+            scales[k : k + 1, :] = jnp.where(place[3] < 4, jnp.concatenate(halves, 1), swapped)
         lam_out[...] = jnp.swapaxes(jnp.broadcast_to(lam, (lam_out.shape[1], chunk)), 0, 1)
 
-    lam_in = decay_rate * scale_in[pl.ds(y, 1), :] + blend_weight * small[pl.ds(4 + y, 1), :] / healthy_rows
+    lam_in = decay_rate * scales[pl.ds(y, 1), :] + blend_weight * small[pl.ds(5 + y, 1), :] / healthy_rows
     rotated = dot(grad[...], basis[0])
     scaled = (rotated / (lam_out[:, :1] * lam_in + damping * healthy_rows)).astype(bf16)
     total[...] += dot(basis[0], scaled, ((1,), (1,)))
@@ -310,7 +318,7 @@
                 out_specs=pl.BlockSpec((wide, tokens), lambda i, p: (at + i, 0)),
             ),
             input_output_aliases={4: 0} if before else {},
-            compiler_params=PARAMS,
+            compiler_params=EARLY,
             name="rotate_kernel",
         )(place, cotangents, marks, basis_out, *before)
 
@@ -347,6 +355,7 @@
             pltpu.VMEM((8 * rows, width), f32),
             pltpu.VMEM((width, cols), f32),
         ],
+        params=EARLY,
     )
     cov_got_up, cov_got_down = send_z(cov_up, cov_down)
 
@@ -366,9 +375,10 @@
         (eigen, eigen_got, activations, act_got),
         scratch=[pltpu.VMEM((width, width), f32)],
     )
+    scale_row = after(scale_out, own_b).reshape(1, width)
     (basis_rows,) = placed(
         rows_kernel,
-        after(place, own_b, cov_got_up, cov_got_down),
+        after(place, own_b, cov_got_up, cov_got_down, scale_row),
         (1,),
         [whole(basis_four.shape)] * 2,
         [shape_of(4, 2, 2 * rows, 2 * cols)],
@@ -394,7 +404,7 @@
 
     by_y = pair_y(squares_in, lax.ppermute(squares_in, "factor", swap_y(1)), y % 2 == 0)
     by_y = pair_y(by_y, lax.ppermute(by_y, "factor", swap_y(2)), y < 2)
-    small = jnp.concatenate([squares_out[:4], by_y, squares_out[4:]], 0)
+    small = jnp.concatenate([squares_out, by_y], 0)
     give, up, down = lax.optimization_barrier((give, up, down, basis_x_lo))[:3]
     got_a = lax.ppermute(give, "dp", XLO)
     got_up, got_down = send_z(up, down)
@@ -416,16 +426,11 @@
     small = after(small, second_up)
     small = small + lax.ppermute(small, "dp", XLO)
     small = added(small, *[lax.ppermute(small, "dp", to_z(i)) for i in (1, 3, 2)])
-    scale_own = lax.dynamic_index_in_dim(scale_in, core, 0, keepdims=False).reshape(2, 4, cols)
-    scale_own = jnp.where(fac // 4 == 0, scale_own, scale_own[::-1])
-    scale_own = jnp.concatenate([scale_own[0], scale_own[1]], 1)
-    scale_own, scale_chip = lax.optimization_barrier((scale_own, scale_out.reshape(4, wide), second_up))[:2]
-
     near = pl.BlockSpec((1, chunk, width - cut), lambda i, p: (1, 0, 0))
     third_in = (second_got_up, second_got_down, own_b, a_first_1, a_second_3, own_a)
     third_up, third_down, b_give, b_keep, a_keep = placed(
         third_kernel,
-        after(place, small, scale_own, scale_chip),
+        after(place, small),
         (1,),
         [near, near] + [whole(t.shape) for t in third_in],
         [
@@ -440,7 +445,7 @@
     b_got = lax.ppermute(b_give, "dp", XLO)
     a_via_up, a_via_down = send_z(third_up, third_down)
 
-    healthy_rows = f32(tokens * lax.axis_size("dp")) - small[8, 0]
+    healthy_rows = f32(tokens * lax.axis_size("dp")) - small[4, 0]
 
     cov_next = forward_z(cov_got_up, cov_got_down, cov_rest[2], cov_rest[3])
     cov_next = lax.optimization_barrier((*cov_next, b_got, a_via_up, a_via_down, healthy_rows))[:2]
@@ -453,13 +458,14 @@
         (4,),
         [whole(t.shape) for t in turn_in]
         + [pl.BlockSpec((1, width, 2 * cols), lambda i, p: (i, 0, 0))]
-        + [whole((9, wide)), whole((4, wide)), whole((4, wide))],
+        + [whole((9, wide)), whole((2, width)), whole((1, width))],
         [shape_of(16, rows * 3 // 2, chunk * 2 // 3)],
-        (*turn_in, basis_all, small, scale_own, scale_chip),
+        (*turn_in, basis_all, small, scale_in, scale_row),
         scratch=[
             pltpu.VMEM((chunk, width), bf16),
             pltpu.VMEM((width, chunk), f32),
             pltpu.VMEM((chunk, 128), f32),
+            pltpu.VMEM((4, wide), f32),
         ],
         name="turn_kernel",
     )

time: 173 us -> 168 us (0.971)
  waiting for transfers between devices: 14.2 us -> 20.3 us
  other arithmetic: 16.9 us -> 11.4 us
  local copies, waits for them, and re-layouts: 14.4 us -> 9.24 us
    ppermute x3, waiting for transfers between devices: 2.58 us -> 5.22 us  [per_device(): lax.ppermute(small, 'dp', to_z(i))]
    slice x3 -> x1, local copies, waits for them, and re-layouts: 3.78 us -> 1.19 us  [per_device(): healthy_rows = f32(tokens * lax.axis_size('dp')) - small[4, 0]]
    unnamed x14 -> x22, local copies, waits for them, and re-layouts: 4.6 us -> 3.39 us
  transfers between devices with their start and end apart: 32 -> 32, of which waited for: 9 -> 11; matrix products, arithmetic and copies ran while one was open for 14% -> 8% of each run, Pallas kernels for 31% -> 32%
where the time goes in v4:
time: 168 us; the launch traced here: 167 us
  Pallas kernels  62.2 us (37%)
  starting transfers between devices  49.2 us (29%)
  waiting for transfers between devices  20.3 us (12%)
  between operations  15 us (9%)
  other arithmetic  11.4 us (7%)
  local copies, waits for them, and re-layouts  9.24 us (6%)
    pallas_call x6, Pallas kernels, placed(): pl.pallas_call(kernel, out_shape=out_shapes, grid_spec=pltpu.PrefetchScal...  42.3 us
    all_to_all x1, starting transfers between devices, per_device(): spread = lax.all_to_all(turned, 'dp', split_axis=0, concat_axis=0)  12.6 us
    ppermute x10, starting transfers between devices, send_z(): return (lax.ppermute(up, 'dp', UP), lax.ppermute(down, 'dp', DOWN))  12.5 us
    pallas_call x2, Pallas kernels, rotate(): pl.pallas_call(rotate_kernel, out_shape=shape_of(width, tokens), grid_spe...  10.9 us
    pallas_call x1, Pallas kernels, per_device(): pl.pallas_call(last_kernel, out_shape=shape_of(2, rows, width), grid=(4,)...  5.7 us
    ppermute x10, waiting for transfers between devices, send_z(): return (lax.ppermute(up, 'dp', UP), lax.ppermute(down, 'dp', DOWN))  5.55 us
    ppermute x3, waiting for transfers between devices, per_device(): lax.ppermute(small, 'dp', to_z(i))  5.22 us
    ppermute x3, starting transfers between devices, per_device(): basis_z = [lax.ppermute(basis_pair, 'dp', to_z(4 - s)) for s in (1, 2, 3)]  5.13 us
  transfers between devices with their start and end apart: 32, of which 11 were waited for; matrix products, arithmetic and copies ran while one was open for 8% of the time, Pallas kernels for 32%

profile of v4, /device:TPU:1, one launch (start us, length us, event | category | flops | bytes accessed | tf_op | source)
XLA Modules:
  0.0 167.3 jit_solution(18264310701649789231)
XLA Ops:
  7.3 2.8 %constant_dynamic-slice_fusion.4 = bf16[512,1536]{1,0:T(8,128)(2,1)} fusion(bf16[512,3072]{1,0:T(8,128)(2,1)} %act_0.5, s32[]{:T(128)S(6)} %select_n.87), kind=kLoop, calls=%fused_computation.32 | loop fusion | bytes 3145732 | tf_op jit(solution)/shard_map/dynamic_slice | solution.py:302
  10.0 1.4 collective-permute-start
  13.0 5.5 %rotate_kernel.2.refs_0_ = bf16[1536,512]{1,0:T(8,128)(2,1)} custom-call(s32[4]{0:T(128)} %pad_add_fusion.place, bf16[512,1536]{1,0:T(8,128)(2,1)} %cot_0.1, s32[1,512]{1,0:T(1,128)} %bitcast.51, bf16[1536,1536]{1,0:T(8,128)(2,1)} %basis_out.1), custom_call_target="tpu_custom_call" | custom-call | tf_op jit(solution)/shard_map/rotate_kernel/pallas_call | solution.py:306
  18.5 2.9 %collective-permute-start.3 = (bf16[192,192]{1,0:T(8,128)(2,1)S(1)}, bf16[192,192]{1,0:T(8,128)(2,1)S(1)}, u32[]{:S(2)}, u32[]{:S(2)}) collective-permute-start(bf16[192,192]{1,0:T(8,128)(2,1)S(1)} %maximum_select_fusion.1), channel_id=1, source_target_pairs={{0,4},{1,5},{2,6},{3,7},{4,0},{5,1},{6,2},{7,3},{8,12},{9,13},{10,... | collective-permute-start | bytes 221192 | tf_op jit(solution)/shard_map/ppermute | solution.py:332
  21.7 0.8 collective-permute-done.1.marks_1
  22.6 5.4 %rotate_kernel.3.eigen_0 = bf16[1536,512]{1,0:T(8,128)(2,1)} custom-call(s32[4]{0:T(128)} %pad_add_fusion.place, bf16[512,1536]{1,0:T(8,128)(2,1)} %cot_0.1, s32[1,512]{1,0:T(1,128)} %bitcast.52, bf16[1536,1536]{1,0:T(8,128)(2,1)} %basis_out.1, bf16[1536,512]{1,0:T(8,128)(2,1)} %rotate_kernel.2.refs_0_), custom_call_target="tpu_custom_call", output_to_operand_aliasing={{}: (4, {})} | custom-call | tf_op jit(solution)/shard_map/rotate_kernel/pallas_call | solution.py:306
  28.4 1.7 %collective-permute-start.7 = (bf16[192,384]{1,0:T(8,128)(2,1)S(1)}, bf16[192,384]{1,0:T(8,128)(2,1)S(1)}, u32[]{:S(2)}, u32[]{:S(2)}) collective-permute-start(bf16[192,384]{1,0:T(8,128)(2,1)S(1)} %pad_maximum_fusion.1), channel_id=1, source_target_pairs={{0,32},{8,40},{16,48},{24,56},{32,64},{40,72},{48,80},{56,88},{64,... | collective-permute-start | bytes 442376 | tf_op jit(solution)/shard_map/ppermute | solution.py:336
  30.2 2.2 %collective-permute-start.5 = (bf16[192,384]{1,0:T(8,128)(2,1)S(1)}, bf16[192,384]{1,0:T(8,128)(2,1)S(1)}, u32[]{:S(2)}, u32[]{:S(2)}) collective-permute-start(bf16[192,384]{1,0:T(8,128)(2,1)S(1)} %pad_maximum_fusion.1), channel_id=1, source_target_pairs={{0,96},{8,104},{16,112},{24,120},{32,0},{40,8},{48,16},{56,24},{64... | collective-permute-start | bytes 442376 | tf_op jit(solution)/shard_map/ppermute | solution.py:336
  32.4 1.2 collective-permute-start.6
  33.6 9.7 %cov_kernel.1 = (bf16[2,96,1920]{2,1,0:T(8,128)(2,1)}, bf16[2,96,1920]{2,1,0:T(8,128)(2,1)}, bf16[4,96,1920]{2,1,0:T(8,128)(2,1)}) custom-call(s32[4]{0:T(128)} %pad_add_fusion.place, bf16[512,1536]{1,0:T(8,128)(2,1)} %cot_0.1, bf16[512,1536]{1,0:T(8,128)(2,1)} %collective-permute-done.4.cot_1, s32[1,512]{1,0:T(1,128)} %bitcast.53, s32[1,512]{1,0:T(1,128)} %copy-done.7, ...), custom_call_target="tpu_custom_call" | custom-call | tf_op jit(solution)/shard_map/cov_kernel/pallas_call | solution.py:72
  43.3 1.3 collective-permute-start.10
  44.8 0.9 pad_maximum_fusion.own
  46.0 10.8 %grad_kernel.1 = (bf16[4,192,512]{2,1,0:T(8,128)(2,1)}, bf16[4,192,512]{2,1,0:T(8,128)(2,1)}, bf16[2,192,1024]{2,1,0:T(8,128)(2,1)}, bf16[2,192,1024]{2,1,0:T(8,...) custom-call(s32[4]{0:T(128)} %pad_add_fusion.place, ...), custom_call_target="tpu_custom_call" | custom-call | tf_op jit(solution)/shard_map/grad_kernel/pallas_call | solution.py:72
  56.8 1.3 reshape.36.scale_out
  58.1 2.4 %collective-permute-done.10 = bf16[2,96,1920]{2,1,0:T(8,128)(2,1)} collective-permute-done((bf16[2,96,1920]{2,1,0:T(8,128)(2,1)}, bf16[2,96,1920]{2,1,0:T(8,128)(2,1)}, u32[]{:S(2)}, u32[]{:S(2)}) %collective-permute-start.10) | collective-permute-done | bytes 737312 | tf_op jit(solution)/shard_map/ppermute | solution.py:56
  60.6 2.6 %collective-permute-done.9 = bf16[2,96,1920]{2,1,0:T(8,128)(2,1)} collective-permute-done((bf16[2,96,1920]{2,1,0:T(8,128)(2,1)}, bf16[2,96,1920]{2,1,0:T(8,128)(2,1)}, u32[]{:S(2)}, u32[]{:S(2)}) %collective-permute-start.9) | collective-permute-done | bytes 737312 | tf_op jit(solution)/shard_map/ppermute | solution.py:56
  63.1 3.1 %rows_kernel.1 = bf16[4,2,192,384]{3,2,1,0:T(8,128)(2,1)} custom-call(s32[4]{0:T(128)} %pad_add_fusion.place, bf16[4,192,384]{2,1,0:T(8,128)(2,1)} %pad_maximum_fusion.own, bf16[4,192,384]{2,1,0:T(8,128)(2,1)} %collective-permute-done.11.got), custom_call_target="tpu_custom_call" | custom-call | tf_op jit(solution)/shard_map/rows_kernel/pallas_call | solution.py:72
  66.6 2.7 %collective-permute-start.16 = (bf16[2,192,1024]{2,1,0:T(8,128)(2,1)}, bf16[2,192,1024]{2,1,0:T(8,128)(2,1)}, u32[]{:S(2)}, u32[]{:S(2)}) collective-permute-start(bf16[2,192,1024]{2,1,0:T(8,128)(2,1)} %get-tuple-element.66), channel_id=1, source_target_pairs={{0,96},{8,104},{16,112},{24,120},{32,0},{40,8},{48,16},{56,24},{64... | collective-permute-start | bytes 2359304 | tf_op jit(solution)/shard_map/ppermute | solution.py:56
  69.3 6.5 %squares_kernel.1 = (f32[1,384]{1,0:T(1,128)}, f32[5,384]{1,0:T(8,128)}) custom-call(s32[4]{0:T(128)} %pad_add_fusion.place, bf16[512,3072]{1,0:T(8,128)(2,1)} %act_0.5, bf16[512,1536]{1,0:T(8,128)(2,1)} %copy-done, s32[1,512]{1,0:T(1,128)} %bitcast.54, s32[1,512]{1,0:T(1,128)} %copy-done.7, bf16[1536,384]{1,0:T(8,128)(2,1)} %bitcast.42, ...), custom_call_target="tpu_custom_call" | custom-call | tf_op jit(solution)/shard_map/squares_kernel/pallas_call | solution.py:72
  75.8 1.3 collective-permute-start.12
  77.1 1.7 %collective-permute-done.12 = f32[1,384]{1,0:T(1,128)S(1)} collective-permute-done((f32[1,384]{1,0:T(1,128)}, f32[1,384]{1,0:T(1,128)S(1)}, u32[]{:S(2)}, u32[]{:S(2)}) %collective-permute-start.12) | collective-permute-done | bytes 1568 | tf_op jit(solution)/shard_map/ppermute | solution.py:405
  79.7 3.0 %collective-permute-start.13 = (f32[2,384]{1,0:T(2,128)S(1)}, f32[2,384]{1,0:T(2,128)S(1)}, u32[]{:S(2)}, u32[]{:S(2)}) collective-permute-start(f32[2,384]{1,0:T(2,128)S(1)} %maximum_select_fusion.3), channel_id=1, source_target_pairs={{0,2},{1,3},{2,0},{3,1},{4,6},{5,7},{6,4},{7,5},{8,10},{9,11},{10,... | collective-permute-start | bytes 9224 | tf_op jit(solution)/shard_map/ppermute | solution.py:406
  82.7 1.1 collective-permute-done.13
  84.9 3.4 %second_kernel.1 = (bf16[192,1536]{1,0:T(8,128)(2,1)}, bf16[192,1536]{1,0:T(8,128)(2,1)}, bf16[96,512]{1,0:T(8,128)(2,1)}, bf16[96,512]{1,0:T(8,128)(2,1)}, bf16[2,96,512]{2,1,0:T(8,128)(2,1)}) custom-call(bf16[4,192,512]{2,1,0:T(8,128)(2,1)} %get-tuple-element.60.keep, bf16[4,192,512]{2,1,0:T(8,128)(2,1)} %collective-permute-done.14.got_a, ...), custom_call_target="tpu_custom_call" | custom-call | tf_op jit(solution)/shard_map/second_kernel/pallas_call | solution.py:412
  88.3 2.7 %collective-permute-start.22 = (bf16[192,1536]{1,0:T(8,128)(2,1)}, bf16[192,1536]{1,0:T(8,128)(2,1)}, u32[]{:S(2)}, u32[]{:S(2)}) collective-permute-start(bf16[192,1536]{1,0:T(8,128)(2,1)} %get-tuple-element.72), channel_id=1, source_target_pairs={{0,96},{8,104},{16,112},{24,120},{32,0},{40,8},{48,16},{56,24},{64... | collective-permute-start | bytes 1769480 | tf_op jit(solution)/shard_map/ppermute | solution.py:56
  91.7 1.2 collective-permute-start.17
  92.9 1.9 %collective-permute-done.17 = f32[9,384]{1,0:T(8,128)S(1)} collective-permute-done((f32[9,384]{1,0:T(8,128)S(1)}, f32[9,384]{1,0:T(8,128)S(1)}, u32[]{:S(2)}, u32[]{:S(2)}) %collective-permute-start.17) | collective-permute-done | bytes 13856 | tf_op jit(solution)/shard_map/ppermute | solution.py:427
  94.8 2.7 %collective-permute-start.19 = (f32[9,384]{1,0:T(8,128)S(1)}, f32[9,384]{1,0:T(8,128)S(1)}, u32[]{:S(2)}, u32[]{:S(2)}) collective-permute-start(f32[9,384]{1,0:T(8,128)S(1)} %add.83), channel_id=1, source_target_pairs={{0,96},{8,104},{16,112},{24,120},{32,0},{40,8},{48,16},{56,24},{64... | collective-permute-start | bytes 41480 | tf_op jit(solution)/shard_map/ppermute | solution.py:428
  97.5 2.7 %collective-permute-done.18 = f32[9,384]{1,0:T(8,128)S(1)} collective-permute-done((f32[9,384]{1,0:T(8,128)S(1)}, f32[9,384]{1,0:T(8,128)S(1)}, u32[]{:S(2)}, u32[]{:S(2)}) %collective-permute-start.18) | collective-permute-done | bytes 13856 | tf_op jit(solution)/shard_map/ppermute | solution.py:428
  100.2 2.5 %collective-permute-done.20 = f32[9,384]{1,0:T(8,128)S(1)} collective-permute-done((f32[9,384]{1,0:T(8,128)S(1)}, f32[9,384]{1,0:T(8,128)S(1)}, u32[]{:S(2)}, u32[]{:S(2)}) %collective-permute-start.20) | collective-permute-done | bytes 13856 | tf_op jit(solution)/shard_map/ppermute | solution.py:428
  103.4 4.0 %third_kernel.1 = (bf16[96,512]{1,0:T(8,128)(2,1)}, bf16[96,512]{1,0:T(8,128)(2,1)}, bf16[192,1024]{1,0:T(8,128)(2,1)}, f32[192,1024]{1,0:T(8,128)}, f32[2,96,512]{2,1,0:T(8,128)}) custom-call(s32[4]{0:T(128)} %pad_add_fusion.place, bf16[2,192,1024]{2,1,0:T(8,128)(2,1)} %collective-permute-done.15.got_up, ...), custom_call_target="tpu_custom_call" | custom-call | tf_op jit(solution)/shard_map/third_kernel/pallas_call | solution.py:72
  107.3 1.1 collective-permute-start.25
  108.5 0.9 collective-permute-start.23
  109.4 1.8 %collective-permute-start.24 = (bf16[96,512]{1,0:T(8,128)(2,1)}, bf16[96,512]{1,0:T(8,128)(2,1)}, u32[]{:S(2)}, u32[]{:S(2)}) collective-permute-start(bf16[96,512]{1,0:T(8,128)(2,1)} %get-tuple-element.78), channel_id=1, source_target_pairs={{0,96},{8,104},{16,112},{24,120},{32,0},{40,8},{48,16},{56,24},{64... | collective-permute-start | bytes 294920 | tf_op jit(solution)/shard_map/ppermute | solution.py:56
  111.1 2.4 %fusion.3 = (bf16[96,1920]{1,0:T(8,128)(2,1)}, bf16[96,1920]{1,0:T(8,128)(2,1)}) fusion(bf16[2,96,1920]{2,1,0:T(8,128)(2,1)} %collective-permute-done.10, bf16[4,96,1920]{2,1,0:T(8,128)(2,1)} %get-tuple-element.82, bf16[2,96,1920]{2,1,0:T(8,128)(2,1)} %collective-permute-done.9), kind=kLoop, calls=%fused_computation.11 | loop fusion | flops 1474560 | bytes 2211840 | tf_op jit(solution)/shard_map/convert_element_type | solution.py:60
  113.6 1.2 slice.47
  115.7 2.7 %collective-permute-start.27 = (bf16[96,1920]{1,0:T(8,128)(2,1)}, bf16[96,1920]{1,0:T(8,128)(2,1)}, u32[]{:S(2)}, u32[]{:S(2)}) collective-permute-start(bf16[96,1920]{1,0:T(8,128)(2,1)} %get-tuple-element.84), channel_id=1, source_target_pairs={{0,96},{8,104},{16,112},{24,120},{32,0},{40,8},{48,16},{56,24},{64... | collective-permute-start | bytes 1105928 | tf_op jit(solution)/shard_map/ppermute | solution.py:56
  118.4 8.2 %turn_kernel.1 = bf16[16,144,128]{2,1,0:T(8,128)(2,1)} custom-call(s32[4]{0:T(128)} %pad_add_fusion.place, f32[2,96,512]{2,1,0:T(8,128)} %get-tuple-element.76.keep_a, bf16[96,512]{1,0:T(8,128)(2,1)} %collective-permute-done.23.via_up, bf16[96,512]{1,0:T(8,128)(2,1)} %collective-permute-done.24.via_down, f32[192,1024]{1,0:T(8,128)} %get-tuple-element.79.keep_b, ...), custom_call_target="tpu_custom_call" | custom-call | tf_op jit(solution)/shard_map/turn_kernel/pallas_call | solution.py:72
  126.6 1.9 %select_convert_fusion = bf16[96,1920]{1,0:T(8,128)(2,1)S(1)} fusion(bf16[96,1920]{1,0:T(8,128)(2,1)} %collective-permute-done.26, bf16[96,1920]{1,0:T(8,128)(2,1)} %collective-permute-done.27, pred[]{:T(512)S(6)} %eq.18, bf16[2,96,1920]{2,1,0:T(8,128)(2,1)} %collective-permute-done.9, bf16[2,96,1920]{2,1,0:T(8,128)(2,1)} %collective-permute-done.10, ...), kind=kLoop, calls=%fused_computation.3 | loop fusion | flops 2211840 | bytes 2580481 | tf_op jit(solution)/shard_map/convert_element_type | solution.py:475
  128.9 12.6 %all-to-all-start = ((bf16[16,144,128]{2,1,0:T(8,128)(2,1)}), bf16[16,144,128]{2,1,0:T(8,128)(2,1)}, u32[]{:S(2)}, u32[]{:S(2)}) async-start(bf16[16,144,128]{2,1,0:T(8,128)(2,1)} %turn_kernel.1), calls=%async_computation | async-start | bytes 1179648 | tf_op jit(solution)/shard_map/all_to_all | solution.py:484
  141.5 1.7 %convert_add_fusion = f32[96,1920]{1,0:T(8,128)S(1)} fusion(bf16[96,1920]{1,0:T(8,128)(2,1)S(1)} %collective-permute-done.28, bf16[96,1920]{1,0:T(8,128)(2,1)} %collective-permute-done.26, bf16[96,1920]{1,0:T(8,128)(2,1)} %collective-permute-done.27, pred[]{:T(512)S(6)} %eq.18, bf16[2,96,1920]{2,1,0:T(8,128)(2,1)} %collective-permute-done.9, ...), kind=kLoop, calls=%fused_computation.2 | loop fusion | flops 2396160 | bytes 3317761 | tf_op jit(solution)/shard_map/add | solution.py:47
  143.3 0.9 fusion.1
  144.5 2.9 %collective-permute-start.29 = (bf16[96,192]{1,0:T(8,128)(2,1)S(1)}, bf16[96,192]{1,0:T(8,128)(2,1)S(1)}, u32[]{:S(2)}, u32[]{:S(2)}) collective-permute-start(bf16[96,192]{1,0:T(8,128)(2,1)S(1)} %bitcast.50), channel_id=1, source_target_pairs={{0,8},{8,0},{16,24},{24,16},{32,40},{40,32},{48,56},{56,48},{64,72... | collective-permute-start | bytes 110600 | tf_op jit(solution)/shard_map/ppermute | solution.py:482
  147.5 0.8 collective-permute-done.29
  148.3 0.8 copy.28
  149.2 3.1 %all-to-all-done.spread = bf16[16,144,128]{2,1,0:T(8,128)(2,1)} async-done(((bf16[16,144,128]{2,1,0:T(8,128)(2,1)}), bf16[16,144,128]{2,1,0:T(8,128)(2,1)}, u32[]{:S(2)}, u32[]{:S(2)}) %all-to-all-start) | async-done | bytes 589856 | tf_op jit(solution)/shard_map/all_to_all | solution.py:484
  152.2 5.7 %last_kernel.1 = bf16[2,96,1536]{2,1,0:T(8,128)(2,1)} custom-call(bf16[16,144,128]{2,1,0:T(8,128)(2,1)} %all-to-all-done.spread, bf16[1536,1536]{1,0:T(8,128)(2,1)} %basis_out.1), custom_call_target="tpu_custom_call" | custom-call | tf_op jit(solution)/shard_map/last_kernel/pallas_call | solution.py:485
  157.9 2.5 %copy.27 = bf16[96,2,1536]{2,1,0:T(2,128)(2,1)} copy(bf16[96,2,1536]{2,0,1:T(8,128)(2,1)} %bitcast.43) | data formatting | bytes 1179648
  (72 shorter events, 7.7 us)
Async XLA Ops:
  7.2 111.2 %all-gather.2.cloned.1.call-start = ((), (), s32[]{:S(2)}) async-start(), calls=%async_computation.1 | async-start | bytes 5898240 | tf_op jit(solution)/shard_map/all_gather | solution.py:388
  7.2 4.2 %copy-start.1 = (bf16[512,1536]{1,0:T(8,128)(2,1)S(1)}, bf16[512,1536]{1,0:T(8,128)(2,1)}, u32[]{:S(2)}) copy-start(bf16[512,1536]{1,0:T(8,128)(2,1)} %cot_0.1) | copy-start | bytes 4718596
  7.2 4.2 %copy-start.4 = (bf16[96,2,192]{2,1,0:T(2,128)(2,1)S(1)}, bf16[96,2,192]{2,1,0:T(2,128)(2,1)}, u32[]{:S(2)}) copy-start(bf16[96,2,192]{2,1,0:T(2,128)(2,1)} %param.11) | copy-start | bytes 221188
  10.0 22.3 %collective-permute-start = (bf16[512,1536]{1,0:T(8,128)(2,1)}, bf16[512,1536]{1,0:T(8,128)(2,1)S(1)}, u32[]{:S(2)}, u32[]{:S(2)}) collective-permute-start(bf16[512,1536]{1,0:T(8,128)(2,1)} %constant_dynamic-slice_fusion.4), channel_id=1, source_target_pairs={{0,8},{8,0},{16,24},{24,16},{32,40},{40,32},{48,56},{56,48},{64,72... | collective-permute-start | bytes 4718600 | tf_op jit(solution)/shard_map/ppermute | solution.py:303
  11.5 22.1 %collective-permute-start.4 = (bf16[512,1536]{1,0:T(8,128)(2,1)S(1)}, bf16[512,1536]{1,0:T(8,128)(2,1)}, u32[]{:S(2)}, u32[]{:S(2)}) collective-permute-start(bf16[512,1536]{1,0:T(8,128)(2,1)S(1)} %copy-done.1), channel_id=1, source_target_pairs={{0,8},{8,0},{16,24},{24,16},{32,40},{40,32},{48,56},{56,48},{64,72... | collective-permute-start | bytes 4718600 | tf_op jit(solution)/shard_map/ppermute | solution.py:301
  11.7 6.8 %collective-permute-start.2 = (bf16[96,192]{1,0:T(8,128)(2,1)S(1)}, bf16[96,192]{1,0:T(8,128)(2,1)S(1)}, u32[]{:S(2)}, u32[]{:S(2)}) collective-permute-start(bf16[96,192]{1,0:T(8,128)(2,1)S(1)} %bitcast.49), channel_id=1, source_target_pairs={{0,8},{8,0},{16,24},{24,16},{32,40},{40,32},{48,56},{56,48},{64,72... | collective-permute-start | bytes 110600 | tf_op jit(solution)/shard_map/ppermute | solution.py:298
  12.9 8.5 %copy-start.6 = (s32[512]{0:T(512)S(1)}, s32[512]{0:T(512)}, u32[]{:S(2)}) copy-start(s32[512]{0:T(512)} %param.17) | copy-start | bytes 6148
  18.5 9.4 %collective-permute-start.3 = (bf16[192,192]{1,0:T(8,128)(2,1)S(1)}, bf16[192,192]{1,0:T(8,128)(2,1)S(1)}, u32[]{:S(2)}, u32[]{:S(2)}) collective-permute-start(bf16[192,192]{1,0:T(8,128)(2,1)S(1)} %maximum_select_fusion.1), channel_id=1, source_target_pairs={{0,4},{1,5},{2,6},{3,7},{4,0},{5,1},{6,2},{7,3},{8,12},{9,13},{10,... | collective-permute-start | bytes 221192 | tf_op jit(solution)/shard_map/ppermute | solution.py:332
  21.4 1.2 collective-permute-start.1
  22.6 5.4 %copy-start.7 = (s32[1,512]{1,0:T(1,128)}, s32[1,512]{1,0:T(1,128)S(1)}, u32[]{:S(2)}) copy-start(s32[1,512]{1,0:T(1,128)S(1)} %collective-permute-done.1.marks_1) | copy-start | bytes 6148
  27.9 18.1 %collective-permute-start.8 = (bf16[1536,512]{1,0:T(8,128)(2,1)}, bf16[1536,512]{1,0:T(8,128)(2,1)}, u32[]{:S(2)}, u32[]{:S(2)}) collective-permute-start(bf16[1536,512]{1,0:T(8,128)(2,1)} %rotate_kernel.3.eigen_0), channel_id=1, source_target_pairs={{0,8},{8,0},{16,24},{24,16},{32,40},{40,32},{48,56},{56,48},{64,72... | collective-permute-start | bytes 4718600 | tf_op jit(solution)/shard_map/ppermute | solution.py:334
  28.4 16.2 %collective-permute-start.7 = (bf16[192,384]{1,0:T(8,128)(2,1)S(1)}, bf16[192,384]{1,0:T(8,128)(2,1)S(1)}, u32[]{:S(2)}, u32[]{:S(2)}) collective-permute-start(bf16[192,384]{1,0:T(8,128)(2,1)S(1)} %pad_maximum_fusion.1), channel_id=1, source_target_pairs={{0,32},{8,40},{16,48},{24,56},{32,64},{40,72},{48,80},{56,88},{64,... | collective-permute-start | bytes 442376 | tf_op jit(solution)/shard_map/ppermute | solution.py:336
  30.2 14.6 %collective-permute-start.5 = (bf16[192,384]{1,0:T(8,128)(2,1)S(1)}, bf16[192,384]{1,0:T(8,128)(2,1)S(1)}, u32[]{:S(2)}, u32[]{:S(2)}) collective-permute-start(bf16[192,384]{1,0:T(8,128)(2,1)S(1)} %pad_maximum_fusion.1), channel_id=1, source_target_pairs={{0,96},{8,104},{16,112},{24,120},{32,0},{40,8},{48,16},{56,24},{64... | collective-permute-start | bytes 442376 | tf_op jit(solution)/shard_map/ppermute | solution.py:336
  32.4 1.2 copy-start
  32.4 12.4 %collective-permute-start.6 = (bf16[192,384]{1,0:T(8,128)(2,1)S(1)}, bf16[192,384]{1,0:T(8,128)(2,1)S(1)}, u32[]{:S(2)}, u32[]{:S(2)}) collective-permute-start(bf16[192,384]{1,0:T(8,128)(2,1)S(1)} %pad_maximum_fusion.1), channel_id=1, source_target_pairs={{0,64},{8,72},{16,80},{24,88},{32,96},{40,104},{48,112},{56,120},{... | collective-permute-start | bytes 442376 | tf_op jit(solution)/shard_map/ppermute | solution.py:336
  43.3 17.2 %collective-permute-start.10 = (bf16[2,96,1920]{2,1,0:T(8,128)(2,1)}, bf16[2,96,1920]{2,1,0:T(8,128)(2,1)}, u32[]{:S(2)}, u32[]{:S(2)}) collective-permute-start(bf16[2,96,1920]{2,1,0:T(8,128)(2,1)} %get-tuple-element.54), channel_id=1, source_target_pairs={{0,96},{8,104},{16,112},{24,120},{32,0},{40,8},{48,16},{56,24},{64... | collective-permute-start | bytes 2211848 | tf_op jit(solution)/shard_map/ppermute | solution.py:56
  44.7 18.5 %collective-permute-start.9 = (bf16[2,96,1920]{2,1,0:T(8,128)(2,1)}, bf16[2,96,1920]{2,1,0:T(8,128)(2,1)}, u32[]{:S(2)}, u32[]{:S(2)}) collective-permute-start(bf16[2,96,1920]{2,1,0:T(8,128)(2,1)} %get-tuple-element.49), channel_id=1, source_target_pairs={{0,32},{8,40},{16,48},{24,56},{32,64},{40,72},{48,80},{56,88},{64,... | collective-permute-start | bytes 2211848 | tf_op jit(solution)/shard_map/ppermute | solution.py:56
  45.7 17.4 %collective-permute-start.11 = (bf16[4,192,384]{2,1,0:T(8,128)(2,1)}, bf16[4,192,384]{2,1,0:T(8,128)(2,1)}, u32[]{:S(2)}, u32[]{:S(2)}) collective-permute-start(bf16[4,192,384]{2,1,0:T(8,128)(2,1)} %pad_maximum_fusion.own), channel_id=1, source_target_pairs={{0,16},{8,24},{16,0},{24,8},{32,48},{40,56},{48,32},{56,40},{64,80... | collective-permute-start | bytes 1769480 | tf_op jit(solution)/shard_map/ppermute | solution.py:363
  66.2 18.2 %collective-permute-start.14 = (bf16[4,192,512]{2,1,0:T(8,128)(2,1)}, bf16[4,192,512]{2,1,0:T(8,128)(2,1)}, u32[]{:S(2)}, u32[]{:S(2)}) collective-permute-start(bf16[4,192,512]{2,1,0:T(8,128)(2,1)} %get-tuple-element.64), channel_id=1, source_target_pairs={{0,16},{8,24},{16,0},{24,8},{32,48},{40,56},{48,32},{56,40},{64,80... | collective-permute-start | bytes 2359304 | tf_op jit(solution)/shard_map/ppermute | solution.py:409
  66.6 18.3 %collective-permute-start.15 = (bf16[2,192,1024]{2,1,0:T(8,128)(2,1)}, bf16[2,192,1024]{2,1,0:T(8,128)(2,1)}, u32[]{:S(2)}, u32[]{:S(2)}) collective-permute-start(bf16[2,192,1024]{2,1,0:T(8,128)(2,1)} %get-tuple-element.65), channel_id=1, source_target_pairs={{0,32},{8,40},{16,48},{24,56},{32,64},{40,72},{48,80},{56,88},{64,... | collective-permute-start | bytes 2359304 | tf_op jit(solution)/shard_map/ppermute | solution.py:56
  66.6 18.3 %collective-permute-start.16 = (bf16[2,192,1024]{2,1,0:T(8,128)(2,1)}, bf16[2,192,1024]{2,1,0:T(8,128)(2,1)}, u32[]{:S(2)}, u32[]{:S(2)}) collective-permute-start(bf16[2,192,1024]{2,1,0:T(8,128)(2,1)} %get-tuple-element.66), channel_id=1, source_target_pairs={{0,96},{8,104},{16,112},{24,120},{32,0},{40,8},{48,16},{56,24},{64... | collective-permute-start | bytes 2359304 | tf_op jit(solution)/shard_map/ppermute | solution.py:56
  75.8 3.0 %collective-permute-start.12 = (f32[1,384]{1,0:T(1,128)}, f32[1,384]{1,0:T(1,128)S(1)}, u32[]{:S(2)}, u32[]{:S(2)}) collective-permute-start(f32[1,384]{1,0:T(1,128)} %get-tuple-element.58), channel_id=1, source_target_pairs={{0,1},{1,0},{2,3},{3,2},{4,5},{5,4},{6,7},{7,6},{8,9},{9,8},{10,11... | collective-permute-start | bytes 4616 | tf_op jit(solution)/shard_map/ppermute | solution.py:405
  79.7 4.1 %collective-permute-start.13 = (f32[2,384]{1,0:T(2,128)S(1)}, f32[2,384]{1,0:T(2,128)S(1)}, u32[]{:S(2)}, u32[]{:S(2)}) collective-permute-start(f32[2,384]{1,0:T(2,128)S(1)} %maximum_select_fusion.3), channel_id=1, source_target_pairs={{0,2},{1,3},{2,0},{3,1},{4,6},{5,7},{6,4},{7,5},{8,10},{9,11},{10,... | collective-permute-start | bytes 9224 | tf_op jit(solution)/shard_map/ppermute | solution.py:406
  88.3 15.1 %collective-permute-start.21 = (bf16[192,1536]{1,0:T(8,128)(2,1)}, bf16[192,1536]{1,0:T(8,128)(2,1)}, u32[]{:S(2)}, u32[]{:S(2)}) collective-permute-start(bf16[192,1536]{1,0:T(8,128)(2,1)} %get-tuple-element.69), channel_id=1, source_target_pairs={{0,32},{8,40},{16,48},{24,56},{32,64},{40,72},{48,80},{56,88},{64,... | collective-permute-start | bytes 1769480 | tf_op jit(solution)/shard_map/ppermute | solution.py:56
  88.3 15.1 %collective-permute-start.22 = (bf16[192,1536]{1,0:T(8,128)(2,1)}, bf16[192,1536]{1,0:T(8,128)(2,1)}, u32[]{:S(2)}, u32[]{:S(2)}) collective-permute-start(bf16[192,1536]{1,0:T(8,128)(2,1)} %get-tuple-element.72), channel_id=1, source_target_pairs={{0,96},{8,104},{16,112},{24,120},{32,0},{40,8},{48,16},{56,24},{64... | collective-permute-start | bytes 1769480 | tf_op jit(solution)/shard_map/ppermute | solution.py:56
  91.7 3.1 %collective-permute-start.17 = (f32[9,384]{1,0:T(8,128)S(1)}, f32[9,384]{1,0:T(8,128)S(1)}, u32[]{:S(2)}, u32[]{:S(2)}) collective-permute-start(f32[9,384]{1,0:T(8,128)S(1)} %pad_maximum_fusion.2), channel_id=1, source_target_pairs={{0,16},{8,24},{16,0},{24,8},{32,48},{40,56},{48,32},{56,40},{64,80... | collective-permute-start | bytes 41480 | tf_op jit(solution)/shard_map/ppermute | solution.py:427
  94.8 5.4 %collective-permute-start.18 = (f32[9,384]{1,0:T(8,128)S(1)}, f32[9,384]{1,0:T(8,128)S(1)}, u32[]{:S(2)}, u32[]{:S(2)}) collective-permute-start(f32[9,384]{1,0:T(8,128)S(1)} %add.83), channel_id=1, source_target_pairs={{0,32},{8,40},{16,48},{24,56},{32,64},{40,72},{48,80},{56,88},{64,... | collective-permute-start | bytes 41480 | tf_op jit(solution)/shard_map/ppermute | solution.py:428
  94.8 5.4 %collective-permute-start.19 = (f32[9,384]{1,0:T(8,128)S(1)}, f32[9,384]{1,0:T(8,128)S(1)}, u32[]{:S(2)}, u32[]{:S(2)}) collective-permute-start(f32[9,384]{1,0:T(8,128)S(1)} %add.83), channel_id=1, source_target_pairs={{0,96},{8,104},{16,112},{24,120},{32,0},{40,8},{48,16},{56,24},{64... | collective-permute-start | bytes 41480 | tf_op jit(solution)/shard_map/ppermute | solution.py:428
  97.5 5.2 %collective-permute-start.20 = (f32[9,384]{1,0:T(8,128)S(1)}, f32[9,384]{1,0:T(8,128)S(1)}, u32[]{:S(2)}, u32[]{:S(2)}) collective-permute-start(f32[9,384]{1,0:T(8,128)S(1)} %add.83), channel_id=1, source_target_pairs={{0,64},{8,72},{16,80},{24,88},{32,96},{40,104},{48,112},{56,120},{... | collective-permute-start | bytes 41480 | tf_op jit(solution)/shard_map/ppermute | solution.py:428
  107.3 8.1 %collective-permute-start.25 = (bf16[192,1024]{1,0:T(8,128)(2,1)}, bf16[192,1024]{1,0:T(8,128)(2,1)}, u32[]{:S(2)}, u32[]{:S(2)}) collective-permute-start(bf16[192,1024]{1,0:T(8,128)(2,1)} %get-tuple-element.80), channel_id=1, source_target_pairs={{0,16},{8,24},{16,0},{24,8},{32,48},{40,56},{48,32},{56,40},{64,80... | collective-permute-start | bytes 1179656 | tf_op jit(solution)/shard_map/ppermute | solution.py:445
  108.5 6.9 %collective-permute-start.23 = (bf16[96,512]{1,0:T(8,128)(2,1)}, bf16[96,512]{1,0:T(8,128)(2,1)}, u32[]{:S(2)}, u32[]{:S(2)}) collective-permute-start(bf16[96,512]{1,0:T(8,128)(2,1)} %get-tuple-element.77), channel_id=1, source_target_pairs={{0,32},{8,40},{16,48},{24,56},{32,64},{40,72},{48,80},{56,88},{64,... | collective-permute-start | bytes 294920 | tf_op jit(solution)/shard_map/ppermute | solution.py:56
  109.4 6.0 %collective-permute-start.24 = (bf16[96,512]{1,0:T(8,128)(2,1)}, bf16[96,512]{1,0:T(8,128)(2,1)}, u32[]{:S(2)}, u32[]{:S(2)}) collective-permute-start(bf16[96,512]{1,0:T(8,128)(2,1)} %get-tuple-element.78), channel_id=1, source_target_pairs={{0,96},{8,104},{16,112},{24,120},{32,0},{40,8},{48,16},{56,24},{64... | collective-permute-start | bytes 294920 | tf_op jit(solution)/shard_map/ppermute | solution.py:56
  115.4 11.1 %collective-permute-start.26 = (bf16[96,1920]{1,0:T(8,128)(2,1)}, bf16[96,1920]{1,0:T(8,128)(2,1)}, u32[]{:S(2)}, u32[]{:S(2)}) collective-permute-start(bf16[96,1920]{1,0:T(8,128)(2,1)} %get-tuple-element.83), channel_id=1, source_target_pairs={{0,32},{8,40},{16,48},{24,56},{32,64},{40,72},{48,80},{56,88},{64,... | collective-permute-start | bytes 1105928 | tf_op jit(solution)/shard_map/ppermute | solution.py:56
  115.7 10.8 %collective-permute-start.27 = (bf16[96,1920]{1,0:T(8,128)(2,1)}, bf16[96,1920]{1,0:T(8,128)(2,1)}, u32[]{:S(2)}, u32[]{:S(2)}) collective-permute-start(bf16[96,1920]{1,0:T(8,128)(2,1)} %get-tuple-element.84), channel_id=1, source_target_pairs={{0,96},{8,104},{16,112},{24,120},{32,0},{40,8},{48,16},{56,24},{64... | collective-permute-start | bytes 1105928 | tf_op jit(solution)/shard_map/ppermute | solution.py:56
  126.6 14.9 %copy-start.2 = (bf16[4,96,1920]{2,1,0:T(8,128)(2,1)S(1)}, bf16[4,96,1920]{2,1,0:T(8,128)(2,1)}, u32[]{:S(2)}) copy-start(bf16[4,96,1920]{2,1,0:T(8,128)(2,1)} %get-tuple-element.82) | copy-start | bytes 4423684
  128.5 13.0 %collective-permute-start.28 = (bf16[96,1920]{1,0:T(8,128)(2,1)S(1)}, bf16[96,1920]{1,0:T(8,128)(2,1)S(1)}, u32[]{:S(2)}, u32[]{:S(2)}) collective-permute-start(bf16[96,1920]{1,0:T(8,128)(2,1)S(1)} %select_convert_fusion), channel_id=1, source_target_pairs={{0,16},{8,24},{16,0},{24,8},{32,48},{40,56},{48,32},{56,40},{64,80... | collective-permute-start | bytes 1105928 | tf_op jit(solution)/shard_map/ppermute | solution.py:477
  128.9 23.3 %all-to-all-start = ((bf16[16,144,128]{2,1,0:T(8,128)(2,1)}), bf16[16,144,128]{2,1,0:T(8,128)(2,1)}, u32[]{:S(2)}, u32[]{:S(2)}) async-start(bf16[16,144,128]{2,1,0:T(8,128)(2,1)} %turn_kernel.1), calls=%async_computation | async-start | bytes 1179648 | tf_op jit(solution)/shard_map/all_to_all | solution.py:484
  141.5 1.7 %copy-start.3 = (f32[96,1536]{1,0:T(8,128)S(1)}, f32[96,1536]{1,0:T(8,128)}, u32[]{:S(2)}) copy-start(f32[96,1536]{1,0:T(8,128)} %param.14) | copy-start | bytes 1769476
  143.2 5.0 %copy-start.5 = (f32[96,2,192]{2,1,0:T(2,128)S(1)}, f32[96,2,192]{2,1,0:T(2,128)}, u32[]{:S(2)}) copy-start(f32[96,2,192]{2,1,0:T(2,128)} %param.13) | copy-start | bytes 442372
  144.5 3.8 %collective-permute-start.29 = (bf16[96,192]{1,0:T(8,128)(2,1)S(1)}, bf16[96,192]{1,0:T(8,128)(2,1)S(1)}, u32[]{:S(2)}, u32[]{:S(2)}) collective-permute-start(bf16[96,192]{1,0:T(8,128)(2,1)S(1)} %bitcast.50), channel_id=1, source_target_pairs={{0,8},{8,0},{16,24},{24,16},{32,40},{40,32},{48,56},{56,48},{64,72... | collective-permute-start | bytes 110600 | tf_op jit(solution)/shard_map/ppermute | solution.py:482
Sparse Core Ops, SparseCore 0:
  66.3 51.0 all-gather.1

commit v5 on v4

--- a/solution.py
+++ b/solution.py
@@ -177,7 +177,7 @@
             out[index] = jnp.concatenate([cov_out[at : at + rows], *pair], 1).astype(bf16)
 
 
-def squares_kernel(place, act_0, act_1, marks_0, marks_1, basis, eigen_0, eigen_1, out_in, out_out):
+def squares_in_kernel(place, act_0, act_1, marks_0, marks_1, basis, out_in):
     total = 0.0
     for act, marks in ((act_0, marks_0), (act_1, marks_1)):
         tokens, columns = act.shape[0], basis.shape[1]
@@ -186,6 +186,9 @@
         mask = jnp.swapaxes(jnp.broadcast_to(healthy(marks), (lanes, tokens)), 0, 1)
         total += jnp.sum(square * jnp.concatenate([mask] * (columns // lanes), 1), axis=0, keepdims=True)
     out_in[...] = total
+
+
+def squares_out_kernel(place, marks_0, marks_1, eigen_0, eigen_1, out_out):
     width, tokens = eigen_0.shape
     lanes = min(128, tokens)
     count = jnp.sum(2.0 - healthy(marks_0) - healthy(marks_1), axis=1, keepdims=True)
@@ -376,9 +379,17 @@
         scratch=[pltpu.VMEM((width, width), f32)],
     )
     scale_row = after(scale_out, own_b).reshape(1, width)
+    (squares_out,) = placed(
+        squares_out_kernel,
+        after(place, own_b),
+        (1,),
+        [whole((1, tokens))] * 2 + [whole((width, tokens))] * 2,
+        [shape_of(5, wide, dtype=f32)],
+        (marks, marks_got, eigen, eigen_got),
+    )
     (basis_rows,) = placed(
         rows_kernel,
-        after(place, own_b, cov_got_up, cov_got_down, scale_row),
+        after(place, own_b, cov_got_up, cov_got_down, scale_row, squares_out),
         (1,),
         [whole(basis_four.shape)] * 2,
         [shape_of(4, 2, 2 * rows, 2 * cols)],
@@ -386,16 +397,15 @@
     )
     basis_rows = basis_rows.reshape(width, 2 * cols)
     basis_all = lax.all_gather(basis_rows, "factor", axis=0, axis_index_groups=SAME_XHI)
-    squares_in, squares_out = placed(
-        squares_kernel,
+    (squares_in,) = placed(
+        squares_in_kernel,
         place,
         (1,),
         [pl.BlockSpec((tokens, width), lambda i, p: (0, p[2])), whole((tokens, width))]
         + [whole((1, tokens))] * 2
-        + [whole((width, 2 * cols))]
-        + [whole((width, tokens))] * 2,
-        [shape_of(1, 2 * cols, dtype=f32), shape_of(5, wide, dtype=f32)],
-        (activations, act_got, marks, marks_got, basis_rows, eigen, eigen_got),
+        + [whole((width, 2 * cols))],
+        [shape_of(1, 2 * cols, dtype=f32)],
+        (activations, act_got, marks, marks_got, basis_rows),
     )
     y = fac % 4
 
@@ -404,7 +414,6 @@
 
     by_y = pair_y(squares_in, lax.ppermute(squares_in, "factor", swap_y(1)), y % 2 == 0)
     by_y = pair_y(by_y, lax.ppermute(by_y, "factor", swap_y(2)), y < 2)
-    small = jnp.concatenate([squares_out, by_y], 0)
     give, up, down = lax.optimization_barrier((give, up, down, basis_x_lo))[:3]
     got_a = lax.ppermute(give, "dp", XLO)
     got_up, got_down = send_z(up, down)
@@ -423,9 +432,11 @@
     )(after(keep, by_y), got_a, got_up, got_down, first_1, second_3)
     second_got_up, second_got_down = send_z(second_up, second_down)
 
-    small = after(small, second_up)
+    small = jnp.concatenate([squares_out, after(by_y, second_up, second_down)], 0)
     small = small + lax.ppermute(small, "dp", XLO)
     small = added(small, *[lax.ppermute(small, "dp", to_z(i)) for i in (1, 3, 2)])
+    cov_late = after(cov_rest, small)
+    cov_next = forward_z(cov_got_up, cov_got_down, cov_late[2], cov_late[3])
     near = pl.BlockSpec((1, chunk, width - cut), lambda i, p: (1, 0, 0))
     third_in = (second_got_up, second_got_down, own_b, a_first_1, a_second_3, own_a)
     third_up, third_down, b_give, b_keep, a_keep = placed(
@@ -447,7 +458,6 @@
 
     healthy_rows = f32(tokens * lax.axis_size("dp")) - small[4, 0]
 
-    cov_next = forward_z(cov_got_up, cov_got_down, cov_rest[2], cov_rest[3])
     cov_next = lax.optimization_barrier((*cov_next, b_got, a_via_up, a_via_down, healthy_rows))[:2]
     cov_via_up, cov_via_down = send_z(*cov_next)
 

time: 168 us -> 170 us (1.012)
  Pallas kernels: 62.2 us -> 64.9 us
    ppermute x10, waiting for transfers between devices: 5.55 us -> 2.11 us  [send_z(): return (lax.ppermute(up, 'dp', UP), lax.ppermute(down, 'dp', DOWN))]
    ppermute x1, waiting for transfers between devices: 0.01 us -> 2.82 us  [per_device(): b_got = lax.ppermute(b_give, 'dp', XLO)]
    pallas_call x6 -> x7, Pallas kernels: 42.3 us -> 45 us  [placed(): pl.pallas_call(kernel, out_shape=out_shapes, grid_spec=pltpu.PrefetchScal...]
    all_to_all x1, starting transfers between devices: 12.6 us -> 10.8 us  [per_device(): spread = lax.all_to_all(turned, 'dp', split_axis=0, concat_axis=0)]
  transfers between devices with their start and end apart: 32 -> 32, of which waited for: 11 -> 9; matrix products, arithmetic and copies ran while one was open for 8% -> 8% of each run, Pallas kernels for 32% -> 33%
where the time goes in v5:
time: 170 us; the launch traced here: 169 us
  Pallas kernels  64.9 us (38%)
  starting transfers between devices  47.6 us (28%)
  waiting for transfers between devices  20 us (12%)
  between operations  14.9 us (9%)
  other arithmetic  12.1 us (7%)
  local copies, waits for them, and re-layouts  9.66 us (6%)
    pallas_call x7, Pallas kernels, placed(): pl.pallas_call(kernel, out_shape=out_shapes, grid_spec=pltpu.PrefetchScal...  45 us
    ppermute x10, starting transfers between devices, send_z(): return (lax.ppermute(up, 'dp', UP), lax.ppermute(down, 'dp', DOWN))  13.4 us
    pallas_call x2, Pallas kernels, rotate(): pl.pallas_call(rotate_kernel, out_shape=shape_of(width, tokens), grid_spe...  10.8 us
    all_to_all x1, starting transfers between devices, per_device(): spread = lax.all_to_all(turned, 'dp', split_axis=0, concat_axis=0)  10.8 us
    ppermute x3, starting transfers between devices, per_device(): basis_z = [lax.ppermute(basis_pair, 'dp', to_z(4 - s)) for s in (1, 2, 3)]  5.74 us
    pallas_call x1, Pallas kernels, per_device(): pl.pallas_call(last_kernel, out_shape=shape_of(2, rows, width), grid=(4,)...  5.71 us
    ppermute x3, waiting for transfers between devices, per_device(): lax.ppermute(small, 'dp', to_z(i))  4.62 us
    unnamed x22, local copies, waits for them, and re-layouts  3.8 us
  transfers between devices with their start and end apart: 32, of which 9 were waited for; matrix products, arithmetic and copies ran while one was open for 8% of the time, Pallas kernels for 33%

profile of v5, /device:TPU:1, one launch (start us, length us, event | category | flops | bytes accessed | tf_op | source)
XLA Modules:
  0.0 169.2 jit_solution(12250667368020099255)
XLA Ops:
  7.3 2.8 %constant_dynamic-slice_fusion.3 = bf16[512,1536]{1,0:T(8,128)(2,1)} fusion(bf16[512,3072]{1,0:T(8,128)(2,1)} %act_0.5, s32[]{:T(128)S(6)} %select_n.89), kind=kLoop, calls=%fused_computation.31 | loop fusion | bytes 3145732 | tf_op jit(solution)/shard_map/dynamic_slice | solution.py:305
  10.1 1.4 collective-permute-start.4
  13.0 5.5 %rotate_kernel.2.refs_0_ = bf16[1536,512]{1,0:T(8,128)(2,1)} custom-call(s32[4]{0:T(128)} %pad_add_fusion.place, bf16[512,1536]{1,0:T(8,128)(2,1)} %cot_0.1, s32[1,512]{1,0:T(1,128)} %bitcast.49, bf16[1536,1536]{1,0:T(8,128)(2,1)} %basis_out.1), custom_call_target="tpu_custom_call" | custom-call | tf_op jit(solution)/shard_map/rotate_kernel/pallas_call | solution.py:309
  18.5 2.9 %collective-permute-start.2 = (bf16[192,192]{1,0:T(8,128)(2,1)S(1)}, bf16[192,192]{1,0:T(8,128)(2,1)S(1)}, u32[]{:S(2)}, u32[]{:S(2)}) collective-permute-start(bf16[192,192]{1,0:T(8,128)(2,1)S(1)} %maximum_select_fusion.1), channel_id=1, source_target_pairs={{0,4},{1,5},{2,6},{3,7},{4,0},{5,1},{6,2},{7,3},{8,12},{9,13},{10,... | collective-permute-start | bytes 221192 | tf_op jit(solution)/shard_map/ppermute | solution.py:335
  21.7 0.8 collective-permute-done.1.marks_1
  22.6 5.3 %rotate_kernel.3.eigen_0 = bf16[1536,512]{1,0:T(8,128)(2,1)} custom-call(s32[4]{0:T(128)} %pad_add_fusion.place, bf16[512,1536]{1,0:T(8,128)(2,1)} %cot_0.1, s32[1,512]{1,0:T(1,128)} %bitcast.50, bf16[1536,1536]{1,0:T(8,128)(2,1)} %basis_out.1, bf16[1536,512]{1,0:T(8,128)(2,1)} %rotate_kernel.2.refs_0_), custom_call_target="tpu_custom_call", output_to_operand_aliasing={{}: (4, {})} | custom-call | tf_op jit(solution)/shard_map/rotate_kernel/pallas_call | solution.py:309
  28.4 1.7 %collective-permute-start.7 = (bf16[192,384]{1,0:T(8,128)(2,1)S(1)}, bf16[192,384]{1,0:T(8,128)(2,1)S(1)}, u32[]{:S(2)}, u32[]{:S(2)}) collective-permute-start(bf16[192,384]{1,0:T(8,128)(2,1)S(1)} %pad_maximum_fusion.1), channel_id=1, source_target_pairs={{0,32},{8,40},{16,48},{24,56},{32,64},{40,72},{48,80},{56,88},{64,... | collective-permute-start | bytes 442376 | tf_op jit(solution)/shard_map/ppermute | solution.py:339
  30.1 3.3 %collective-permute-start.6 = (bf16[192,384]{1,0:T(8,128)(2,1)S(1)}, bf16[192,384]{1,0:T(8,128)(2,1)S(1)}, u32[]{:S(2)}, u32[]{:S(2)}) collective-permute-start(bf16[192,384]{1,0:T(8,128)(2,1)S(1)} %pad_maximum_fusion.1), channel_id=1, source_target_pairs={{0,64},{8,72},{16,80},{24,88},{32,96},{40,104},{48,112},{56,120},{... | collective-permute-start | bytes 442376 | tf_op jit(solution)/shard_map/ppermute | solution.py:339
  34.6 9.8 %cov_kernel.1 = (bf16[2,96,1920]{2,1,0:T(8,128)(2,1)}, bf16[2,96,1920]{2,1,0:T(8,128)(2,1)}, bf16[4,96,1920]{2,1,0:T(8,128)(2,1)}) custom-call(s32[4]{0:T(128)} %pad_add_fusion.place, bf16[512,1536]{1,0:T(8,128)(2,1)} %cot_0.1, bf16[512,1536]{1,0:T(8,128)(2,1)} %collective-permute-done.3.cot_1, s32[1,512]{1,0:T(1,128)} %bitcast.51, s32[1,512]{1,0:T(1,128)} %copy-done.7, ...), custom_call_target="tpu_custom_call" | custom-call | tf_op jit(solution)/shard_map/cov_kernel/pallas_call | solution.py:72
  44.7 2.4 %collective-permute-start.10 = (bf16[2,96,1920]{2,1,0:T(8,128)(2,1)}, bf16[2,96,1920]{2,1,0:T(8,128)(2,1)}, u32[]{:S(2)}, u32[]{:S(2)}) collective-permute-start(bf16[2,96,1920]{2,1,0:T(8,128)(2,1)} %get-tuple-element.55), channel_id=1, source_target_pairs={{0,96},{8,104},{16,112},{24,120},{32,0},{40,8},{48,16},{56,24},{64... | collective-permute-start | bytes 2211848 | tf_op jit(solution)/shard_map/ppermute | solution.py:56
  47.0 0.9 pad_maximum_fusion.own
  48.3 10.8 %grad_kernel.1 = (bf16[4,192,512]{2,1,0:T(8,128)(2,1)}, bf16[4,192,512]{2,1,0:T(8,128)(2,1)}, bf16[2,192,1024]{2,1,0:T(8,128)(2,1)}, bf16[2,192,1024]{2,1,0:T(8,...) custom-call(s32[4]{0:T(128)} %pad_add_fusion.place, ...), custom_call_target="tpu_custom_call" | custom-call | tf_op jit(solution)/shard_map/grad_kernel/pallas_call | solution.py:72
  59.1 1.3 reshape.36.scale_out
  60.4 3.9 %squares_out_kernel.1 = f32[5,384]{1,0:T(8,128)} custom-call(s32[4]{0:T(128)} %pad_add_fusion.place, s32[1,512]{1,0:T(1,128)} %bitcast.52, s32[1,512]{1,0:T(1,128)} %copy-done.7, bf16[1536,512]{1,0:T(8,128)(2,1)} %rotate_kernel.3.eigen_0, bf16[1536,512]{1,0:T(8,128)(2,1)} %collective-permute-done.8.eigen_1), custom_call_target="tpu_custom_call" | custom-call | tf_op jit(solution)/shard_map/squares_out_kernel/pallas_call | solution.py:72
  64.3 3.1 %rows_kernel.1 = bf16[4,2,192,384]{3,2,1,0:T(8,128)(2,1)} custom-call(s32[4]{0:T(128)} %pad_add_fusion.place, bf16[4,192,384]{2,1,0:T(8,128)(2,1)} %pad_maximum_fusion.own, bf16[4,192,384]{2,1,0:T(8,128)(2,1)} %collective-permute-done.11.got), custom_call_target="tpu_custom_call" | custom-call | tf_op jit(solution)/shard_map/rows_kernel/pallas_call | solution.py:72
  67.4 1.2 collective-permute-start.14
  68.7 2.7 %collective-permute-start.16 = (bf16[2,192,1024]{2,1,0:T(8,128)(2,1)}, bf16[2,192,1024]{2,1,0:T(8,128)(2,1)}, u32[]{:S(2)}, u32[]{:S(2)}) collective-permute-start(bf16[2,192,1024]{2,1,0:T(8,128)(2,1)} %get-tuple-element.65), channel_id=1, source_target_pairs={{0,96},{8,104},{16,112},{24,120},{32,0},{40,8},{48,16},{56,24},{64... | collective-permute-start | bytes 2359304 | tf_op jit(solution)/shard_map/ppermute | solution.py:56
  71.3 5.3 %squares_in_kernel.1 = f32[1,384]{1,0:T(1,128)} custom-call(s32[4]{0:T(128)} %pad_add_fusion.place, bf16[512,3072]{1,0:T(8,128)(2,1)} %act_0.5, bf16[512,1536]{1,0:T(8,128)(2,1)} %copy-done, s32[1,512]{1,0:T(1,128)} %bitcast.53, s32[1,512]{1,0:T(1,128)} %copy-done.7, bf16[1536,384]{1,0:T(8,128)(2,1)} %bitcast.42), custom_call_target="tpu_custom_call" | custom-call | tf_op jit(solution)/shard_map/squares_in_kernel/pallas_call | solution.py:72
  76.6 1.3 collective-permute-start.12
  77.9 1.8 %collective-permute-done.12 = f32[1,384]{1,0:T(1,128)S(1)} collective-permute-done((f32[1,384]{1,0:T(1,128)}, f32[1,384]{1,0:T(1,128)S(1)}, u32[]{:S(2)}, u32[]{:S(2)}) %collective-permute-start.12) | collective-permute-done | bytes 1568 | tf_op jit(solution)/shard_map/ppermute | solution.py:415
  79.7 0.8 maximum_select_fusion.3
  80.5 3.0 %collective-permute-start.13 = (f32[2,384]{1,0:T(2,128)S(1)}, f32[2,384]{1,0:T(2,128)S(1)}, u32[]{:S(2)}, u32[]{:S(2)}) collective-permute-start(f32[2,384]{1,0:T(2,128)S(1)} %maximum_select_fusion.3), channel_id=1, source_target_pairs={{0,2},{1,3},{2,0},{3,1},{4,6},{5,7},{6,4},{7,5},{8,10},{9,11},{10,... | collective-permute-start | bytes 9224 | tf_op jit(solution)/shard_map/ppermute | solution.py:416
  83.4 1.2 collective-permute-done.13
  85.3 2.1 %collective-permute-done.15.got_up = bf16[2,192,1024]{2,1,0:T(8,128)(2,1)} collective-permute-done((bf16[2,192,1024]{2,1,0:T(8,128)(2,1)}, bf16[2,192,1024]{2,1,0:T(8,128)(2,1)}, u32[]{:S(2)}, u32[]{:S(2)}) %collective-permute-start.15) | collective-permute-done | bytes 786464 | tf_op jit(solution)/shard_map/ppermute | solution.py:56
  87.4 3.4 %second_kernel.1 = (bf16[192,1536]{1,0:T(8,128)(2,1)}, bf16[192,1536]{1,0:T(8,128)(2,1)}, bf16[96,512]{1,0:T(8,128)(2,1)}, bf16[96,512]{1,0:T(8,128)(2,1)}, bf16[2,96,512]{2,1,0:T(8,128)(2,1)}) custom-call(bf16[4,192,512]{2,1,0:T(8,128)(2,1)} %get-tuple-element.59.keep, bf16[4,192,512]{2,1,0:T(8,128)(2,1)} %collective-permute-done.14.got_a, ...), custom_call_target="tpu_custom_call" | custom-call | tf_op jit(solution)/shard_map/second_kernel/pallas_call | solution.py:421
  90.7 2.7 %collective-permute-start.22 = (bf16[192,1536]{1,0:T(8,128)(2,1)}, bf16[192,1536]{1,0:T(8,128)(2,1)}, u32[]{:S(2)}, u32[]{:S(2)}) collective-permute-start(bf16[192,1536]{1,0:T(8,128)(2,1)} %get-tuple-element.69), channel_id=1, source_target_pairs={{0,96},{8,104},{16,112},{24,120},{32,0},{40,8},{48,16},{56,24},{64... | collective-permute-start | bytes 1769480 | tf_op jit(solution)/shard_map/ppermute | solution.py:56
  94.5 2.8 %collective-permute-done.17 = f32[9,384]{1,0:T(8,128)S(1)} collective-permute-done((f32[9,384]{1,0:T(8,128)S(1)}, f32[9,384]{1,0:T(8,128)S(1)}, u32[]{:S(2)}, u32[]{:S(2)}) %collective-permute-start.17) | collective-permute-done | bytes 13856 | tf_op jit(solution)/shard_map/ppermute | solution.py:436
  97.3 0.7 fusion.8
  98.0 1.0 collective-permute-start.20
  99.4 1.1 collective-permute-start.18
  100.5 4.6 %collective-permute-done.20 = f32[9,384]{1,0:T(8,128)S(1)} collective-permute-done((f32[9,384]{1,0:T(8,128)S(1)}, f32[9,384]{1,0:T(8,128)S(1)}, u32[]{:S(2)}, u32[]{:S(2)}) %collective-permute-start.20) | collective-permute-done | bytes 13856 | tf_op jit(solution)/shard_map/ppermute | solution.py:437
  105.7 4.0 %third_kernel.1 = (bf16[96,512]{1,0:T(8,128)(2,1)}, bf16[96,512]{1,0:T(8,128)(2,1)}, bf16[192,1024]{1,0:T(8,128)(2,1)}, f32[192,1024]{1,0:T(8,128)}, f32[2,96,512]{2,1,0:T(8,128)}) custom-call(s32[4]{0:T(128)} %pad_add_fusion.place, bf16[2,192,1024]{2,1,0:T(8,128)(2,1)} %collective-permute-done.15.got_up, ...), custom_call_target="tpu_custom_call" | custom-call | tf_op jit(solution)/shard_map/third_kernel/pallas_call | solution.py:72
  109.7 0.9 collective-permute-start.23
  110.6 1.8 %collective-permute-start.24 = (bf16[96,512]{1,0:T(8,128)(2,1)}, bf16[96,512]{1,0:T(8,128)(2,1)}, u32[]{:S(2)}, u32[]{:S(2)}) collective-permute-start(bf16[96,512]{1,0:T(8,128)(2,1)} %get-tuple-element.77), channel_id=1, source_target_pairs={{0,96},{8,104},{16,112},{24,120},{32,0},{40,8},{48,16},{56,24},{64... | collective-permute-start | bytes 294920 | tf_op jit(solution)/shard_map/ppermute | solution.py:56
  112.6 2.4 %fusion.3 = (bf16[96,1920]{1,0:T(8,128)(2,1)}, bf16[96,1920]{1,0:T(8,128)(2,1)}) fusion(bf16[2,96,1920]{2,1,0:T(8,128)(2,1)} %collective-permute-done.10, bf16[4,96,1920]{2,1,0:T(8,128)(2,1)} %get-tuple-element.81, bf16[2,96,1920]{2,1,0:T(8,128)(2,1)} %collective-permute-done.9), kind=kLoop, calls=%fused_computation.11 | loop fusion | flops 1474560 | bytes 2211840 | tf_op jit(solution)/shard_map/convert_element_type | solution.py:60
  114.9 1.2 slice.47
  116.8 2.8 %collective-permute-done.25.got_b = bf16[192,1024]{1,0:T(8,128)(2,1)} collective-permute-done((bf16[192,1024]{1,0:T(8,128)(2,1)}, bf16[192,1024]{1,0:T(8,128)(2,1)}, u32[]{:S(2)}, u32[]{:S(2)}) %collective-permute-start.25) | collective-permute-done | bytes 393248 | tf_op jit(solution)/shard_map/ppermute | solution.py:456
  119.6 2.7 %collective-permute-start.27 = (bf16[96,1920]{1,0:T(8,128)(2,1)}, bf16[96,1920]{1,0:T(8,128)(2,1)}, u32[]{:S(2)}, u32[]{:S(2)}) collective-permute-start(bf16[96,1920]{1,0:T(8,128)(2,1)} %get-tuple-element.84), channel_id=1, source_target_pairs={{0,96},{8,104},{16,112},{24,120},{32,0},{40,8},{48,16},{56,24},{64... | collective-permute-start | bytes 1105928 | tf_op jit(solution)/shard_map/ppermute | solution.py:56
  122.3 8.2 %turn_kernel.1 = bf16[16,144,128]{2,1,0:T(8,128)(2,1)} custom-call(s32[4]{0:T(128)} %pad_add_fusion.place, f32[2,96,512]{2,1,0:T(8,128)} %get-tuple-element.75.keep_a, bf16[96,512]{1,0:T(8,128)(2,1)} %collective-permute-done.23.via_up, bf16[96,512]{1,0:T(8,128)(2,1)} %collective-permute-done.24.via_down, f32[192,1024]{1,0:T(8,128)} %get-tuple-element.78.keep_b, ...), custom_call_target="tpu_custom_call" | custom-call | tf_op jit(solution)/shard_map/turn_kernel/pallas_call | solution.py:72
  130.4 1.9 %select_convert_fusion = bf16[96,1920]{1,0:T(8,128)(2,1)S(1)} fusion(bf16[96,1920]{1,0:T(8,128)(2,1)} %collective-permute-done.26, bf16[96,1920]{1,0:T(8,128)(2,1)} %collective-permute-done.27, pred[]{:T(512)S(6)} %eq.18, bf16[2,96,1920]{2,1,0:T(8,128)(2,1)} %collective-permute-done.9, bf16[2,96,1920]{2,1,0:T(8,128)(2,1)} %collective-permute-done.10, ...), kind=kLoop, calls=%fused_computation.3 | loop fusion | flops 2211840 | bytes 2580481 | tf_op jit(solution)/shard_map/convert_element_type | solution.py:485
  132.7 10.8 %all-to-all-start = ((bf16[16,144,128]{2,1,0:T(8,128)(2,1)}), bf16[16,144,128]{2,1,0:T(8,128)(2,1)}, u32[]{:S(2)}, u32[]{:S(2)}) async-start(bf16[16,144,128]{2,1,0:T(8,128)(2,1)} %turn_kernel.1), calls=%async_computation | async-start | bytes 1179648 | tf_op jit(solution)/shard_map/all_to_all | solution.py:494
  143.5 1.7 %convert_add_fusion = f32[96,1920]{1,0:T(8,128)S(1)} fusion(bf16[96,1920]{1,0:T(8,128)(2,1)S(1)} %collective-permute-done.28, bf16[96,1920]{1,0:T(8,128)(2,1)} %collective-permute-done.26, bf16[96,1920]{1,0:T(8,128)(2,1)} %collective-permute-done.27, pred[]{:T(512)S(6)} %eq.18, bf16[2,96,1920]{2,1,0:T(8,128)(2,1)} %collective-permute-done.9, ...), kind=kLoop, calls=%fused_computation.2 | loop fusion | flops 2396160 | bytes 3317761 | tf_op jit(solution)/shard_map/add | solution.py:47
  145.5 3.0 %collective-permute-start.29 = (bf16[96,192]{1,0:T(8,128)(2,1)S(1)}, bf16[96,192]{1,0:T(8,128)(2,1)S(1)}, u32[]{:S(2)}, u32[]{:S(2)}) collective-permute-start(bf16[96,192]{1,0:T(8,128)(2,1)S(1)} %bitcast.56), channel_id=1, source_target_pairs={{0,8},{8,0},{16,24},{24,16},{32,40},{40,32},{48,56},{56,48},{64,72... | collective-permute-start | bytes 110600 | tf_op jit(solution)/shard_map/ppermute | solution.py:492
  148.5 0.9 fusion.1
  149.6 0.8 copy.28
  150.4 3.8 %all-to-all-done.spread = bf16[16,144,128]{2,1,0:T(8,128)(2,1)} async-done(((bf16[16,144,128]{2,1,0:T(8,128)(2,1)}), bf16[16,144,128]{2,1,0:T(8,128)(2,1)}, u32[]{:S(2)}, u32[]{:S(2)}) %all-to-all-start) | async-done | bytes 589856 | tf_op jit(solution)/shard_map/all_to_all | solution.py:494
  154.2 5.7 %last_kernel.1 = bf16[2,96,1536]{2,1,0:T(8,128)(2,1)} custom-call(bf16[16,144,128]{2,1,0:T(8,128)(2,1)} %all-to-all-done.spread, bf16[1536,1536]{1,0:T(8,128)(2,1)} %basis_out.1), custom_call_target="tpu_custom_call" | custom-call | tf_op jit(solution)/shard_map/last_kernel/pallas_call | solution.py:495
  159.9 2.5 %copy.27 = bf16[96,2,1536]{2,1,0:T(2,128)(2,1)} copy(bf16[96,2,1536]{2,0,1:T(8,128)(2,1)} %bitcast.43) | data formatting | bytes 1179648
  (73 shorter events, 7.9 us)
Async XLA Ops:
  7.2 115.1 %all-gather.2.cloned.1.call-start = ((), (), s32[]{:S(2)}) async-start(), calls=%async_computation.1 | async-start | bytes 5898240 | tf_op jit(solution)/shard_map/all_gather | solution.py:399
  7.2 4.3 %copy-start.1 = (bf16[512,1536]{1,0:T(8,128)(2,1)S(1)}, bf16[512,1536]{1,0:T(8,128)(2,1)}, u32[]{:S(2)}) copy-start(bf16[512,1536]{1,0:T(8,128)(2,1)} %cot_0.1) | copy-start | bytes 4718596
  7.2 4.2 %copy-start.4 = (bf16[96,2,192]{2,1,0:T(2,128)(2,1)S(1)}, bf16[96,2,192]{2,1,0:T(2,128)(2,1)}, u32[]{:S(2)}) copy-start(bf16[96,2,192]{2,1,0:T(2,128)(2,1)} %param.11) | copy-start | bytes 221188
  10.1 23.4 %collective-permute-start.4 = (bf16[512,1536]{1,0:T(8,128)(2,1)}, bf16[512,1536]{1,0:T(8,128)(2,1)S(1)}, u32[]{:S(2)}, u32[]{:S(2)}) collective-permute-start(bf16[512,1536]{1,0:T(8,128)(2,1)} %constant_dynamic-slice_fusion.3), channel_id=1, source_target_pairs={{0,8},{8,0},{16,24},{24,16},{32,40},{40,32},{48,56},{56,48},{64,72... | collective-permute-start | bytes 4718600 | tf_op jit(solution)/shard_map/ppermute | solution.py:306
  11.5 22.7 %collective-permute-start.3 = (bf16[512,1536]{1,0:T(8,128)(2,1)S(1)}, bf16[512,1536]{1,0:T(8,128)(2,1)}, u32[]{:S(2)}, u32[]{:S(2)}) collective-permute-start(bf16[512,1536]{1,0:T(8,128)(2,1)S(1)} %copy-done.1), channel_id=1, source_target_pairs={{0,8},{8,0},{16,24},{24,16},{32,40},{40,32},{48,56},{56,48},{64,72... | collective-permute-start | bytes 4718600 | tf_op jit(solution)/shard_map/ppermute | solution.py:304
  11.7 6.7 %collective-permute-start = (bf16[96,192]{1,0:T(8,128)(2,1)S(1)}, bf16[96,192]{1,0:T(8,128)(2,1)S(1)}, u32[]{:S(2)}, u32[]{:S(2)}) collective-permute-start(bf16[96,192]{1,0:T(8,128)(2,1)S(1)} %bitcast.55), channel_id=1, source_target_pairs={{0,8},{8,0},{16,24},{24,16},{32,40},{40,32},{48,56},{56,48},{64,72... | collective-permute-start | bytes 110600 | tf_op jit(solution)/shard_map/ppermute | solution.py:301
  13.0 8.4 %copy-start.6 = (s32[512]{0:T(512)S(1)}, s32[512]{0:T(512)}, u32[]{:S(2)}) copy-start(s32[512]{0:T(512)} %param.17) | copy-start | bytes 6148
  18.5 9.4 %collective-permute-start.2 = (bf16[192,192]{1,0:T(8,128)(2,1)S(1)}, bf16[192,192]{1,0:T(8,128)(2,1)S(1)}, u32[]{:S(2)}, u32[]{:S(2)}) collective-permute-start(bf16[192,192]{1,0:T(8,128)(2,1)S(1)} %maximum_select_fusion.1), channel_id=1, source_target_pairs={{0,4},{1,5},{2,6},{3,7},{4,0},{5,1},{6,2},{7,3},{8,12},{9,13},{10,... | collective-permute-start | bytes 221192 | tf_op jit(solution)/shard_map/ppermute | solution.py:335
  21.4 1.2 collective-permute-start.1
  22.6 5.3 %copy-start.7 = (s32[1,512]{1,0:T(1,128)}, s32[1,512]{1,0:T(1,128)S(1)}, u32[]{:S(2)}) copy-start(s32[1,512]{1,0:T(1,128)S(1)} %collective-permute-done.1.marks_1) | copy-start | bytes 6148
  27.9 20.4 %collective-permute-start.8 = (bf16[1536,512]{1,0:T(8,128)(2,1)}, bf16[1536,512]{1,0:T(8,128)(2,1)}, u32[]{:S(2)}, u32[]{:S(2)}) collective-permute-start(bf16[1536,512]{1,0:T(8,128)(2,1)} %rotate_kernel.3.eigen_0), channel_id=1, source_target_pairs={{0,8},{8,0},{16,24},{24,16},{32,40},{40,32},{48,56},{56,48},{64,72... | collective-permute-start | bytes 4718600 | tf_op jit(solution)/shard_map/ppermute | solution.py:337
  28.4 16.3 %collective-permute-start.7 = (bf16[192,384]{1,0:T(8,128)(2,1)S(1)}, bf16[192,384]{1,0:T(8,128)(2,1)S(1)}, u32[]{:S(2)}, u32[]{:S(2)}) collective-permute-start(bf16[192,384]{1,0:T(8,128)(2,1)S(1)} %pad_maximum_fusion.1), channel_id=1, source_target_pairs={{0,32},{8,40},{16,48},{24,56},{32,64},{40,72},{48,80},{56,88},{64,... | collective-permute-start | bytes 442376 | tf_op jit(solution)/shard_map/ppermute | solution.py:339
  30.1 16.9 %collective-permute-start.6 = (bf16[192,384]{1,0:T(8,128)(2,1)S(1)}, bf16[192,384]{1,0:T(8,128)(2,1)S(1)}, u32[]{:S(2)}, u32[]{:S(2)}) collective-permute-start(bf16[192,384]{1,0:T(8,128)(2,1)S(1)} %pad_maximum_fusion.1), channel_id=1, source_target_pairs={{0,64},{8,72},{16,80},{24,88},{32,96},{40,104},{48,112},{56,120},{... | collective-permute-start | bytes 442376 | tf_op jit(solution)/shard_map/ppermute | solution.py:339
  33.5 1.1 copy-start
  33.5 13.6 %collective-permute-start.5 = (bf16[192,384]{1,0:T(8,128)(2,1)S(1)}, bf16[192,384]{1,0:T(8,128)(2,1)S(1)}, u32[]{:S(2)}, u32[]{:S(2)}) collective-permute-start(bf16[192,384]{1,0:T(8,128)(2,1)S(1)} %pad_maximum_fusion.1), channel_id=1, source_target_pairs={{0,96},{8,104},{16,112},{24,120},{32,0},{40,8},{48,16},{56,24},{64... | collective-permute-start | bytes 442376 | tf_op jit(solution)/shard_map/ppermute | solution.py:339
  44.4 19.9 %collective-permute-start.9 = (bf16[2,96,1920]{2,1,0:T(8,128)(2,1)}, bf16[2,96,1920]{2,1,0:T(8,128)(2,1)}, u32[]{:S(2)}, u32[]{:S(2)}) collective-permute-start(bf16[2,96,1920]{2,1,0:T(8,128)(2,1)} %get-tuple-element.49), channel_id=1, source_target_pairs={{0,32},{8,40},{16,48},{24,56},{32,64},{40,72},{48,80},{56,88},{64,... | collective-permute-start | bytes 2211848 | tf_op jit(solution)/shard_map/ppermute | solution.py:56
  44.7 19.6 %collective-permute-start.10 = (bf16[2,96,1920]{2,1,0:T(8,128)(2,1)}, bf16[2,96,1920]{2,1,0:T(8,128)(2,1)}, u32[]{:S(2)}, u32[]{:S(2)}) collective-permute-start(bf16[2,96,1920]{2,1,0:T(8,128)(2,1)} %get-tuple-element.55), channel_id=1, source_target_pairs={{0,96},{8,104},{16,112},{24,120},{32,0},{40,8},{48,16},{56,24},{64... | collective-permute-start | bytes 2211848 | tf_op jit(solution)/shard_map/ppermute | solution.py:56
  48.0 16.3 %collective-permute-start.11 = (bf16[4,192,384]{2,1,0:T(8,128)(2,1)}, bf16[4,192,384]{2,1,0:T(8,128)(2,1)}, u32[]{:S(2)}, u32[]{:S(2)}) collective-permute-start(bf16[4,192,384]{2,1,0:T(8,128)(2,1)} %pad_maximum_fusion.own), channel_id=1, source_target_pairs={{0,16},{8,24},{16,0},{24,8},{32,48},{40,56},{48,32},{56,40},{64,80... | collective-permute-start | bytes 1769480 | tf_op jit(solution)/shard_map/ppermute | solution.py:366
  67.4 17.9 %collective-permute-start.14 = (bf16[4,192,512]{2,1,0:T(8,128)(2,1)}, bf16[4,192,512]{2,1,0:T(8,128)(2,1)}, u32[]{:S(2)}, u32[]{:S(2)}) collective-permute-start(bf16[4,192,512]{2,1,0:T(8,128)(2,1)} %get-tuple-element.63), channel_id=1, source_target_pairs={{0,16},{8,24},{16,0},{24,8},{32,48},{40,56},{48,32},{56,40},{64,80... | collective-permute-start | bytes 2359304 | tf_op jit(solution)/shard_map/ppermute | solution.py:418
  68.7 18.7 %collective-permute-start.15 = (bf16[2,192,1024]{2,1,0:T(8,128)(2,1)}, bf16[2,192,1024]{2,1,0:T(8,128)(2,1)}, u32[]{:S(2)}, u32[]{:S(2)}) collective-permute-start(bf16[2,192,1024]{2,1,0:T(8,128)(2,1)} %get-tuple-element.64), channel_id=1, source_target_pairs={{0,32},{8,40},{16,48},{24,56},{32,64},{40,72},{48,80},{56,88},{64,... | collective-permute-start | bytes 2359304 | tf_op jit(solution)/shard_map/ppermute | solution.py:56
  68.7 18.7 %collective-permute-start.16 = (bf16[2,192,1024]{2,1,0:T(8,128)(2,1)}, bf16[2,192,1024]{2,1,0:T(8,128)(2,1)}, u32[]{:S(2)}, u32[]{:S(2)}) collective-permute-start(bf16[2,192,1024]{2,1,0:T(8,128)(2,1)} %get-tuple-element.65), channel_id=1, source_target_pairs={{0,96},{8,104},{16,112},{24,120},{32,0},{40,8},{48,16},{56,24},{64... | collective-permute-start | bytes 2359304 | tf_op jit(solution)/shard_map/ppermute | solution.py:56
  76.6 3.0 %collective-permute-start.12 = (f32[1,384]{1,0:T(1,128)}, f32[1,384]{1,0:T(1,128)S(1)}, u32[]{:S(2)}, u32[]{:S(2)}) collective-permute-start(f32[1,384]{1,0:T(1,128)} %squares_in_kernel.1), channel_id=1, source_target_pairs={{0,1},{1,0},{2,3},{3,2},{4,5},{5,4},{6,7},{7,6},{8,9},{9,8},{10,11... | collective-permute-start | bytes 4616 | tf_op jit(solution)/shard_map/ppermute | solution.py:415
  80.5 4.1 %collective-permute-start.13 = (f32[2,384]{1,0:T(2,128)S(1)}, f32[2,384]{1,0:T(2,128)S(1)}, u32[]{:S(2)}, u32[]{:S(2)}) collective-permute-start(f32[2,384]{1,0:T(2,128)S(1)} %maximum_select_fusion.3), channel_id=1, source_target_pairs={{0,2},{1,3},{2,0},{3,1},{4,6},{5,7},{6,4},{7,5},{8,10},{9,11},{10,... | collective-permute-start | bytes 9224 | tf_op jit(solution)/shard_map/ppermute | solution.py:416
  90.7 15.0 %collective-permute-start.21 = (bf16[192,1536]{1,0:T(8,128)(2,1)}, bf16[192,1536]{1,0:T(8,128)(2,1)}, u32[]{:S(2)}, u32[]{:S(2)}) collective-permute-start(bf16[192,1536]{1,0:T(8,128)(2,1)} %get-tuple-element.68), channel_id=1, source_target_pairs={{0,32},{8,40},{16,48},{24,56},{32,64},{40,72},{48,80},{56,88},{64,... | collective-permute-start | bytes 1769480 | tf_op jit(solution)/shard_map/ppermute | solution.py:56
  90.7 15.0 %collective-permute-start.22 = (bf16[192,1536]{1,0:T(8,128)(2,1)}, bf16[192,1536]{1,0:T(8,128)(2,1)}, u32[]{:S(2)}, u32[]{:S(2)}) collective-permute-start(bf16[192,1536]{1,0:T(8,128)(2,1)} %get-tuple-element.69), channel_id=1, source_target_pairs={{0,96},{8,104},{16,112},{24,120},{32,0},{40,8},{48,16},{56,24},{64... | collective-permute-start | bytes 1769480 | tf_op jit(solution)/shard_map/ppermute | solution.py:56
  94.2 3.1 %collective-permute-start.17 = (f32[9,384]{1,0:T(8,128)S(1)}, f32[9,384]{1,0:T(8,128)S(1)}, u32[]{:S(2)}, u32[]{:S(2)}) collective-permute-start(f32[9,384]{1,0:T(8,128)S(1)} %pad_maximum_fusion.2), channel_id=1, source_target_pairs={{0,16},{8,24},{16,0},{24,8},{32,48},{40,56},{48,32},{56,40},{64,80... | collective-permute-start | bytes 41480 | tf_op jit(solution)/shard_map/ppermute | solution.py:436
  98.0 7.0 %collective-permute-start.20 = (f32[9,384]{1,0:T(8,128)S(1)}, f32[9,384]{1,0:T(8,128)S(1)}, u32[]{:S(2)}, u32[]{:S(2)}) collective-permute-start(f32[9,384]{1,0:T(8,128)S(1)} %fusion.8), channel_id=1, source_target_pairs={{0,64},{8,72},{16,80},{24,88},{32,96},{40,104},{48,112},{56,120},{... | collective-permute-start | bytes 41480 | tf_op jit(solution)/shard_map/ppermute | solution.py:437
  99.0 6.1 %collective-permute-start.19 = (f32[9,384]{1,0:T(8,128)S(1)}, f32[9,384]{1,0:T(8,128)S(1)}, u32[]{:S(2)}, u32[]{:S(2)}) collective-permute-start(f32[9,384]{1,0:T(8,128)S(1)} %fusion.8), channel_id=1, source_target_pairs={{0,96},{8,104},{16,112},{24,120},{32,0},{40,8},{48,16},{56,24},{64... | collective-permute-start | bytes 41480 | tf_op jit(solution)/shard_map/ppermute | solution.py:437
  99.4 5.7 %collective-permute-start.18 = (f32[9,384]{1,0:T(8,128)S(1)}, f32[9,384]{1,0:T(8,128)S(1)}, u32[]{:S(2)}, u32[]{:S(2)}) collective-permute-start(f32[9,384]{1,0:T(8,128)S(1)} %fusion.8), channel_id=1, source_target_pairs={{0,32},{8,40},{16,48},{24,56},{32,64},{40,72},{48,80},{56,88},{64,... | collective-permute-start | bytes 41480 | tf_op jit(solution)/shard_map/ppermute | solution.py:437
  109.7 7.1 %collective-permute-start.23 = (bf16[96,512]{1,0:T(8,128)(2,1)}, bf16[96,512]{1,0:T(8,128)(2,1)}, u32[]{:S(2)}, u32[]{:S(2)}) collective-permute-start(bf16[96,512]{1,0:T(8,128)(2,1)} %get-tuple-element.76), channel_id=1, source_target_pairs={{0,32},{8,40},{16,48},{24,56},{32,64},{40,72},{48,80},{56,88},{64,... | collective-permute-start | bytes 294920 | tf_op jit(solution)/shard_map/ppermute | solution.py:56
  110.6 6.2 %collective-permute-start.24 = (bf16[96,512]{1,0:T(8,128)(2,1)}, bf16[96,512]{1,0:T(8,128)(2,1)}, u32[]{:S(2)}, u32[]{:S(2)}) collective-permute-start(bf16[96,512]{1,0:T(8,128)(2,1)} %get-tuple-element.77), channel_id=1, source_target_pairs={{0,96},{8,104},{16,112},{24,120},{32,0},{40,8},{48,16},{56,24},{64... | collective-permute-start | bytes 294920 | tf_op jit(solution)/shard_map/ppermute | solution.py:56
  112.3 7.2 %collective-permute-start.25 = (bf16[192,1024]{1,0:T(8,128)(2,1)}, bf16[192,1024]{1,0:T(8,128)(2,1)}, u32[]{:S(2)}, u32[]{:S(2)}) collective-permute-start(bf16[192,1024]{1,0:T(8,128)(2,1)} %get-tuple-element.79), channel_id=1, source_target_pairs={{0,16},{8,24},{16,0},{24,8},{32,48},{40,56},{48,32},{56,40},{64,80... | collective-permute-start | bytes 1179656 | tf_op jit(solution)/shard_map/ppermute | solution.py:456
  119.6 10.8 %collective-permute-start.26 = (bf16[96,1920]{1,0:T(8,128)(2,1)}, bf16[96,1920]{1,0:T(8,128)(2,1)}, u32[]{:S(2)}, u32[]{:S(2)}) collective-permute-start(bf16[96,1920]{1,0:T(8,128)(2,1)} %get-tuple-element.83), channel_id=1, source_target_pairs={{0,32},{8,40},{16,48},{24,56},{32,64},{40,72},{48,80},{56,88},{64,... | collective-permute-start | bytes 1105928 | tf_op jit(solution)/shard_map/ppermute | solution.py:56
  119.6 10.9 %collective-permute-start.27 = (bf16[96,1920]{1,0:T(8,128)(2,1)}, bf16[96,1920]{1,0:T(8,128)(2,1)}, u32[]{:S(2)}, u32[]{:S(2)}) collective-permute-start(bf16[96,1920]{1,0:T(8,128)(2,1)} %get-tuple-element.84), channel_id=1, source_target_pairs={{0,96},{8,104},{16,112},{24,120},{32,0},{40,8},{48,16},{56,24},{64... | collective-permute-start | bytes 1105928 | tf_op jit(solution)/shard_map/ppermute | solution.py:56
  130.4 13.1 %copy-start.2 = (bf16[4,96,1920]{2,1,0:T(8,128)(2,1)S(1)}, bf16[4,96,1920]{2,1,0:T(8,128)(2,1)}, u32[]{:S(2)}) copy-start(bf16[4,96,1920]{2,1,0:T(8,128)(2,1)} %get-tuple-element.81) | copy-start | bytes 4423684
  132.4 11.1 %collective-permute-start.28 = (bf16[96,1920]{1,0:T(8,128)(2,1)S(1)}, bf16[96,1920]{1,0:T(8,128)(2,1)S(1)}, u32[]{:S(2)}, u32[]{:S(2)}) collective-permute-start(bf16[96,1920]{1,0:T(8,128)(2,1)S(1)} %select_convert_fusion), channel_id=1, source_target_pairs={{0,16},{8,24},{16,0},{24,8},{32,48},{40,56},{48,32},{56,40},{64,80... | collective-permute-start | bytes 1105928 | tf_op jit(solution)/shard_map/ppermute | solution.py:487
  132.7 21.5 %all-to-all-start = ((bf16[16,144,128]{2,1,0:T(8,128)(2,1)}), bf16[16,144,128]{2,1,0:T(8,128)(2,1)}, u32[]{:S(2)}, u32[]{:S(2)}) async-start(bf16[16,144,128]{2,1,0:T(8,128)(2,1)} %turn_kernel.1), calls=%async_computation | async-start | bytes 1179648 | tf_op jit(solution)/shard_map/all_to_all | solution.py:494
  143.5 5.0 %copy-start.3 = (f32[96,1536]{1,0:T(8,128)S(1)}, f32[96,1536]{1,0:T(8,128)}, u32[]{:S(2)}) copy-start(f32[96,1536]{1,0:T(8,128)} %param.14) | copy-start | bytes 1769476
  145.2 4.3 %copy-start.5 = (f32[96,2,192]{2,1,0:T(2,128)S(1)}, f32[96,2,192]{2,1,0:T(2,128)}, u32[]{:S(2)}) copy-start(f32[96,2,192]{2,1,0:T(2,128)} %param.13) | copy-start | bytes 442372
  145.5 4.0 %collective-permute-start.29 = (bf16[96,192]{1,0:T(8,128)(2,1)S(1)}, bf16[96,192]{1,0:T(8,128)(2,1)S(1)}, u32[]{:S(2)}, u32[]{:S(2)}) collective-permute-start(bf16[96,192]{1,0:T(8,128)(2,1)S(1)} %bitcast.56), channel_id=1, source_target_pairs={{0,8},{8,0},{16,24},{24,16},{32,40},{40,32},{48,56},{56,48},{64,72... | collective-permute-start | bytes 110600 | tf_op jit(solution)/shard_map/ppermute | solution.py:492
Sparse Core Ops, SparseCore 0:
  67.5 51.9 all-gather.1

commit v6 on v5

--- a/solution.py
+++ b/solution.py
@@ -435,8 +435,6 @@
     small = jnp.concatenate([squares_out, after(by_y, second_up, second_down)], 0)
     small = small + lax.ppermute(small, "dp", XLO)
     small = added(small, *[lax.ppermute(small, "dp", to_z(i)) for i in (1, 3, 2)])
-    cov_late = after(cov_rest, small)
-    cov_next = forward_z(cov_got_up, cov_got_down, cov_late[2], cov_late[3])
     near = pl.BlockSpec((1, chunk, width - cut), lambda i, p: (1, 0, 0))
     third_in = (second_got_up, second_got_down, own_b, a_first_1, a_second_3, own_a)
     third_up, third_down, b_give, b_keep, a_keep = placed(
@@ -453,12 +451,14 @@
         ],
         (got_up, got_down, *third_in),
     )
+    healthy_rows = f32(tokens * lax.axis_size("dp")) - after(small, b_give)[4, 0]
     b_got = lax.ppermute(b_give, "dp", XLO)
+    third_up, third_down = lax.optimization_barrier((third_up, third_down, healthy_rows))[:2]
     a_via_up, a_via_down = send_z(third_up, third_down)
 
-    healthy_rows = f32(tokens * lax.axis_size("dp")) - small[4, 0]
-
-    cov_next = lax.optimization_barrier((*cov_next, b_got, a_via_up, a_via_down, healthy_rows))[:2]
+
+    cov_next = forward_z(cov_got_up, cov_got_down, cov_rest[2], cov_rest[3])
+    cov_next = lax.optimization_barrier((*cov_next, a_via_up, a_via_down, b_got, healthy_rows))[:2]
     cov_via_up, cov_via_down = send_z(*cov_next)
 
     turn_in = (a_keep, a_via_up, a_via_down, b_keep, b_got)

time: 170 us -> 169 us (level)
    ppermute x1, waiting for transfers between devices: 2.82 us -> 0.01 us  [per_device(): b_got = lax.ppermute(b_give, 'dp', XLO)]
where the time goes in v6:
time: 169 us; the launch traced here: 168 us
  Pallas kernels  64.9 us (38%)
  starting transfers between devices  48.6 us (29%)
  waiting for transfers between devices  18.3 us (11%)
  between operations  14.9 us (9%)
  other arithmetic  12.1 us (7%)
  local copies, waits for them, and re-layouts  9.66 us (6%)
    pallas_call x7, Pallas kernels, placed(): pl.pallas_call(kernel, out_shape=out_shapes, grid_spec=pltpu.PrefetchScal...  45 us
    ppermute x10, starting transfers between devices, send_z(): return (lax.ppermute(up, 'dp', UP), lax.ppermute(down, 'dp', DOWN))  13.5 us
    all_to_all x1, starting transfers between devices, per_device(): spread = lax.all_to_all(turned, 'dp', split_axis=0, concat_axis=0)  11.4 us
    pallas_call x2, Pallas kernels, rotate(): pl.pallas_call(rotate_kernel, out_shape=shape_of(width, tokens), grid_spe...  10.8 us
    ppermute x3, starting transfers between devices, per_device(): basis_z = [lax.ppermute(basis_pair, 'dp', to_z(4 - s)) for s in (1, 2, 3)]  5.74 us
    pallas_call x1, Pallas kernels, per_device(): pl.pallas_call(last_kernel, out_shape=shape_of(2, rows, width), grid=(4,)...  5.67 us
    all_to_all x1, waiting for transfers between devices, per_device(): spread = lax.all_to_all(turned, 'dp', split_axis=0, concat_axis=0)  4.65 us
    ppermute x3, waiting for transfers between devices, per_device(): lax.ppermute(small, 'dp', to_z(i))  4.62 us
  transfers between devices with their start and end apart: 32, of which 9 were waited for; matrix products, arithmetic and copies ran while one was open for 8% of the time, Pallas kernels for 33%

profile of v6, /device:TPU:1, one launch (start us, length us, event | category | flops | bytes accessed | tf_op | source)
XLA Modules:
  0.0 168.4 jit_solution(7368095884639320269)
XLA Ops:
  7.3 2.8 %constant_dynamic-slice_fusion.3 = bf16[512,1536]{1,0:T(8,128)(2,1)} fusion(bf16[512,3072]{1,0:T(8,128)(2,1)} %act_0.5, s32[]{:T(128)S(6)} %select_n.89), kind=kLoop, calls=%fused_computation.31 | loop fusion | bytes 3145732 | tf_op jit(solution)/shard_map/dynamic_slice | solution.py:305
  10.1 1.4 collective-permute-start.4
  13.0 5.5 %rotate_kernel.2.refs_0_ = bf16[1536,512]{1,0:T(8,128)(2,1)} custom-call(s32[4]{0:T(128)} %pad_add_fusion.place, bf16[512,1536]{1,0:T(8,128)(2,1)} %cot_0.1, s32[1,512]{1,0:T(1,128)} %bitcast.49, bf16[1536,1536]{1,0:T(8,128)(2,1)} %basis_out.1), custom_call_target="tpu_custom_call" | custom-call | tf_op jit(solution)/shard_map/rotate_kernel/pallas_call | solution.py:309
  18.5 2.9 %collective-permute-start.2 = (bf16[192,192]{1,0:T(8,128)(2,1)S(1)}, bf16[192,192]{1,0:T(8,128)(2,1)S(1)}, u32[]{:S(2)}, u32[]{:S(2)}) collective-permute-start(bf16[192,192]{1,0:T(8,128)(2,1)S(1)} %maximum_select_fusion.1), channel_id=1, source_target_pairs={{0,4},{1,5},{2,6},{3,7},{4,0},{5,1},{6,2},{7,3},{8,12},{9,13},{10,... | collective-permute-start | bytes 221192 | tf_op jit(solution)/shard_map/ppermute | solution.py:335
  21.7 0.8 collective-permute-done.1.marks_1
  22.6 5.3 %rotate_kernel.3.eigen_0 = bf16[1536,512]{1,0:T(8,128)(2,1)} custom-call(s32[4]{0:T(128)} %pad_add_fusion.place, bf16[512,1536]{1,0:T(8,128)(2,1)} %cot_0.1, s32[1,512]{1,0:T(1,128)} %bitcast.50, bf16[1536,1536]{1,0:T(8,128)(2,1)} %basis_out.1, bf16[1536,512]{1,0:T(8,128)(2,1)} %rotate_kernel.2.refs_0_), custom_call_target="tpu_custom_call", output_to_operand_aliasing={{}: (4, {})} | custom-call | tf_op jit(solution)/shard_map/rotate_kernel/pallas_call | solution.py:309
  28.4 1.7 %collective-permute-start.7 = (bf16[192,384]{1,0:T(8,128)(2,1)S(1)}, bf16[192,384]{1,0:T(8,128)(2,1)S(1)}, u32[]{:S(2)}, u32[]{:S(2)}) collective-permute-start(bf16[192,384]{1,0:T(8,128)(2,1)S(1)} %pad_maximum_fusion.1), channel_id=1, source_target_pairs={{0,32},{8,40},{16,48},{24,56},{32,64},{40,72},{48,80},{56,88},{64,... | collective-permute-start | bytes 442376 | tf_op jit(solution)/shard_map/ppermute | solution.py:339
  30.1 3.3 %collective-permute-start.6 = (bf16[192,384]{1,0:T(8,128)(2,1)S(1)}, bf16[192,384]{1,0:T(8,128)(2,1)S(1)}, u32[]{:S(2)}, u32[]{:S(2)}) collective-permute-start(bf16[192,384]{1,0:T(8,128)(2,1)S(1)} %pad_maximum_fusion.1), channel_id=1, source_target_pairs={{0,64},{8,72},{16,80},{24,88},{32,96},{40,104},{48,112},{56,120},{... | collective-permute-start | bytes 442376 | tf_op jit(solution)/shard_map/ppermute | solution.py:339
  34.6 9.8 %cov_kernel.1 = (bf16[2,96,1920]{2,1,0:T(8,128)(2,1)}, bf16[2,96,1920]{2,1,0:T(8,128)(2,1)}, bf16[4,96,1920]{2,1,0:T(8,128)(2,1)}) custom-call(s32[4]{0:T(128)} %pad_add_fusion.place, bf16[512,1536]{1,0:T(8,128)(2,1)} %cot_0.1, bf16[512,1536]{1,0:T(8,128)(2,1)} %collective-permute-done.3.cot_1, s32[1,512]{1,0:T(1,128)} %bitcast.51, s32[1,512]{1,0:T(1,128)} %copy-done.7, ...), custom_call_target="tpu_custom_call" | custom-call | tf_op jit(solution)/shard_map/cov_kernel/pallas_call | solution.py:72
  44.7 2.4 %collective-permute-start.10 = (bf16[2,96,1920]{2,1,0:T(8,128)(2,1)}, bf16[2,96,1920]{2,1,0:T(8,128)(2,1)}, u32[]{:S(2)}, u32[]{:S(2)}) collective-permute-start(bf16[2,96,1920]{2,1,0:T(8,128)(2,1)} %get-tuple-element.57), channel_id=1, source_target_pairs={{0,96},{8,104},{16,112},{24,120},{32,0},{40,8},{48,16},{56,24},{64... | collective-permute-start | bytes 2211848 | tf_op jit(solution)/shard_map/ppermute | solution.py:56
  47.0 0.9 pad_maximum_fusion.own
  48.3 10.8 %grad_kernel.1 = (bf16[4,192,512]{2,1,0:T(8,128)(2,1)}, bf16[4,192,512]{2,1,0:T(8,128)(2,1)}, bf16[2,192,1024]{2,1,0:T(8,128)(2,1)}, bf16[2,192,1024]{2,1,0:T(8,...) custom-call(s32[4]{0:T(128)} %pad_add_fusion.place, ...), custom_call_target="tpu_custom_call" | custom-call | tf_op jit(solution)/shard_map/grad_kernel/pallas_call | solution.py:72
  59.1 1.3 reshape.36.scale_out
  60.4 3.9 %squares_out_kernel.1 = f32[5,384]{1,0:T(8,128)} custom-call(s32[4]{0:T(128)} %pad_add_fusion.place, s32[1,512]{1,0:T(1,128)} %bitcast.52, s32[1,512]{1,0:T(1,128)} %copy-done.7, bf16[1536,512]{1,0:T(8,128)(2,1)} %rotate_kernel.3.eigen_0, bf16[1536,512]{1,0:T(8,128)(2,1)} %collective-permute-done.8.eigen_1), custom_call_target="tpu_custom_call" | custom-call | tf_op jit(solution)/shard_map/squares_out_kernel/pallas_call | solution.py:72
  64.3 3.1 %rows_kernel.1 = bf16[4,2,192,384]{3,2,1,0:T(8,128)(2,1)} custom-call(s32[4]{0:T(128)} %pad_add_fusion.place, bf16[4,192,384]{2,1,0:T(8,128)(2,1)} %pad_maximum_fusion.own, bf16[4,192,384]{2,1,0:T(8,128)(2,1)} %collective-permute-done.11.got), custom_call_target="tpu_custom_call" | custom-call | tf_op jit(solution)/shard_map/rows_kernel/pallas_call | solution.py:72
  67.4 1.2 collective-permute-start.14
  68.7 2.7 %collective-permute-start.16 = (bf16[2,192,1024]{2,1,0:T(8,128)(2,1)}, bf16[2,192,1024]{2,1,0:T(8,128)(2,1)}, u32[]{:S(2)}, u32[]{:S(2)}) collective-permute-start(bf16[2,192,1024]{2,1,0:T(8,128)(2,1)} %get-tuple-element.67), channel_id=1, source_target_pairs={{0,96},{8,104},{16,112},{24,120},{32,0},{40,8},{48,16},{56,24},{64... | collective-permute-start | bytes 2359304 | tf_op jit(solution)/shard_map/ppermute | solution.py:56
  71.3 5.3 %squares_in_kernel.1 = f32[1,384]{1,0:T(1,128)} custom-call(s32[4]{0:T(128)} %pad_add_fusion.place, bf16[512,3072]{1,0:T(8,128)(2,1)} %act_0.5, bf16[512,1536]{1,0:T(8,128)(2,1)} %copy-done, s32[1,512]{1,0:T(1,128)} %bitcast.53, s32[1,512]{1,0:T(1,128)} %copy-done.7, bf16[1536,384]{1,0:T(8,128)(2,1)} %bitcast.42), custom_call_target="tpu_custom_call" | custom-call | tf_op jit(solution)/shard_map/squares_in_kernel/pallas_call | solution.py:72
  76.6 1.3 collective-permute-start.12
  77.9 1.8 %collective-permute-done.12 = f32[1,384]{1,0:T(1,128)S(1)} collective-permute-done((f32[1,384]{1,0:T(1,128)}, f32[1,384]{1,0:T(1,128)S(1)}, u32[]{:S(2)}, u32[]{:S(2)}) %collective-permute-start.12) | collective-permute-done | bytes 1568 | tf_op jit(solution)/shard_map/ppermute | solution.py:415
  79.7 0.8 maximum_select_fusion.3
  80.5 3.0 %collective-permute-start.13 = (f32[2,384]{1,0:T(2,128)S(1)}, f32[2,384]{1,0:T(2,128)S(1)}, u32[]{:S(2)}, u32[]{:S(2)}) collective-permute-start(f32[2,384]{1,0:T(2,128)S(1)} %maximum_select_fusion.3), channel_id=1, source_target_pairs={{0,2},{1,3},{2,0},{3,1},{4,6},{5,7},{6,4},{7,5},{8,10},{9,11},{10,... | collective-permute-start | bytes 9224 | tf_op jit(solution)/shard_map/ppermute | solution.py:416
  83.4 1.2 collective-permute-done.13
  85.3 2.1 %collective-permute-done.15.got_up = bf16[2,192,1024]{2,1,0:T(8,128)(2,1)} collective-permute-done((bf16[2,192,1024]{2,1,0:T(8,128)(2,1)}, bf16[2,192,1024]{2,1,0:T(8,128)(2,1)}, u32[]{:S(2)}, u32[]{:S(2)}) %collective-permute-start.15) | collective-permute-done | bytes 786464 | tf_op jit(solution)/shard_map/ppermute | solution.py:56
  87.4 3.4 %second_kernel.1 = (bf16[192,1536]{1,0:T(8,128)(2,1)}, bf16[192,1536]{1,0:T(8,128)(2,1)}, bf16[96,512]{1,0:T(8,128)(2,1)}, bf16[96,512]{1,0:T(8,128)(2,1)}, bf16[2,96,512]{2,1,0:T(8,128)(2,1)}) custom-call(bf16[4,192,512]{2,1,0:T(8,128)(2,1)} %get-tuple-element.61.keep, bf16[4,192,512]{2,1,0:T(8,128)(2,1)} %collective-permute-done.14.got_a, ...), custom_call_target="tpu_custom_call" | custom-call | tf_op jit(solution)/shard_map/second_kernel/pallas_call | solution.py:421
  90.7 2.7 %collective-permute-start.22 = (bf16[192,1536]{1,0:T(8,128)(2,1)}, bf16[192,1536]{1,0:T(8,128)(2,1)}, u32[]{:S(2)}, u32[]{:S(2)}) collective-permute-start(bf16[192,1536]{1,0:T(8,128)(2,1)} %get-tuple-element.71), channel_id=1, source_target_pairs={{0,96},{8,104},{16,112},{24,120},{32,0},{40,8},{48,16},{56,24},{64... | collective-permute-start | bytes 1769480 | tf_op jit(solution)/shard_map/ppermute | solution.py:56
  94.5 2.8 %collective-permute-done.17 = f32[9,384]{1,0:T(8,128)S(1)} collective-permute-done((f32[9,384]{1,0:T(8,128)S(1)}, f32[9,384]{1,0:T(8,128)S(1)}, u32[]{:S(2)}, u32[]{:S(2)}) %collective-permute-start.17) | collective-permute-done | bytes 13856 | tf_op jit(solution)/shard_map/ppermute | solution.py:436
  98.0 1.0 collective-permute-start.20
  99.4 1.1 collective-permute-start.18
  100.5 4.6 %collective-permute-done.20 = f32[9,384]{1,0:T(8,128)S(1)} collective-permute-done((f32[9,384]{1,0:T(8,128)S(1)}, f32[9,384]{1,0:T(8,128)S(1)}, u32[]{:S(2)}, u32[]{:S(2)}) %collective-permute-start.20) | collective-permute-done | bytes 13856 | tf_op jit(solution)/shard_map/ppermute | solution.py:437
  105.7 4.0 %third_kernel.1 = (bf16[96,512]{1,0:T(8,128)(2,1)}, bf16[96,512]{1,0:T(8,128)(2,1)}, bf16[192,1024]{1,0:T(8,128)(2,1)}, f32[192,1024]{1,0:T(8,128)}, f32[2,96,512]{2,1,0:T(8,128)}) custom-call(s32[4]{0:T(128)} %pad_add_fusion.place, bf16[2,192,1024]{2,1,0:T(8,128)(2,1)} %collective-permute-done.15.got_up, ...), custom_call_target="tpu_custom_call" | custom-call | tf_op jit(solution)/shard_map/third_kernel/pallas_call | solution.py:72
  109.9 1.2 slice.33
  111.7 1.0 collective-permute-start.23
  112.7 1.7 %collective-permute-start.24 = (bf16[96,512]{1,0:T(8,128)(2,1)}, bf16[96,512]{1,0:T(8,128)(2,1)}, u32[]{:S(2)}, u32[]{:S(2)}) collective-permute-start(bf16[96,512]{1,0:T(8,128)(2,1)} %get-tuple-element.83), channel_id=1, source_target_pairs={{0,96},{8,104},{16,112},{24,120},{32,0},{40,8},{48,16},{56,24},{64... | collective-permute-start | bytes 294920 | tf_op jit(solution)/shard_map/ppermute | solution.py:56
  114.5 2.4 %fusion.3 = (bf16[96,1920]{1,0:T(8,128)(2,1)}, bf16[96,1920]{1,0:T(8,128)(2,1)}) fusion(bf16[2,96,1920]{2,1,0:T(8,128)(2,1)} %collective-permute-done.10, bf16[4,96,1920]{2,1,0:T(8,128)(2,1)} %get-tuple-element.86, bf16[2,96,1920]{2,1,0:T(8,128)(2,1)} %collective-permute-done.9), kind=kLoop, calls=%fused_computation.11 | loop fusion | flops 1474560 | bytes 2211840 | tf_op jit(solution)/shard_map/convert_element_type | solution.py:60
  117.1 0.7 collective-permute-start.26
  117.8 2.0 %collective-permute-start.27 = (bf16[96,1920]{1,0:T(8,128)(2,1)}, bf16[96,1920]{1,0:T(8,128)(2,1)}, u32[]{:S(2)}, u32[]{:S(2)}) collective-permute-start(bf16[96,1920]{1,0:T(8,128)(2,1)} %get-tuple-element.88), channel_id=1, source_target_pairs={{0,96},{8,104},{16,112},{24,120},{32,0},{40,8},{48,16},{56,24},{64... | collective-permute-start | bytes 1105928 | tf_op jit(solution)/shard_map/ppermute | solution.py:56
  119.8 8.2 %turn_kernel.1 = bf16[16,144,128]{2,1,0:T(8,128)(2,1)} custom-call(s32[4]{0:T(128)} %pad_add_fusion.place, f32[2,96,512]{2,1,0:T(8,128)} %get-tuple-element.77.keep_a, bf16[96,512]{1,0:T(8,128)(2,1)} %collective-permute-done.23.via_up, bf16[96,512]{1,0:T(8,128)(2,1)} %collective-permute-done.24.via_down, f32[192,1024]{1,0:T(8,128)} %get-tuple-element.84.keep_b, ...), custom_call_target="tpu_custom_call" | custom-call | tf_op jit(solution)/shard_map/turn_kernel/pallas_call | solution.py:72
  128.0 1.9 %select_convert_fusion = bf16[96,1920]{1,0:T(8,128)(2,1)S(1)} fusion(bf16[96,1920]{1,0:T(8,128)(2,1)} %collective-permute-done.26, bf16[96,1920]{1,0:T(8,128)(2,1)} %collective-permute-done.27, pred[]{:T(512)S(6)} %eq.18, bf16[2,96,1920]{2,1,0:T(8,128)(2,1)} %collective-permute-done.9, bf16[2,96,1920]{2,1,0:T(8,128)(2,1)} %collective-permute-done.10, ...), kind=kLoop, calls=%fused_computation.3 | loop fusion | flops 2211840 | bytes 2580481 | tf_op jit(solution)/shard_map/convert_element_type | solution.py:485
  129.9 1.4 collective-permute-start.28
  131.3 11.4 %all-to-all-start = ((bf16[16,144,128]{2,1,0:T(8,128)(2,1)}), bf16[16,144,128]{2,1,0:T(8,128)(2,1)}, u32[]{:S(2)}, u32[]{:S(2)}) async-start(bf16[16,144,128]{2,1,0:T(8,128)(2,1)} %turn_kernel.1), calls=%async_computation | async-start | bytes 1179648 | tf_op jit(solution)/shard_map/all_to_all | solution.py:494
  142.7 1.7 %convert_add_fusion = f32[96,1920]{1,0:T(8,128)S(1)} fusion(bf16[96,1920]{1,0:T(8,128)(2,1)S(1)} %collective-permute-done.28, bf16[96,1920]{1,0:T(8,128)(2,1)} %collective-permute-done.26, bf16[96,1920]{1,0:T(8,128)(2,1)} %collective-permute-done.27, pred[]{:T(512)S(6)} %eq.18, bf16[2,96,1920]{2,1,0:T(8,128)(2,1)} %collective-permute-done.9, ...), kind=kLoop, calls=%fused_computation.2 | loop fusion | flops 2396160 | bytes 3317761 | tf_op jit(solution)/shard_map/add | solution.py:47
  144.8 2.1 %collective-permute-start.29 = (bf16[96,192]{1,0:T(8,128)(2,1)S(1)}, bf16[96,192]{1,0:T(8,128)(2,1)S(1)}, u32[]{:S(2)}, u32[]{:S(2)}) collective-permute-start(bf16[96,192]{1,0:T(8,128)(2,1)S(1)} %bitcast.56), channel_id=1, source_target_pairs={{0,8},{8,0},{16,24},{24,16},{32,40},{40,32},{48,56},{56,48},{64,72... | collective-permute-start | bytes 110600 | tf_op jit(solution)/shard_map/ppermute | solution.py:492
  146.8 0.9 fusion.1
  147.9 0.8 copy.28
  148.8 4.7 %all-to-all-done.spread = bf16[16,144,128]{2,1,0:T(8,128)(2,1)} async-done(((bf16[16,144,128]{2,1,0:T(8,128)(2,1)}), bf16[16,144,128]{2,1,0:T(8,128)(2,1)}, u32[]{:S(2)}, u32[]{:S(2)}) %all-to-all-start) | async-done | bytes 589856 | tf_op jit(solution)/shard_map/all_to_all | solution.py:494
  153.4 5.7 %last_kernel.1 = bf16[2,96,1536]{2,1,0:T(8,128)(2,1)} custom-call(bf16[16,144,128]{2,1,0:T(8,128)(2,1)} %all-to-all-done.spread, bf16[1536,1536]{1,0:T(8,128)(2,1)} %basis_out.1), custom_call_target="tpu_custom_call" | custom-call | tf_op jit(solution)/shard_map/last_kernel/pallas_call | solution.py:495
  159.1 2.5 %copy.27 = bf16[96,2,1536]{2,1,0:T(2,128)(2,1)} copy(bf16[96,2,1536]{2,0,1:T(8,128)(2,1)} %bitcast.43) | data formatting | bytes 1179648
  (73 shorter events, 8.6 us)
Async XLA Ops:
  7.2 112.6 %all-gather.2.cloned.1.call-start = ((), (), s32[]{:S(2)}) async-start(), calls=%async_computation.1 | async-start | bytes 5898240 | tf_op jit(solution)/shard_map/all_gather | solution.py:399
  7.2 4.3 %copy-start.1 = (bf16[512,1536]{1,0:T(8,128)(2,1)S(1)}, bf16[512,1536]{1,0:T(8,128)(2,1)}, u32[]{:S(2)}) copy-start(bf16[512,1536]{1,0:T(8,128)(2,1)} %cot_0.1) | copy-start | bytes 4718596
  7.2 4.2 %copy-start.4 = (bf16[96,2,192]{2,1,0:T(2,128)(2,1)S(1)}, bf16[96,2,192]{2,1,0:T(2,128)(2,1)}, u32[]{:S(2)}) copy-start(bf16[96,2,192]{2,1,0:T(2,128)(2,1)} %param.11) | copy-start | bytes 221188
  10.1 23.4 %collective-permute-start.4 = (bf16[512,1536]{1,0:T(8,128)(2,1)}, bf16[512,1536]{1,0:T(8,128)(2,1)S(1)}, u32[]{:S(2)}, u32[]{:S(2)}) collective-permute-start(bf16[512,1536]{1,0:T(8,128)(2,1)} %constant_dynamic-slice_fusion.3), channel_id=1, source_target_pairs={{0,8},{8,0},{16,24},{24,16},{32,40},{40,32},{48,56},{56,48},{64,72... | collective-permute-start | bytes 4718600 | tf_op jit(solution)/shard_map/ppermute | solution.py:306
  11.5 22.7 %collective-permute-start.3 = (bf16[512,1536]{1,0:T(8,128)(2,1)S(1)}, bf16[512,1536]{1,0:T(8,128)(2,1)}, u32[]{:S(2)}, u32[]{:S(2)}) collective-permute-start(bf16[512,1536]{1,0:T(8,128)(2,1)S(1)} %copy-done.1), channel_id=1, source_target_pairs={{0,8},{8,0},{16,24},{24,16},{32,40},{40,32},{48,56},{56,48},{64,72... | collective-permute-start | bytes 4718600 | tf_op jit(solution)/shard_map/ppermute | solution.py:304
  11.7 6.7 %collective-permute-start = (bf16[96,192]{1,0:T(8,128)(2,1)S(1)}, bf16[96,192]{1,0:T(8,128)(2,1)S(1)}, u32[]{:S(2)}, u32[]{:S(2)}) collective-permute-start(bf16[96,192]{1,0:T(8,128)(2,1)S(1)} %bitcast.55), channel_id=1, source_target_pairs={{0,8},{8,0},{16,24},{24,16},{32,40},{40,32},{48,56},{56,48},{64,72... | collective-permute-start | bytes 110600 | tf_op jit(solution)/shard_map/ppermute | solution.py:301
  13.0 8.4 %copy-start.6 = (s32[512]{0:T(512)S(1)}, s32[512]{0:T(512)}, u32[]{:S(2)}) copy-start(s32[512]{0:T(512)} %param.17) | copy-start | bytes 6148
  18.5 9.4 %collective-permute-start.2 = (bf16[192,192]{1,0:T(8,128)(2,1)S(1)}, bf16[192,192]{1,0:T(8,128)(2,1)S(1)}, u32[]{:S(2)}, u32[]{:S(2)}) collective-permute-start(bf16[192,192]{1,0:T(8,128)(2,1)S(1)} %maximum_select_fusion.1), channel_id=1, source_target_pairs={{0,4},{1,5},{2,6},{3,7},{4,0},{5,1},{6,2},{7,3},{8,12},{9,13},{10,... | collective-permute-start | bytes 221192 | tf_op jit(solution)/shard_map/ppermute | solution.py:335
  21.4 1.2 collective-permute-start.1
  22.6 5.3 %copy-start.7 = (s32[1,512]{1,0:T(1,128)}, s32[1,512]{1,0:T(1,128)S(1)}, u32[]{:S(2)}) copy-start(s32[1,512]{1,0:T(1,128)S(1)} %collective-permute-done.1.marks_1) | copy-start | bytes 6148
  27.9 20.4 %collective-permute-start.8 = (bf16[1536,512]{1,0:T(8,128)(2,1)}, bf16[1536,512]{1,0:T(8,128)(2,1)}, u32[]{:S(2)}, u32[]{:S(2)}) collective-permute-start(bf16[1536,512]{1,0:T(8,128)(2,1)} %rotate_kernel.3.eigen_0), channel_id=1, source_target_pairs={{0,8},{8,0},{16,24},{24,16},{32,40},{40,32},{48,56},{56,48},{64,72... | collective-permute-start | bytes 4718600 | tf_op jit(solution)/shard_map/ppermute | solution.py:337
  28.4 16.3 %collective-permute-start.7 = (bf16[192,384]{1,0:T(8,128)(2,1)S(1)}, bf16[192,384]{1,0:T(8,128)(2,1)S(1)}, u32[]{:S(2)}, u32[]{:S(2)}) collective-permute-start(bf16[192,384]{1,0:T(8,128)(2,1)S(1)} %pad_maximum_fusion.1), channel_id=1, source_target_pairs={{0,32},{8,40},{16,48},{24,56},{32,64},{40,72},{48,80},{56,88},{64,... | collective-permute-start | bytes 442376 | tf_op jit(solution)/shard_map/ppermute | solution.py:339
  30.1 16.9 %collective-permute-start.6 = (bf16[192,384]{1,0:T(8,128)(2,1)S(1)}, bf16[192,384]{1,0:T(8,128)(2,1)S(1)}, u32[]{:S(2)}, u32[]{:S(2)}) collective-permute-start(bf16[192,384]{1,0:T(8,128)(2,1)S(1)} %pad_maximum_fusion.1), channel_id=1, source_target_pairs={{0,64},{8,72},{16,80},{24,88},{32,96},{40,104},{48,112},{56,120},{... | collective-permute-start | bytes 442376 | tf_op jit(solution)/shard_map/ppermute | solution.py:339
  33.5 1.1 copy-start
  33.5 13.6 %collective-permute-start.5 = (bf16[192,384]{1,0:T(8,128)(2,1)S(1)}, bf16[192,384]{1,0:T(8,128)(2,1)S(1)}, u32[]{:S(2)}, u32[]{:S(2)}) collective-permute-start(bf16[192,384]{1,0:T(8,128)(2,1)S(1)} %pad_maximum_fusion.1), channel_id=1, source_target_pairs={{0,96},{8,104},{16,112},{24,120},{32,0},{40,8},{48,16},{56,24},{64... | collective-permute-start | bytes 442376 | tf_op jit(solution)/shard_map/ppermute | solution.py:339
  44.4 19.9 %collective-permute-start.9 = (bf16[2,96,1920]{2,1,0:T(8,128)(2,1)}, bf16[2,96,1920]{2,1,0:T(8,128)(2,1)}, u32[]{:S(2)}, u32[]{:S(2)}) collective-permute-start(bf16[2,96,1920]{2,1,0:T(8,128)(2,1)} %get-tuple-element.51), channel_id=1, source_target_pairs={{0,32},{8,40},{16,48},{24,56},{32,64},{40,72},{48,80},{56,88},{64,... | collective-permute-start | bytes 2211848 | tf_op jit(solution)/shard_map/ppermute | solution.py:56
  44.7 19.6 %collective-permute-start.10 = (bf16[2,96,1920]{2,1,0:T(8,128)(2,1)}, bf16[2,96,1920]{2,1,0:T(8,128)(2,1)}, u32[]{:S(2)}, u32[]{:S(2)}) collective-permute-start(bf16[2,96,1920]{2,1,0:T(8,128)(2,1)} %get-tuple-element.57), channel_id=1, source_target_pairs={{0,96},{8,104},{16,112},{24,120},{32,0},{40,8},{48,16},{56,24},{64... | collective-permute-start | bytes 2211848 | tf_op jit(solution)/shard_map/ppermute | solution.py:56
  48.0 16.3 %collective-permute-start.11 = (bf16[4,192,384]{2,1,0:T(8,128)(2,1)}, bf16[4,192,384]{2,1,0:T(8,128)(2,1)}, u32[]{:S(2)}, u32[]{:S(2)}) collective-permute-start(bf16[4,192,384]{2,1,0:T(8,128)(2,1)} %pad_maximum_fusion.own), channel_id=1, source_target_pairs={{0,16},{8,24},{16,0},{24,8},{32,48},{40,56},{48,32},{56,40},{64,80... | collective-permute-start | bytes 1769480 | tf_op jit(solution)/shard_map/ppermute | solution.py:366
  67.4 17.9 %collective-permute-start.14 = (bf16[4,192,512]{2,1,0:T(8,128)(2,1)}, bf16[4,192,512]{2,1,0:T(8,128)(2,1)}, u32[]{:S(2)}, u32[]{:S(2)}) collective-permute-start(bf16[4,192,512]{2,1,0:T(8,128)(2,1)} %get-tuple-element.65), channel_id=1, source_target_pairs={{0,16},{8,24},{16,0},{24,8},{32,48},{40,56},{48,32},{56,40},{64,80... | collective-permute-start | bytes 2359304 | tf_op jit(solution)/shard_map/ppermute | solution.py:418
  68.7 18.7 %collective-permute-start.15 = (bf16[2,192,1024]{2,1,0:T(8,128)(2,1)}, bf16[2,192,1024]{2,1,0:T(8,128)(2,1)}, u32[]{:S(2)}, u32[]{:S(2)}) collective-permute-start(bf16[2,192,1024]{2,1,0:T(8,128)(2,1)} %get-tuple-element.66), channel_id=1, source_target_pairs={{0,32},{8,40},{16,48},{24,56},{32,64},{40,72},{48,80},{56,88},{64,... | collective-permute-start | bytes 2359304 | tf_op jit(solution)/shard_map/ppermute | solution.py:56
  68.7 18.7 %collective-permute-start.16 = (bf16[2,192,1024]{2,1,0:T(8,128)(2,1)}, bf16[2,192,1024]{2,1,0:T(8,128)(2,1)}, u32[]{:S(2)}, u32[]{:S(2)}) collective-permute-start(bf16[2,192,1024]{2,1,0:T(8,128)(2,1)} %get-tuple-element.67), channel_id=1, source_target_pairs={{0,96},{8,104},{16,112},{24,120},{32,0},{40,8},{48,16},{56,24},{64... | collective-permute-start | bytes 2359304 | tf_op jit(solution)/shard_map/ppermute | solution.py:56
  76.6 3.0 %collective-permute-start.12 = (f32[1,384]{1,0:T(1,128)}, f32[1,384]{1,0:T(1,128)S(1)}, u32[]{:S(2)}, u32[]{:S(2)}) collective-permute-start(f32[1,384]{1,0:T(1,128)} %squares_in_kernel.1), channel_id=1, source_target_pairs={{0,1},{1,0},{2,3},{3,2},{4,5},{5,4},{6,7},{7,6},{8,9},{9,8},{10,11... | collective-permute-start | bytes 4616 | tf_op jit(solution)/shard_map/ppermute | solution.py:415
  80.5 4.1 %collective-permute-start.13 = (f32[2,384]{1,0:T(2,128)S(1)}, f32[2,384]{1,0:T(2,128)S(1)}, u32[]{:S(2)}, u32[]{:S(2)}) collective-permute-start(f32[2,384]{1,0:T(2,128)S(1)} %maximum_select_fusion.3), channel_id=1, source_target_pairs={{0,2},{1,3},{2,0},{3,1},{4,6},{5,7},{6,4},{7,5},{8,10},{9,11},{10,... | collective-permute-start | bytes 9224 | tf_op jit(solution)/shard_map/ppermute | solution.py:416
  90.7 15.0 %collective-permute-start.21 = (bf16[192,1536]{1,0:T(8,128)(2,1)}, bf16[192,1536]{1,0:T(8,128)(2,1)}, u32[]{:S(2)}, u32[]{:S(2)}) collective-permute-start(bf16[192,1536]{1,0:T(8,128)(2,1)} %get-tuple-element.70), channel_id=1, source_target_pairs={{0,32},{8,40},{16,48},{24,56},{32,64},{40,72},{48,80},{56,88},{64,... | collective-permute-start | bytes 1769480 | tf_op jit(solution)/shard_map/ppermute | solution.py:56
  90.7 15.0 %collective-permute-start.22 = (bf16[192,1536]{1,0:T(8,128)(2,1)}, bf16[192,1536]{1,0:T(8,128)(2,1)}, u32[]{:S(2)}, u32[]{:S(2)}) collective-permute-start(bf16[192,1536]{1,0:T(8,128)(2,1)} %get-tuple-element.71), channel_id=1, source_target_pairs={{0,96},{8,104},{16,112},{24,120},{32,0},{40,8},{48,16},{56,24},{64... | collective-permute-start | bytes 1769480 | tf_op jit(solution)/shard_map/ppermute | solution.py:56
  94.2 3.1 %collective-permute-start.17 = (f32[9,384]{1,0:T(8,128)S(1)}, f32[9,384]{1,0:T(8,128)S(1)}, u32[]{:S(2)}, u32[]{:S(2)}) collective-permute-start(f32[9,384]{1,0:T(8,128)S(1)} %pad_maximum_fusion.2), channel_id=1, source_target_pairs={{0,16},{8,24},{16,0},{24,8},{32,48},{40,56},{48,32},{56,40},{64,80... | collective-permute-start | bytes 41480 | tf_op jit(solution)/shard_map/ppermute | solution.py:436
  98.0 7.0 %collective-permute-start.20 = (f32[9,384]{1,0:T(8,128)S(1)}, f32[9,384]{1,0:T(8,128)S(1)}, u32[]{:S(2)}, u32[]{:S(2)}) collective-permute-start(f32[9,384]{1,0:T(8,128)S(1)} %fusion.8), channel_id=1, source_target_pairs={{0,64},{8,72},{16,80},{24,88},{32,96},{40,104},{48,112},{56,120},{... | collective-permute-start | bytes 41480 | tf_op jit(solution)/shard_map/ppermute | solution.py:437
  99.0 6.1 %collective-permute-start.19 = (f32[9,384]{1,0:T(8,128)S(1)}, f32[9,384]{1,0:T(8,128)S(1)}, u32[]{:S(2)}, u32[]{:S(2)}) collective-permute-start(f32[9,384]{1,0:T(8,128)S(1)} %fusion.8), channel_id=1, source_target_pairs={{0,96},{8,104},{16,112},{24,120},{32,0},{40,8},{48,16},{56,24},{64... | collective-permute-start | bytes 41480 | tf_op jit(solution)/shard_map/ppermute | solution.py:437
  99.4 5.7 %collective-permute-start.18 = (f32[9,384]{1,0:T(8,128)S(1)}, f32[9,384]{1,0:T(8,128)S(1)}, u32[]{:S(2)}, u32[]{:S(2)}) collective-permute-start(f32[9,384]{1,0:T(8,128)S(1)} %fusion.8), channel_id=1, source_target_pairs={{0,32},{8,40},{16,48},{24,56},{32,64},{40,72},{48,80},{56,88},{64,... | collective-permute-start | bytes 41480 | tf_op jit(solution)/shard_map/ppermute | solution.py:437
  109.7 7.4 %collective-permute-start.25 = (bf16[192,1024]{1,0:T(8,128)(2,1)}, bf16[192,1024]{1,0:T(8,128)(2,1)}, u32[]{:S(2)}, u32[]{:S(2)}) collective-permute-start(bf16[192,1024]{1,0:T(8,128)(2,1)} %get-tuple-element.80), channel_id=1, source_target_pairs={{0,16},{8,24},{16,0},{24,8},{32,48},{40,56},{48,32},{56,40},{64,80... | collective-permute-start | bytes 1179656 | tf_op jit(solution)/shard_map/ppermute | solution.py:455
  111.7 5.4 %collective-permute-start.23 = (bf16[96,512]{1,0:T(8,128)(2,1)}, bf16[96,512]{1,0:T(8,128)(2,1)}, u32[]{:S(2)}, u32[]{:S(2)}) collective-permute-start(bf16[96,512]{1,0:T(8,128)(2,1)} %get-tuple-element.82), channel_id=1, source_target_pairs={{0,32},{8,40},{16,48},{24,56},{32,64},{40,72},{48,80},{56,88},{64,... | collective-permute-start | bytes 294920 | tf_op jit(solution)/shard_map/ppermute | solution.py:56
  112.7 4.3 %collective-permute-start.24 = (bf16[96,512]{1,0:T(8,128)(2,1)}, bf16[96,512]{1,0:T(8,128)(2,1)}, u32[]{:S(2)}, u32[]{:S(2)}) collective-permute-start(bf16[96,512]{1,0:T(8,128)(2,1)} %get-tuple-element.83), channel_id=1, source_target_pairs={{0,96},{8,104},{16,112},{24,120},{32,0},{40,8},{48,16},{56,24},{64... | collective-permute-start | bytes 294920 | tf_op jit(solution)/shard_map/ppermute | solution.py:56
  117.1 10.9 %collective-permute-start.26 = (bf16[96,1920]{1,0:T(8,128)(2,1)}, bf16[96,1920]{1,0:T(8,128)(2,1)}, u32[]{:S(2)}, u32[]{:S(2)}) collective-permute-start(bf16[96,1920]{1,0:T(8,128)(2,1)} %get-tuple-element.87), channel_id=1, source_target_pairs={{0,32},{8,40},{16,48},{24,56},{32,64},{40,72},{48,80},{56,88},{64,... | collective-permute-start | bytes 1105928 | tf_op jit(solution)/shard_map/ppermute | solution.py:56
  117.8 10.1 %collective-permute-start.27 = (bf16[96,1920]{1,0:T(8,128)(2,1)}, bf16[96,1920]{1,0:T(8,128)(2,1)}, u32[]{:S(2)}, u32[]{:S(2)}) collective-permute-start(bf16[96,1920]{1,0:T(8,128)(2,1)} %get-tuple-element.88), channel_id=1, source_target_pairs={{0,96},{8,104},{16,112},{24,120},{32,0},{40,8},{48,16},{56,24},{64... | collective-permute-start | bytes 1105928 | tf_op jit(solution)/shard_map/ppermute | solution.py:56
  127.9 14.8 %copy-start.2 = (bf16[4,96,1920]{2,1,0:T(8,128)(2,1)S(1)}, bf16[4,96,1920]{2,1,0:T(8,128)(2,1)}, u32[]{:S(2)}) copy-start(bf16[4,96,1920]{2,1,0:T(8,128)(2,1)} %get-tuple-element.86) | copy-start | bytes 4423684
  129.9 12.8 %collective-permute-start.28 = (bf16[96,1920]{1,0:T(8,128)(2,1)S(1)}, bf16[96,1920]{1,0:T(8,128)(2,1)S(1)}, u32[]{:S(2)}, u32[]{:S(2)}) collective-permute-start(bf16[96,1920]{1,0:T(8,128)(2,1)S(1)} %select_convert_fusion), channel_id=1, source_target_pairs={{0,16},{8,24},{16,0},{24,8},{32,48},{40,56},{48,32},{56,40},{64,80... | collective-permute-start | bytes 1105928 | tf_op jit(solution)/shard_map/ppermute | solution.py:487
  131.3 22.2 %all-to-all-start = ((bf16[16,144,128]{2,1,0:T(8,128)(2,1)}), bf16[16,144,128]{2,1,0:T(8,128)(2,1)}, u32[]{:S(2)}, u32[]{:S(2)}) async-start(bf16[16,144,128]{2,1,0:T(8,128)(2,1)} %turn_kernel.1), calls=%async_computation | async-start | bytes 1179648 | tf_op jit(solution)/shard_map/all_to_all | solution.py:494
  142.7 4.1 %copy-start.3 = (f32[96,1536]{1,0:T(8,128)S(1)}, f32[96,1536]{1,0:T(8,128)}, u32[]{:S(2)}) copy-start(f32[96,1536]{1,0:T(8,128)} %param.14) | copy-start | bytes 1769476
  144.4 3.4 %copy-start.5 = (f32[96,2,192]{2,1,0:T(2,128)S(1)}, f32[96,2,192]{2,1,0:T(2,128)}, u32[]{:S(2)}) copy-start(f32[96,2,192]{2,1,0:T(2,128)} %param.13) | copy-start | bytes 442372
  144.8 3.1 %collective-permute-start.29 = (bf16[96,192]{1,0:T(8,128)(2,1)S(1)}, bf16[96,192]{1,0:T(8,128)(2,1)S(1)}, u32[]{:S(2)}, u32[]{:S(2)}) collective-permute-start(bf16[96,192]{1,0:T(8,128)(2,1)S(1)} %bitcast.56), channel_id=1, source_target_pairs={{0,8},{8,0},{16,24},{24,16},{32,40},{40,32},{48,56},{56,48},{64,72... | collective-permute-start | bytes 110600 | tf_op jit(solution)/shard_map/ppermute | solution.py:492
Sparse Core Ops, SparseCore 0:
  67.5 51.9 all-gather.1
